TPU v7x, 128 devices: a whole 4x4x4 slice. The times are simulated.
128 devices in a mesh: dp: 32 (over y, z, core), ctx: 4 (over x).
Axes of the slice: x: 4, y: 4, z: 4, core: 2. Of those that a mesh axis runs over, the one named last changes fastest.
Arguments:
- char_ids: int32 [16384, 50], P(('dp', 'ctx')), may hold values from 0 to 261
- word_lengths: int32 [16384], P(('dp', 'ctx')), may hold values from 1 to 50, as said below
- word_home: int32 [16384], P(('dp', 'ctx')), may hold values from 0 to 16383, as said below
- seq_lengths: int32 [32], P('dp'), may hold values from 385 to 512, as said below
- char_table: bfloat16 [262, 16], replicated, may hold values from -6 to 6
- conv_weight: bfloat16 [112, 2048], replicated, may hold values from -0.75 to 0.75
- conv_bias: bfloat16 [2048], replicated, may hold values from -3 to 3
- highway_weight: bfloat16 [1, 2048, 4096], replicated, may hold values from -0.125 to 0.125
- highway_bias: bfloat16 [1, 4096], replicated, may hold values from -3 to 3
- proj_weight: bfloat16 [2048, 768], replicated, may hold values from -0.125 to 0.125
- norm_gain: bfloat16 [3, 768], replicated, may hold values from 0.099609375 to 1.8984375
- norm_shift: bfloat16 [3, 768], replicated, may hold values from -2 to 2
- qkv_weight: bfloat16 [768, 2304], replicated, may hold values from -0.21875 to 0.21875
- out_weight: bfloat16 [768, 768], replicated, may hold values from -1.75 to 1.75
- up_weight: bfloat16 [768, 3072], replicated, may hold values from -0.21875 to 0.21875
- down_weight: bfloat16 [3072, 768], replicated, may hold values from -0.109375 to 0.109375
- cotangent: bfloat16 [32, 512, 768], P('dp', 'ctx'), may hold values from -6 to 6
Outputs:
- out_hidden: bfloat16 [32, 512, 768], P('dp', 'ctx')
- grad_char_table: float32 [262, 16], replicated
- grad_conv_weight: float32 [112, 2048], P(None, ('dp', 'ctx'))
- grad_conv_bias: float32 [2048], replicated
- grad_highway_weight: float32 [1, 2048, 4096], P(None, ('dp', 'ctx'))
- grad_highway_bias: float32 [1, 4096], replicated
- grad_proj_weight: float32 [2048, 768], P(('dp', 'ctx'))
- grad_norm_gain: float32 [3, 768], replicated
- grad_norm_shift: float32 [3, 768], replicated
- grad_qkv_weight: float32 [768, 2304], P(('dp', 'ctx'))
- grad_out_weight: float32 [768, 768], P(('dp', 'ctx'))
- grad_up_weight: float32 [768, 3072], P(('dp', 'ctx'))
- grad_down_weight: float32 [3072, 768], P(('dp', 'ctx'))
Inputs may be any that keep to these rules, and one draw needn't show every extreme that they name: A word's characters are its first word_lengths slots; later slots hold ids that are ignored. Some word has 50 characters. word_home is a permutation. A device's block is the words that out_hidden's layout puts on it; the 128 rows of each device hold exactly 1 words of every device's block. `seq_lengths`: some sequence has length 512.
All inputs are finite; a program needn't handle non-finite values.
Results may differ from a plain program's by a relative error of at most 0.02.
Values may be sent and summed in bfloat16 or wider, within the bound.
A program may use at most 256 MiB of HBM per device.

v0:
```python
import jax
import jax.numpy as jnp
from jax import lax
from jax.sharding import PartitionSpec as P

D = 768
HEADS = 12
HEAD_DIM = 64
FILTERS = 2048
CHAR_DIM = 16
CHARS = 262
WORD_CHARS = 50
TAPS = 7
HIGHWAY = 1
SEQ_LEN = 512


EPSILON = 1e-05
NEG_LARGE = -1e30
BLOCK_WORDS = 32


def filter_widths():
    unit_count = FILTERS // 64
    filter_index = jnp.arange(FILTERS)
    widths = jnp.ones((FILTERS,), jnp.int32)
    for bound_units in (1, 2, 4, 8, 16, 32):
        widths = widths + (filter_index >= unit_count * bound_units).astype(jnp.int32)
    return widths


def tap_mask():
    tap_rows = jnp.arange(TAPS * CHAR_DIM) // CHAR_DIM
    return tap_rows[:, None] < filter_widths()[None, :]


def char_features(char_ids, word_lens, char_table):
    present = jnp.arange(WORD_CHARS)[None, :] < word_lens[:, None]
    onehot = (char_ids[:, :, None] == jnp.arange(CHARS)[None, None, :]).astype(jnp.bfloat16)
    char_vals = jnp.einsum("bpv,vc->bpc", onehot, char_table, preferred_element_type=jnp.float32)
    char_vals = jnp.where(present[:, :, None], char_vals, 0.0)
    padded = jnp.pad(char_vals, ((0, 0), (0, TAPS - 1), (0, 0)))
    unfolded = jnp.concatenate(
        [padded[:, tap_index : tap_index + WORD_CHARS, :] for tap_index in range(TAPS)], axis=-1
    ).astype(jnp.bfloat16)
    return (present, onehot, unfolded)


def pool_block(char_ids, word_lens, char_table, conv_masked, conv_shift):
    present, onehot, unfolded = char_features(char_ids, word_lens, char_table)
    conv_rows = (
        jnp.einsum("bpc,cf->bpf", unfolded, conv_masked, preferred_element_type=jnp.float32)
        + conv_shift
    )
    masked = jnp.where(present[:, :, None], conv_rows, NEG_LARGE)
    top_val = jnp.max(masked, axis=1, keepdims=True)
    expo_val = jnp.where(present[:, :, None], jnp.exp(masked - top_val), 0.0)
    totals = jnp.sum(expo_val, axis=1)
    pooled = top_val[:, 0, :] + jnp.log(totals)
    return (pooled, present, onehot, unfolded, expo_val / totals[:, None, :])


def gate_mix(current, mixed_rows):
    carry_gate = jax.nn.sigmoid(mixed_rows[:, FILTERS:])
    return carry_gate * current + (1.0 - carry_gate) * jax.nn.gelu(mixed_rows[:, :FILTERS])


def highway_forward(pooled, highway_weight, high_shift):
    current = jax.nn.gelu(pooled).astype(jnp.bfloat16)
    mixed_rows = (
        jnp.dot(current, highway_weight[0], preferred_element_type=jnp.float32) + high_shift[0]
    )
    inputs_kept = [current]
    mixed_kept = [mixed_rows]
    current = gate_mix(current.astype(jnp.float32), mixed_rows).astype(jnp.bfloat16)
    return (current, inputs_kept, mixed_kept)


def norm_parts(values_in, gain_row, shift_row):
    mean_val = jnp.mean(values_in, -1, keepdims=True)
    centred = values_in - mean_val
    inverse = lax.rsqrt(jnp.mean(centred * centred, -1, keepdims=True) + EPSILON)
    normal = centred * inverse
    return (normal * gain_row + shift_row, normal, inverse)


def norm_back(grad_out, normal, inverse, gain_row):
    scaled = grad_out * gain_row
    grad_in = inverse * (
        scaled
        - jnp.mean(scaled, -1, keepdims=True)
        - normal * jnp.mean(scaled * normal, -1, keepdims=True)
    )
    return (grad_in, jnp.sum(grad_out * normal, 0), jnp.sum(grad_out, 0))


def transpose_dot(left_rows, right_rows):
    return lax.dot_general(
        left_rows, right_rows, (((0,), (0,)), ((), ())), preferred_element_type=jnp.float32
    )


def back_dot(rows_in, weight_rows):
    return lax.dot_general(
        rows_in, weight_rows, (((1,), (1,)), ((), ())), preferred_element_type=jnp.float32
    )


def body(
    char_ids,
    word_lengths,
    word_home,
    seq_lengths,
    char_table,
    conv_weight,
    conv_bias,
    highway_weight,
    highway_bias,
    proj_weight,
    norm_gain,
    norm_shift,
    qkv_weight,
    out_weight,
    up_weight,
    down_weight,
    cotangent,
):
    word_count = char_ids.shape[0]
    seq_count = seq_lengths.shape[0]
    group_len = cotangent.shape[1]
    ctx_size = lax.axis_size("ctx")
    full_len = group_len * ctx_size
    head_scale = HEAD_DIM ** (-0.5)
    taps_on = tap_mask()
    conv_masked = jnp.where(taps_on, conv_weight, jnp.zeros_like(conv_weight))
    conv_shift = conv_bias.astype(jnp.float32)
    high_shift = highway_bias.astype(jnp.float32)
    gain_rows = norm_gain.astype(jnp.float32)
    shift_rows = norm_shift.astype(jnp.float32)
    blocks = word_count // BLOCK_WORDS
    id_blocks = char_ids.reshape(blocks, BLOCK_WORDS, WORD_CHARS)
    len_blocks = word_lengths.reshape(blocks, BLOCK_WORDS)

    def pool_only(packed):
        return pool_block(packed[0], packed[1], char_table, conv_masked, conv_shift)[0]

    pooled = lax.map(pool_only, (id_blocks, len_blocks)).reshape(word_count, FILTERS)
    final_rows, _, _ = highway_forward(pooled, highway_weight, high_shift)
    embedded = jnp.dot(final_rows, proj_weight, preferred_element_type=jnp.float32).astype(
        jnp.bfloat16
    )
    seq_index = word_home // SEQ_LEN
    pos_index = word_home % SEQ_LEN
    target = seq_index // seq_count * ctx_size + pos_index // group_len
    local_slot = seq_index % seq_count * group_len + pos_index % group_len
    send_order = jnp.argsort(target * word_count + local_slot)
    arrived, arrived_slot = (
        lax.all_to_all(
            jnp.take(embedded, send_order, axis=0),
            ("dp", "ctx"),
            split_axis=0,
            concat_axis=0,
            tiled=True,
        ),
        lax.all_to_all(
            jnp.take(local_slot, send_order), ("dp", "ctx"), split_axis=0, concat_axis=0, tiled=True
        ),
    )
    placement = jnp.argsort(arrived_slot)
    word_rows = jnp.take(arrived, placement, axis=0).astype(jnp.float32)
    first_f, first_normal, first_inv = norm_parts(word_rows, gain_rows[0], shift_rows[0])
    first_norm = first_f.astype(jnp.bfloat16)
    joint_proj = jnp.dot(first_norm, qkv_weight, preferred_element_type=jnp.float32).astype(
        jnp.bfloat16
    )
    queries = joint_proj[:, :D].reshape(seq_count, group_len, HEADS, HEAD_DIM)
    key_part = joint_proj[:, D : 2 * D].reshape(seq_count, group_len, D)
    value_part = joint_proj[:, 2 * D :].reshape(seq_count, group_len, D)
    keys_all, values_all = (
        lax.all_gather(key_part, "ctx", axis=1, tiled=True),
        lax.all_gather(value_part, "ctx", axis=1, tiled=True),
    )
    key_valid = jnp.arange(full_len)[None, :] < seq_lengths[:, None]
    valid_wide = key_valid[:, None, None, :]
    key_heads = keys_all.reshape(seq_count, full_len, HEADS, HEAD_DIM)
    value_heads = values_all.reshape(seq_count, full_len, HEADS, HEAD_DIM)
    scores = (
        jnp.einsum("sqhd,skhd->shqk", queries, key_heads, preferred_element_type=jnp.float32)
        * head_scale
    )
    masked = jnp.where(valid_wide, scores, NEG_LARGE)
    top_val = jnp.max(masked, -1, keepdims=True)
    expo_val = jnp.where(valid_wide, jnp.exp(masked - top_val), 0.0)
    totals = jnp.sum(expo_val, -1, keepdims=True)
    probs_low = (expo_val / totals).astype(jnp.bfloat16)
    log_total = top_val + jnp.log(totals)
    context = (
        jnp.einsum("shqk,skhd->sqhd", probs_low, value_heads, preferred_element_type=jnp.float32)
        .reshape(word_count, D)
        .astype(jnp.bfloat16)
    )
    attn_out = jnp.dot(context, out_weight, preferred_element_type=jnp.float32)
    mid_f, mid_normal, mid_inv = norm_parts(
        first_norm.astype(jnp.float32) + attn_out, gain_rows[1], shift_rows[1]
    )
    middle = mid_f.astype(jnp.bfloat16)
    up_proj = jnp.dot(middle, up_weight, preferred_element_type=jnp.float32)
    hidden_act = jax.nn.gelu(up_proj).astype(jnp.bfloat16)
    down_proj = jnp.dot(hidden_act, down_weight, preferred_element_type=jnp.float32)
    out_f, out_normal, out_inv = norm_parts(
        middle.astype(jnp.float32) + down_proj, gain_rows[2], shift_rows[2]
    )
    out_hidden = out_f.astype(jnp.bfloat16).reshape(seq_count, group_len, D)
    grad_rows = cotangent.reshape(word_count, D).astype(jnp.float32)
    grad_pre2, gain_two, shift_two = norm_back(grad_rows, out_normal, out_inv, gain_rows[2])
    grad_down = grad_pre2.astype(jnp.bfloat16)
    grad_down_weight = transpose_dot(hidden_act, grad_down)
    _, gelu_pull = jax.vjp(jax.nn.gelu, up_proj)
    grad_up = gelu_pull(back_dot(grad_down, down_weight))[0].astype(jnp.bfloat16)
    grad_up_weight = transpose_dot(middle, grad_up)
    grad_mid = grad_pre2 + back_dot(grad_up, up_weight)
    grad_pre1, gain_one, shift_one = norm_back(grad_mid, mid_normal, mid_inv, gain_rows[1])
    grad_attn = grad_pre1.astype(jnp.bfloat16)
    grad_out_weight = transpose_dot(context, grad_attn)
    grad_context = (
        back_dot(grad_attn, out_weight)
        .astype(jnp.bfloat16)
        .reshape(seq_count, group_len, HEADS, HEAD_DIM)
    )
    keys_back, values_back = (
        lax.all_gather(key_part, "ctx", axis=1, tiled=True),
        lax.all_gather(value_part, "ctx", axis=1, tiled=True),
    )
    key_heads = keys_back.reshape(seq_count, full_len, HEADS, HEAD_DIM)
    value_heads = values_back.reshape(seq_count, full_len, HEADS, HEAD_DIM)
    scores = (
        jnp.einsum("sqhd,skhd->shqk", queries, key_heads, preferred_element_type=jnp.float32)
        * head_scale
    )
    probs_back = jnp.where(valid_wide, jnp.exp(scores - log_total), 0.0)
    grad_probs = jnp.einsum(
        "sqhd,skhd->shqk", grad_context, value_heads, preferred_element_type=jnp.float32
    )
    delta_rows = jnp.sum(probs_back * grad_probs, -1, keepdims=True)
    grad_scores = (probs_back * (grad_probs - delta_rows)).astype(jnp.bfloat16)
    grad_query = (
        jnp.einsum("shqk,skhd->sqhd", grad_scores, key_heads, preferred_element_type=jnp.float32)
        * head_scale
    )
    grad_keys = (
        jnp.einsum("shqk,sqhd->skhd", grad_scores, queries, preferred_element_type=jnp.float32)
        * head_scale
    )
    grad_values = jnp.einsum(
        "shqk,sqhd->skhd",
        probs_back.astype(jnp.bfloat16),
        grad_context,
        preferred_element_type=jnp.float32,
    )
    key_sum, value_sum = (
        lax.psum_scatter(
            grad_keys.reshape(seq_count, full_len, D).astype(jnp.bfloat16),
            "ctx",
            scatter_dimension=1,
            tiled=True,
        ).astype(jnp.float32),
        lax.psum_scatter(
            grad_values.reshape(seq_count, full_len, D).astype(jnp.bfloat16),
            "ctx",
            scatter_dimension=1,
            tiled=True,
        ).astype(jnp.float32),
    )
    grad_joint = jnp.concatenate(
        [
            grad_query.reshape(word_count, D),
            key_sum.reshape(word_count, D),
            value_sum.reshape(word_count, D),
        ],
        axis=-1,
    ).astype(jnp.bfloat16)
    grad_qkv_weight = transpose_dot(first_norm, grad_joint)
    grad_first = back_dot(grad_joint, qkv_weight) + grad_pre1
    grad_words, gain_zero, shift_zero = norm_back(grad_first, first_normal, first_inv, gain_rows[0])
    send_back = jnp.take(grad_words.astype(jnp.bfloat16), arrived_slot, axis=0)
    returned = lax.all_to_all(send_back, ("dp", "ctx"), split_axis=0, concat_axis=0, tiled=True)
    grad_embedded = jnp.take(returned, jnp.argsort(send_order), axis=0)
    final_rows, inputs_kept, mixed_kept = highway_forward(pooled, highway_weight, high_shift)
    grad_proj_weight = transpose_dot(final_rows, grad_embedded)
    grad_act = back_dot(grad_embedded, proj_weight)
    high_grads = [None] * HIGHWAY
    high_bias_grads = [None] * HIGHWAY
    for depth_index in reversed(range(HIGHWAY)):
        kept_in = inputs_kept[depth_index]
        _, mix_pull = jax.vjp(gate_mix, kept_in.astype(jnp.float32), mixed_kept[depth_index])
        grad_direct, grad_mixed = mix_pull(grad_act)
        grad_mixed = grad_mixed.astype(jnp.bfloat16)
        high_grads[depth_index] = transpose_dot(kept_in, grad_mixed)
        high_bias_grads[depth_index] = jnp.sum(grad_mixed.astype(jnp.float32), 0)
        grad_act = grad_direct + back_dot(grad_mixed, highway_weight[depth_index])
    grad_highway_weight = jnp.stack(high_grads)
    grad_highway_bias = jnp.stack(high_bias_grads)
    _, pool_pull = jax.vjp(jax.nn.gelu, pooled)
    grad_pooled = pool_pull(grad_act)[0].reshape(blocks, BLOCK_WORDS, FILTERS)

    def back_block(running, packed):
        _, present, onehot, unfolded, pool_weights = pool_block(
            packed[0], packed[1], char_table, conv_masked, conv_shift
        )
        grad_conv = (packed[2][:, None, :] * pool_weights).astype(jnp.bfloat16)
        new_weight = running[0] + jnp.einsum(
            "bpc,bpf->cf", unfolded, grad_conv, preferred_element_type=jnp.float32
        )
        new_bias = running[1] + jnp.sum(grad_conv.astype(jnp.float32), axis=(0, 1))
        grad_unfolded = jnp.einsum(
            "bpf,cf->bpc", grad_conv, conv_masked, preferred_element_type=jnp.float32
        )
        grad_padded = jnp.zeros((BLOCK_WORDS, WORD_CHARS + TAPS - 1, CHAR_DIM), jnp.float32)
        for tap_index in range(TAPS):
            grad_padded = grad_padded.at[:, tap_index : tap_index + WORD_CHARS, :].add(
                grad_unfolded[:, :, tap_index * CHAR_DIM : (tap_index + 1) * CHAR_DIM]
            )
        grad_chars = jnp.where(present[:, :, None], grad_padded[:, :WORD_CHARS, :], 0.0)
        new_table = running[2] + jnp.einsum(
            "bpv,bpc->vc", onehot.astype(jnp.float32), grad_chars, precision=lax.Precision.HIGHEST
        )
        return ((new_weight, new_bias, new_table), None)

    start_sums = (
        jnp.zeros((TAPS * CHAR_DIM, FILTERS), jnp.float32),
        jnp.zeros((FILTERS,), jnp.float32),
        jnp.zeros((CHARS, CHAR_DIM), jnp.float32),
    )
    (conv_grad_raw, grad_conv_bias, grad_char_table), _ = lax.scan(
        back_block, start_sums, (id_blocks, len_blocks, grad_pooled)
    )
    grad_conv_weight = jnp.where(taps_on, conv_grad_raw, 0.0)
    conv_shard, high_shard, proj_shard, qkv_shard, out_shard, up_shard, down_shard = (
        lax.psum_scatter(grad_conv_weight, ("dp", "ctx"), scatter_dimension=1, tiled=True),
        lax.psum_scatter(grad_highway_weight, ("dp", "ctx"), scatter_dimension=1, tiled=True),
        lax.psum_scatter(grad_proj_weight, ("dp", "ctx"), scatter_dimension=0, tiled=True),
        lax.psum_scatter(grad_qkv_weight, ("dp", "ctx"), scatter_dimension=0, tiled=True),
        lax.psum_scatter(grad_out_weight, ("dp", "ctx"), scatter_dimension=0, tiled=True),
        lax.psum_scatter(grad_up_weight, ("dp", "ctx"), scatter_dimension=0, tiled=True),
        lax.psum_scatter(grad_down_weight, ("dp", "ctx"), scatter_dimension=0, tiled=True),
    )
    grad_gain_rows = jnp.stack([gain_zero, gain_one, gain_two])
    grad_shift_rows = jnp.stack([shift_zero, shift_one, shift_two])
    table_sum, conv_bias_sum, high_bias_sum, gain_sum, shift_sum = lax.psum(
        (grad_char_table, grad_conv_bias, grad_highway_bias, grad_gain_rows, grad_shift_rows),
        ("dp", "ctx"),
    )
    return (
        out_hidden,
        table_sum,
        conv_shard,
        conv_bias_sum,
        high_shard,
        high_bias_sum,
        proj_shard,
        gain_sum,
        shift_sum,
        qkv_shard,
        out_shard,
        up_shard,
        down_shard,
    )


def solution(mesh):
    placed = (
        P(("dp", "ctx"), None),
        P(("dp", "ctx")),
        P(("dp", "ctx")),
        P("dp"),
        P(),
        P(),
        P(),
        P(),
        P(),
        P(),
        P(),
        P(),
        P(),
        P(),
        P(),
        P(),
        P("dp", "ctx", None),
    )
    return jax.shard_map(
        body,
        mesh=mesh,
        in_specs=placed,
        out_specs=(
            P("dp", "ctx", None),
            P(),
            P(None, ("dp", "ctx")),
            P(),
            P(None, ("dp", "ctx"), None),
            P(),
            P(("dp", "ctx"), None),
            P(),
            P(),
            P(("dp", "ctx"), None),
            P(("dp", "ctx"), None),
            P(("dp", "ctx"), None),
            P(("dp", "ctx"), None),
        ),
        check_vma=False,
    )
```

profile of v0, /device:TPU:0, one launch (start us, length us, event | category | flops | bytes accessed | tf_op | source)
XLA Modules:
  0.0 2343.1 jit_solution(5708324765580929913)
XLA Ops:
  13.9 11.7 all-to-all-start.1
  40.5 51.6 %while.37 = (s32[]{:T(128)}, f32[4,32,2048]{2,1,0:T(8,128)}, s32[4,32]{1,0:T(4,128)}, s32[4,32,50]{2,1,0:T(8,128)}, bf16[262,16]{0,1:T(8,128)(2,1)}, /*index=5*/...) while((s32[]{:T(128)}, f32[4,32,2048]{2,1,0:T(8,128)}, s32[4,32]{1,0:T(4,128)}, s32[4,32,50]{2,1,0:T(8,128)}, ...), condition=%wide.region_3.4_spmd, body=%wide.region_0.3_spmd.sunk | while | flops 774012864 | bytes 32433860 | solution.py:147
  93.7 8.2 fusion.45
  118.4 10.2 all-to-all-start
  152.0 15.7 all-gather.1
  170.0 15.2 all-gather
  246.6 18.6 reduce-scatter.25.cloned.1.call-done
  275.8 8.5 all-to-all-start.2
  284.4 9.8 all-to-all-done.2
  300.8 14.3 fusion.81
  315.2 235.7 %while.38 = (s32[]{:T(128)}, f32[112,2048]{1,0:T(8,128)}, f32[2048]{0:T(1024)S(1)}, f32[262,16]{0,1:T(8,128)S(1)}, s32[4,32]{1,0:T(4,128)}, /*index=5*/s32[4,32,...) while((s32[]{:T(128)}, f32[112,2048]{1,0:T(8,128)}, ...), condition=%wide.region_28.30_spmd.clone, body=%wide.region_24.29_spmd.clone.sunk | while | flops 2330192384 | bytes 57039644 | solution.py:334
  319.9 9.0 fusion.223
  377.8 9.0 fusion.223
  436.9 9.0 fusion.223
  495.9 9.0 fusion.223
  566.1 13.3 convolution_bitcast_fusion.1
  591.8 383.9 %fusion.153 = (f32[8,2304]{1,0:T(8,128)S(1)}, f32[8,768]{1,0:T(8,128)S(1)}, f32[8,3072]{1,0:T(8,128)}) fusion(f32[768,2304]{1,0:T(8,128)} %fusion.127, f32[768,768]{1,0:T(8,128)S(1)} %fusion.129, f32[768,3072]{1,0:T(8,128)} %fusion.163), kind=kCustom, calls=%all-reduce-scatter.3 | all-reduce-scatter fusion | flops 6291457 | bytes 19070976
  987.6 17.4 collective-permute-start.54
  1206.8 10.8 concatenate.48
  1232.6 52.9 %concatenate.47 = f32[262,2304]{1,0:T(8,128)} concatenate(f32[6,2304]{1,0:T(8,128)S(1)} %collective-permute-done.31, f32[8,2304]{1,0:T(8,128)S(1)} %collective-permute-done.30, f32[8,2304]{1,0:T(8,128)S(1)} %collective-permute-done.29, f32[8,2304]{1,0:T(8,128)S(1)} %collective-permute-done.28, f32[8,2304]{1,0:T(8,128)S(1)} %collective-permute-done.27, ...), dimensions={0} | concatenate | bytes 4829184
  1304.0 56.3 %concatenate.49 = f32[262,3072]{1,0:T(8,128)} concatenate(f32[6,3072]{1,0:T(8,128)} %copy-done.51, f32[8,3072]{1,0:T(8,128)} %copy-done.50, f32[8,3072]{1,0:T(8,128)} %copy-done.52, f32[8,3072]{1,0:T(8,128)} %copy-done.53, f32[8,3072]{1,0:T(8,128)} %copy-done.54, f32[8,3072]{1,0:T(8,128)} %copy-done.55, f32[8,3072]{1,0:T(8,128)} %copy-done.56, f32[8,3072]{1,0:T(8,128)} %copy-done.57, ...), dimensions={0} | concatenate | bytes 6438912
  1364.3 69.5 %all-reduce.11 = (f32[262,16]{0,1:T(8,128)}, f32[2048]{0:T(1024)}, f32[1,4096]{1,0:T(1,128)}, f32[3,768]{1,0:T(4,128)}, f32[3,768]{1,0:T(4,128)}) all-reduce(f32[262,16]{0,1:T(8,128)} %copy-done.108, f32[2048]{0:T(1024)S(1)} %get-tuple-element.377, f32[1,4096]{1,0:T(1,128)} %bitcast.268, ...), channel_id=1, replica_groups=mesh['dp'=32,'ctx'=4] {'dp','ctx'}, use_global_device_ids=true, to_apply=%region_29.31 | all-reduce | flops 14944 | bytes 119552 | tf_op jit(solution)/shard_map/psum | solution.py:349
  1433.8 191.6 %reduce-scatter.23.cloned.1.call-done = f32[24,768]{1,0:T(8,128)} async-done(((f32[3072,768]{1,0:T(8,128)}), f32[24,768]{1,0:T(8,128)}) %reduce-scatter.23.cloned.1.call-update) | async-done | bytes 73744 | tf_op jit(solution)/shard_map/reduce_scatter | solution.py:345
  1625.4 710.5 %reduce-scatter.19.cloned.1.call-done = f32[1,16,4096]{2,1,0:T(8,128)} async-done(((f32[1,2048,4096]{2,1,0:T(8,128)}), f32[1,16,4096]{2,1,0:T(8,128)}) %reduce-scatter.19.cloned.1.call-update) | async-done | bytes 262160 | tf_op jit(solution)/shard_map/reduce_scatter | solution.py:340
  (835 shorter events, 668.4 us)
Async XLA Ops:
  13.9 104.4 %all-to-all-start.1 = ((s32[128,1,1]{2,1,0:T(1,128)}), s32[128,1,1]{2,1,0:T(1,128)}, u32[]{:S(2)}, u32[]{:S(2)}) async-start(s32[128,1,1]{2,1,0:T(1,128)} %copy.155), calls=%async_computation.1 | async-start | bytes 131072 | tf_op jit(solution)/shard_map/all_to_all | solution.py:165
  118.4 20.5 all-to-all-start
  128.5 114.3 %reduce-scatter.27.cloned.1.call-start = ((), (), s32[]{:S(2)}) async-start(), calls=%async_computation.14 | async-start | bytes 983040
  217.9 47.3 %reduce-scatter.25.cloned.1.call-start = ((), (), s32[]{:S(2)}) async-start(), calls=%async_computation.13 | async-start | bytes 983040
  284.3 1149.5 %reduce-scatter.17.cloned.1.call-start = ((), (), s32[]{:S(2)}) async-start(), calls=%async_computation.9 | async-start | bytes 1056768 | tf_op jit(solution)/shard_map/reduce_scatter | solution.py:339
  553.9 879.9 %reduce-scatter.21.cloned.1.call-start = ((), (), s32[]{:S(2)}) async-start(), calls=%async_computation.11 | async-start | bytes 6340608 | tf_op jit(solution)/shard_map/reduce_scatter | solution.py:341
  557.7 1067.7 %reduce-scatter.23.cloned.1.call-start = ((), (), s32[]{:S(2)}) async-start(), calls=%async_computation.12 | async-start | bytes 9510912 | tf_op jit(solution)/shard_map/reduce_scatter | solution.py:345
  564.5 1771.4 %reduce-scatter.19.cloned.1.call-start = ((), (), s32[]{:S(2)}) async-start(), calls=%async_computation.10 | async-start | bytes 33816576 | tf_op jit(solution)/shard_map/reduce_scatter | solution.py:340
  982.4 22.7 collective-permute-start.58
  983.7 22.8 collective-permute-start.57
  985.0 23.0 collective-permute-start.56
  986.3 23.0 collective-permute-start.55
  987.6 25.1 %collective-permute-start.54 = (f32[8,768]{1,0:T(8,128)S(1)}, f32[8,768]{1,0:T(8,128)S(1)}, u32[]{:S(2)}, u32[]{:S(2)}) collective-permute-start(f32[8,768]{1,0:T(8,128)S(1)} %get-tuple-element.556), channel_id=1, source_target_pairs={{0,23},{1,24},{2,25},{3,26},{4,27},{5,28},{6,29},{7,30},{8,31},{9,... | collective-permute-start | bytes 73736
  1138.3 20.9 collective-permute-start.94
  1191.9 25.7 %collective-permute-start.78 = (f32[8,3072]{1,0:T(8,128)}, f32[8,3072]{1,0:T(8,128)S(1)}, u32[]{:S(2)}, u32[]{:S(2)}) collective-permute-start(f32[8,3072]{1,0:T(8,128)} %get-tuple-element.557), channel_id=1, source_target_pairs={{0,15},{1,16},{2,17},{3,18},{4,19},{5,20},{6,21},{7,22},{8,23},{9,... | collective-permute-start | bytes 294920
  1195.0 24.8 %collective-permute-start.77 = (f32[8,3072]{1,0:T(8,128)}, f32[8,3072]{1,0:T(8,128)S(1)}, u32[]{:S(2)}, u32[]{:S(2)}) collective-permute-start(f32[8,3072]{1,0:T(8,128)} %get-tuple-element.557), channel_id=1, source_target_pairs={{0,14},{1,15},{2,16},{3,17},{4,18},{5,19},{6,20},{7,21},{8,22},{9,... | collective-permute-start | bytes 294920
  1196.3 25.7 %collective-permute-start.76 = (f32[8,3072]{1,0:T(8,128)}, f32[8,3072]{1,0:T(8,128)S(1)}, u32[]{:S(2)}, u32[]{:S(2)}) collective-permute-start(f32[8,3072]{1,0:T(8,128)} %get-tuple-element.557), channel_id=1, source_target_pairs={{0,13},{1,14},{2,15},{3,16},{4,17},{5,18},{6,19},{7,20},{8,21},{9,... | collective-permute-start | bytes 294920
  1199.1 25.9 %collective-permute-start.75 = (f32[8,3072]{1,0:T(8,128)}, f32[8,3072]{1,0:T(8,128)S(1)}, u32[]{:S(2)}, u32[]{:S(2)}) collective-permute-start(f32[8,3072]{1,0:T(8,128)} %get-tuple-element.557), channel_id=1, source_target_pairs={{0,12},{1,13},{2,14},{3,15},{4,16},{5,17},{6,18},{7,19},{8,20},{9,... | collective-permute-start | bytes 294920
  1200.9 27.5 %collective-permute-start.74 = (f32[8,3072]{1,0:T(8,128)}, f32[8,3072]{1,0:T(8,128)S(1)}, u32[]{:S(2)}, u32[]{:S(2)}) collective-permute-start(f32[8,3072]{1,0:T(8,128)} %get-tuple-element.557), channel_id=1, source_target_pairs={{0,11},{1,12},{2,13},{3,14},{4,15},{5,16},{6,17},{7,18},{8,19},{9,... | collective-permute-start | bytes 294920
  1217.7 67.9 %collective-permute-start.73 = (f32[8,3072]{1,0:T(8,128)}, f32[8,3072]{1,0:T(8,128)S(1)}, u32[]{:S(2)}, u32[]{:S(2)}) collective-permute-start(f32[8,3072]{1,0:T(8,128)} %get-tuple-element.557), channel_id=1, source_target_pairs={{0,10},{1,11},{2,12},{3,13},{4,14},{5,15},{6,16},{7,17},{8,18},{9,... | collective-permute-start | bytes 294920
  1219.9 69.3 %collective-permute-start.72 = (f32[8,3072]{1,0:T(8,128)}, f32[8,3072]{1,0:T(8,128)S(1)}, u32[]{:S(2)}, u32[]{:S(2)}) collective-permute-start(f32[8,3072]{1,0:T(8,128)} %get-tuple-element.557), channel_id=1, source_target_pairs={{0,9},{1,10},{2,11},{3,12},{4,13},{5,14},{6,15},{7,16},{8,17},{9,1... | collective-permute-start | bytes 294920
  1222.1 69.0 %collective-permute-start.71 = (f32[8,3072]{1,0:T(8,128)}, f32[8,3072]{1,0:T(8,128)S(1)}, u32[]{:S(2)}, u32[]{:S(2)}) collective-permute-start(f32[8,3072]{1,0:T(8,128)} %get-tuple-element.557), channel_id=1, source_target_pairs={{0,8},{1,9},{2,10},{3,11},{4,12},{5,13},{6,14},{7,15},{8,16},{9,17... | collective-permute-start | bytes 294920
  1225.0 71.1 %collective-permute-start.70 = (f32[8,3072]{1,0:T(8,128)}, f32[8,3072]{1,0:T(8,128)S(1)}, u32[]{:S(2)}, u32[]{:S(2)}) collective-permute-start(f32[8,3072]{1,0:T(8,128)} %get-tuple-element.557), channel_id=1, source_target_pairs={{0,7},{1,8},{2,9},{3,10},{4,11},{5,12},{6,13},{7,14},{8,15},{9,16}... | collective-permute-start | bytes 294920
  1228.4 70.0 %collective-permute-start.69 = (f32[8,3072]{1,0:T(8,128)}, f32[8,3072]{1,0:T(8,128)S(1)}, u32[]{:S(2)}, u32[]{:S(2)}) collective-permute-start(f32[8,3072]{1,0:T(8,128)} %get-tuple-element.557), channel_id=1, source_target_pairs={{0,6},{1,7},{2,8},{3,9},{4,10},{5,11},{6,12},{7,13},{8,14},{9,15},... | collective-permute-start | bytes 294920
  (238 other events, 6894.2 us)
Sparse Core Ops, SparseCore 0:
  218.0 22.5 reduce-scatter.26
  243.0 22.1 reduce-scatter.24
  554.0 637.5 reduce-scatter.16
  1197.7 208.1 reduce-scatter.20
  1411.3 214.0 reduce-scatter.22
  1628.2 707.6 reduce-scatter.18
where the time goes:
time: 2360 us; the launch traced here: 2340 us
  waiting for transfers between devices  933 us (40%)
  blocking collectives  484 us (21%)
  local copies, waits for them, and re-layouts  335 us (14%)
  starting transfers between devices  282 us (12%)
  matrix products  181 us (8%)
  other arithmetic  107 us (5%)
    reduce_scatter x1, waiting for transfers between devices, body(): lax.psum_scatter(grad_highway_weight, ('dp', 'ctx'), scatter_dimension=1,...  711 us
    unnamed x1, blocking collectives  384 us
    unnamed x98, starting transfers between devices  252 us
    reduce_scatter x1, waiting for transfers between devices, body(): lax.psum_scatter(grad_down_weight, ('dp', 'ctx'), scatter_dimension=0, ti...  192 us
    unnamed x331, local copies, waits for them, and re-layouts  168 us
    scatter-add x28, local copies, waits for them, and re-layouts, back_block(): grad_padded.at[:, tap_index:tap_index + WORD_CHARS, :]  116 us
    psum x1, blocking collectives, body(): lax.psum((grad_char_table, grad_conv_bias, grad_highway_bias, grad_gain_r...  69.5 us
  transfers between devices with their start and end apart: 105, of which 8 were waited for; matrix products, arithmetic and copies ran while one was open for 29% of the time, Pallas kernels for 0%

commit v1 on v0

v1 whole, which is shorter than its diff:
```python
import functools
import jax
import jax.numpy as jnp
from jax import lax
from jax.experimental import pallas as pl
from jax.experimental.pallas import tpu as pltpu
from jax.sharding import PartitionSpec as P

D = 768
FF = 3072
HEADS = 12
HEAD_DIM = 64
FILTERS = 2048
CHAR_DIM = 16
CHARS = 262
WORD_CHARS = 50
TAPS = 7
SEQ_LEN = 512
WORDS = 128

EPSILON = 1e-05
NEG_LARGE = -1e30
MESH = pl.DeviceIdType.MESH
BF16 = jnp.bfloat16
F32 = jnp.float32

BIAS_ROW = TAPS * CHAR_DIM
ABSENT_ROW = BIAS_ROW + 1
CHAR_ROWS = 272


def filter_widths():
    unit_count = FILTERS // 64
    filter_index = jnp.arange(FILTERS)
    widths = jnp.ones((FILTERS,), jnp.int32)
    for bound_units in (1, 2, 4, 8, 16, 32):
        widths = widths + (filter_index >= unit_count * bound_units).astype(jnp.int32)
    return widths


def tap_mask():
    tap_rows = jnp.arange(TAPS * CHAR_DIM) // CHAR_DIM
    return tap_rows[:, None] < filter_widths()[None, :]


def gate_mix(current, mixed_rows):
    carry_gate = jax.nn.sigmoid(mixed_rows[:, FILTERS:])
    return carry_gate * current + (1.0 - carry_gate) * jax.nn.gelu(mixed_rows[:, :FILTERS])


def norm_parts(values_in, gain_row, shift_row):
    mean_val = jnp.mean(values_in, -1, keepdims=True)
    centred = values_in - mean_val
    inverse = lax.rsqrt(jnp.mean(centred * centred, -1, keepdims=True) + EPSILON)
    normal = centred * inverse
    return (normal * gain_row + shift_row, normal, inverse)


def norm_back(grad_out, normal, inverse, gain_row):
    scaled = grad_out * gain_row
    grad_in = inverse * (
        scaled
        - jnp.mean(scaled, -1, keepdims=True)
        - normal * jnp.mean(scaled * normal, -1, keepdims=True)
    )
    return (grad_in, jnp.sum(grad_out * normal, 0), jnp.sum(grad_out, 0))


def dot(left, right):
    return jnp.dot(left, right, preferred_element_type=F32)


def back_dot(rows_in, weight_rows):
    return lax.dot_general(
        rows_in, weight_rows, (((1,), (1,)), ((), ())), preferred_element_type=F32
    )


def first_dot(left, right):
    return lax.dot_general(left, right, (((0,), (0,)), ((), ())), preferred_element_type=F32)


POOL_COLS = 256


def pool_kernel(ids_ref, table_ref, weight_ref, act_ref, pooled_ref, unfolded_ref, values, rows):
    @pl.when(pl.program_id(0) == 0)
    def _():
        lane = lax.broadcasted_iota(jnp.int32, (WORDS, 128), 1)
        code = lax.broadcasted_iota(jnp.int32, (WORDS, 384), 1)
        values[WORD_CHARS:, :, :] = jnp.zeros((TAPS - 1, WORDS, 128), F32)

        def look_up(place, ids):
            column = ids[:, :1]
            onehot = (column == code).astype(F32).astype(BF16)
            found = dot(onehot, table_ref[...])
            found = jnp.where(lane == BIAS_ROW, 1.0, found)
            absent = jnp.where(column < 0, 1.0, 0.0)
            values[place] = jnp.where(lane == ABSENT_ROW, absent, found)
            return pltpu.roll(ids, 127, 1)

        lax.fori_loop(0, WORD_CHARS, look_up, ids_ref[...])

        @pl.loop(0, WORD_CHARS)
        def _(place):
            taps = values[place]
            for tap in range(1, TAPS):
                taps = jnp.where(lane // CHAR_DIM == tap, values[place + tap], taps)
            unfolded_ref[place] = taps.astype(BF16)

    weight = weight_ref[...]

    def convolve(pair, top):
        left = unfolded_ref[pl.ds(2 * pair, 2)].reshape(2 * WORDS, 128)
        block = dot(left, weight).reshape(2, WORDS, POOL_COLS)
        rows[pl.ds(2 * pair, 2)] = block
        return jnp.maximum(top, jnp.maximum(block[0], block[1]))

    top = lax.fori_loop(
        0, WORD_CHARS // 2, convolve, jnp.full((WORDS, POOL_COLS), -3e38, F32)
    )

    def gather(pair, total):
        block = rows[pl.ds(2 * pair, 2)]
        return total + (jnp.exp(block[0] - top) + jnp.exp(block[1] - top))

    total = lax.fori_loop(0, WORD_CHARS // 2, gather, jnp.zeros((WORDS, POOL_COLS), F32))
    pooled = top + jnp.log(total)
    pooled_ref[...] = pooled
    act_ref[...] = jax.nn.gelu(pooled).astype(BF16)


def pool_words(ids_wide, table_wide, weight_wide):
    return pl.pallas_call(
        pool_kernel,
        grid=(FILTERS // POOL_COLS,),
        out_shape=(
            jax.ShapeDtypeStruct((WORDS, FILTERS), BF16),
            jax.ShapeDtypeStruct((WORDS, FILTERS), F32),
            jax.ShapeDtypeStruct((WORD_CHARS, WORDS, 128), BF16),
        ),
        in_specs=[
            pl.BlockSpec((WORDS, 128), lambda c: (0, 0)),
            pl.BlockSpec((384, 128), lambda c: (0, 0)),
            pl.BlockSpec((128, POOL_COLS), lambda c: (0, c)),
        ],
        out_specs=(
            pl.BlockSpec((WORDS, POOL_COLS), lambda c: (0, c)),
            pl.BlockSpec((WORDS, POOL_COLS), lambda c: (0, c)),
            pl.BlockSpec((WORD_CHARS, WORDS, 128), lambda c: (0, 0, 0)),
        ),
        scratch_shapes=[
            pltpu.VMEM((WORD_CHARS + TAPS - 1, WORDS, 128), F32),
            pltpu.VMEM((WORD_CHARS, WORDS, POOL_COLS), F32),
        ],
        compiler_params=pltpu.CompilerParams(
            dimension_semantics=("arbitrary",), vmem_limit_bytes=40 << 20
        ),
        cost_estimate=pl.CostEstimate(
            flops=2 * WORDS * WORD_CHARS * 128 * FILTERS,
            bytes_accessed=8 << 20,
            transcendentals=WORDS * WORD_CHARS * FILTERS,
        ),
    )(ids_wide, table_wide, weight_wide)


Y, Z, X = 0, 1, 2
ORDERS = ((Y, Z, X), (Z, X, Y), (X, Y, Z))
LEFT_COLS = {"high": 2048, "proj": 2048, "qkv": 768, "out": 768, "up": 768, "down": 3072}
RIGHT_COLS = {"high": 4096, "proj": 768, "qkv": 2304, "out": 768, "up": 3072, "down": 768}
CHUNK_ROWS = {"high": 16, "proj": 16, "qkv": 6, "out": 6, "up": 6, "down": 24}
NAMES = tuple(LEFT_COLS)
GROUPS = tuple((name, group) for name in NAMES for group in range(-(-CHUNK_ROWS[name] // 8)))
GROUP_AT = {key: at for at, key in enumerate(GROUPS)}
RIGHT_AT = {}
for _name in NAMES:
    RIGHT_AT[_name] = sum(RIGHT_COLS[n] for n in NAMES[: NAMES.index(_name)])
RIGHT_ALL = sum(RIGHT_COLS.values())

PIECES = {
    "high": (("high", 0, 0, 1, 0, 4096),),
    "proj": (("proj", 0, 0, 1, 0, 768),),
    "qkv": (("qkv", 0, 0, 0, 1152, 1152),),
    "out": (("out", 0, 0, 0, 384, 384),),
    "up": (("up", 0, 0, 0, 1536, 1536),),
    "down": (("down", 0, 0, 1, 0, 768), ("down", 2, 0, 2, 384, 384)),
}


def cut(pieces, widths):
    parts, rest = [], list(pieces)
    for width in widths:
        part, room = [], width
        while room:
            name, upper, upper_at, lower, lower_at, cols = rest.pop(0)
            used = min(cols, room)
            part.append((name, upper, upper_at, lower, lower_at, used))
            room -= used
            if used < cols:
                rest.insert(
                    0, (name, upper, upper_at + used, lower, lower_at + used, cols - used)
                )
        parts.append(tuple(part))
    assert not rest
    return tuple(parts)


def narrow(piece, most):
    name, upper, upper_at, lower, lower_at, cols = piece
    start = 0
    while start < cols:
        used = min(most, cols - start)
        yield (name, upper, upper_at + start, lower, lower_at + start, used, start)
        start += used


_HIGH = (("high", 0, 0, 1, 0, 2048), ("high", 0, 2048, 1, 2048, 2048))
STREAMS = (
    (("up", "down"), cut(PIECES["down"] + PIECES["up"], (896, 896, 896))),
    (("proj", "qkv", "out"), cut(PIECES["qkv"] + PIECES["out"] + PIECES["proj"], (768, 768, 768))),
    (("high",), cut(_HIGH[:1], (768, 640, 640))),
    ((), cut(_HIGH[1:], (640, 640, 768))),
)
PART_WIDTHS = tuple(
    tuple(sum(piece[5] for piece in part) for part in parts) for _, parts in STREAMS
)
PARTS = tuple(
    (stream, place, width)
    for stream, widths in enumerate(PART_WIDTHS)
    for place, width in enumerate(widths)
) + ((len(STREAMS), 0, 128),)
SMALL_ROWS = 72
SHARED = ((SMALL_ROWS, 128), (16, 384), (8, FILTERS))


def place_of():
    index = lax.axis_index("dp")
    return index // 8, lax.rem(index // 2, 4), lax.rem(index, 2), lax.axis_index("ctx")


def device_of(y, z, core, x):
    return ((y * 4 + z) * 2 + core, x)


def around(value, step):
    return lax.rem(value + step, 4)


def remote(source, target, sems, index, device):
    return pltpu.make_async_remote_copy(
        src_ref=source,
        dst_ref=target,
        send_sem=sems[0].at[index],
        recv_sem=sems[1].at[index],
        device_id=device,
        device_id_type=MESH,
    )


class Part:
    def __init__(self, order, refs, sems, where):
        self.tiles, self.relay1, self.last1, self.relay2, self.last2, self.last3 = refs
        self.order, self.sems, self.where = order, sems, where
        self.width = self.tiles.shape[-1]
        y, z, core, x = where
        self.here = [(y, z, x)[axis] for axis in order]
        self.copies = {}

    def peer(self, level, step):
        y, z, core, x = self.where
        spot = [y, z, x]
        spot[self.order[level]] = around(self.here[level], step)
        return device_of(spot[0], spot[1], core, spot[2])

    def start(self, index, source, target, level, step):
        copy = remote(source, target, self.sems, index, self.peer(level, step))
        copy.start()
        self.copies[index] = copy

    def slices(self, level):
        prefix = tuple(self.here[:level])
        return lambda at, half=None: self.tiles.at[
            prefix + (at,) + (() if half is None else (pl.ds(2 * half, 2),))
        ]

    def buffers(self, level):
        return (self.relay1, self.last1) if level == 0 else (self.relay2, self.last2)

    def ring_start(self, level):
        me, base, tiles = self.here[level], 6 * level, self.slices(level)
        relay, last = self.buffers(level)
        far, right, left = around(me, 2), around(me, 1), around(me, 3)
        self.start(base, tiles(far, 0), relay.at[0], level, 1)
        self.start(base + 1, tiles(far, 1), relay.at[1], level, 3)
        self.start(base + 2, tiles(right, 1), last.at[0, pl.ds(2, 2)], level, 1)
        self.start(base + 3, tiles(left, 0), last.at[1, pl.ds(0, 2)], level, 3)

    def ring_relay(self, level):
        me, base, tiles = self.here[level], 6 * level, self.slices(level)
        relay, last = self.buffers(level)
        for side in (0, 1):
            target = tiles(around(me, (1, 3)[side]), side)
            self.copies[base + side].wait_recv()
            self.add(target, (relay.at[side],), 3 - level)
            self.start(
                base + 4 + side, target, last.at[side, pl.ds(2 * side, 2)], level, (1, 3)[side]
            )

    def ring_end(self, level):
        me, base, tiles = self.here[level], 6 * level, self.slices(level)
        _, last = self.buffers(level)
        for index in range(2, 6):
            self.copies[base + index].wait_recv()
        self.add(tiles(me), (last.at[0], last.at[1]), 3 - level)

    def add(self, target, terms, dims):
        lead = target.shape[:-2]
        count = 1
        for size in lead:
            count *= size

        @pl.loop(0, count)
        def _(flat):
            at, rest = [], flat
            for size in reversed(lead):
                at.insert(0, lax.rem(rest, size))
                rest = rest // size
            at = tuple(at)
            total = target[at].astype(F32)
            for term in terms:
                total = total + term[at].astype(F32)
            target[at] = total.astype(BF16)

    def direct_start(self):
        for step in (1, 2, 3):
            source = self.tiles.at[self.here[0], self.here[1], around(self.here[2], step)]
            self.start(11 + step, source, self.last3.at[step - 1], 2, step)

    def direct_end(self):
        total = self.tiles[tuple(self.here)].astype(F32)
        for step in (1, 2, 3):
            self.copies[11 + step].wait_recv()
            total = total + self.last3[step - 1].astype(F32)
        return total

    def sent(self):
        for copy in self.copies.values():
            copy.wait_send()


class Shared:
    def __init__(self, pair, rings, sems, where):
        self.pair, self.rings, self.sems, self.where = pair, rings, sems, where
        self.copies = []

    def start(self, level, value):
        y, z, core, x = self.where
        if level == 0:
            self.pair[core] = value
            mine = self.pair.at[core]
            peers = [device_of(y, z, 1 - core, x)]
            targets = mine
        else:
            axis = level - 1
            here = (y, z, x)[axis]
            self.rings[axis, here] = value
            mine = self.rings.at[axis, here]
            peers = []
            for step in (1, 2, 3):
                spot = [y, z, x]
                spot[axis] = around(here, step)
                peers.append(device_of(spot[0], spot[1], core, spot[2]))
            targets = mine
        base = 0 if level == 0 else 3 * level - 2
        self.now = []
        for number, peer in enumerate(peers):
            copy = remote(mine, targets, self.sems, base + number, peer)
            copy.start()
            self.now.append(copy)
        self.copies += self.now

    def end(self, level):
        for copy in self.now:
            copy.wait_recv()
        if level == 0:
            return self.pair[0] + self.pair[1]
        ring = self.rings.at[level - 1]
        return (ring[0] + ring[1]) + (ring[2] + ring[3])

    def sent(self):
        for copy in self.copies:
            copy.wait_send()


def pick(rows_per_chunk, group, core, blocks, lanes):
    rows = blocks * 32
    row = lax.broadcasted_iota(jnp.int32, (rows, lanes), 0)
    lane = lax.broadcasted_iota(jnp.int32, (rows, lanes), 1)
    inner = lax.rem(row, 8) + 8 * group
    wanted = ((row // 32 * 2 + core) * 4 + lax.rem(row // 8, 4)) * rows_per_chunk + inner
    hit = jnp.logical_and(wanted == lane, inner < rows_per_chunk)
    return jnp.where(hit, 1.0, 0.0).astype(BF16)


PICK_LANES = {16: 512, 6: 384, 24: 768}


def sums_kernel(schedule, *refs):
    rest = list(refs)

    def take(count):
        taken = rest[:count]
        del rest[:count]
        return taken

    left_in = dict(zip(NAMES, take(6)))
    right_in = dict(zip(NAMES, take(6)))
    chars, unfolded, conv_w, conv_back, pooled, grad_pooled, small_in = take(7)
    outs = dict(zip(NAMES, take(6)))
    out_conv, out_small, out_table, out_bias = take(4)
    left, left_out, right = take(3)
    part_refs = [take(6) for _ in PARTS]
    part_sems = take(2)
    shared_refs = [take(2) for _ in SHARED]
    shared_sems = take(2)
    pair_left_sems, pair_right_sems, load_sems = take(3)
    conv_grad, conv_rows, conv_other, conv_sems = take(4)
    pair_left_sems, pair_right_sems, conv_sems = (
        (sems.at[0], sems.at[1]) for sems in (pair_left_sems, pair_right_sems, conv_sems)
    )
    unfolded_grad, table_grad = take(2)

    where = place_of()
    y, z, core, x = where
    partner = device_of(y, z, 1 - core, x)

    loads = {}
    for at, name in enumerate(NAMES):
        cols = pl.ds(RIGHT_AT[name], RIGHT_COLS[name])
        loads[name] = pltpu.make_async_copy(
            right_in[name], right.at[pl.ds(0, WORDS), cols], load_sems.at[at]
        )
        loads[name].start()

    barrier = pltpu.get_barrier_semaphore()
    greeted = [partner]
    for step in (1, 2, 3):
        greeted.append(device_of(around(y, step), z, core, x))
        greeted.append(device_of(y, around(z, step), core, x))
        greeted.append(device_of(y, z, core, around(x, step)))
    for device in greeted:
        pl.semaphore_signal(barrier, inc=1, device_id=device, device_id_type=MESH)
    pl.semaphore_wait(barrier, len(greeted))

    parts = [
        Part(
            ORDERS[place],
            part_refs[at],
            (part_sems[0].at[at], part_sems[1].at[at]),
            where,
        )
        for at, (_, place, _) in enumerate(PARTS)
    ]
    shared = [
        Shared(pair, rings, (shared_sems[0].at[at], shared_sems[1].at[at]), where)
        for at, (pair, rings) in enumerate(shared_refs)
    ]

    right_sent = {}
    for at, name in enumerate(("down", "up", "qkv", "out", "proj", "high")):
        cols = pl.ds(RIGHT_AT[name], RIGHT_COLS[name])
        right_sent[name] = remote(
            right_in[name],
            right.at[pl.ds(WORDS, WORDS), cols],
            pair_right_sems,
            at,
            partner,
        )
        right_sent[name].start()

    picks = {}

    def picked(rows_per_chunk, group, mine):
        key = (rows_per_chunk, group, mine)
        if key not in picks:
            lanes = PICK_LANES[rows_per_chunk]
            picks[key] = pick(
                rows_per_chunk,
                group,
                core if mine else 1 - core,
                lanes // (8 * rows_per_chunk),
                lanes,
            )
        return picks[key]

    left_sent = {}

    def prepare(stream):
        for name in STREAMS[stream][0]:
            rows_per_chunk = CHUNK_ROWS[name]
            lanes = PICK_LANES[rows_per_chunk]
            ys = lanes // (32 * rows_per_chunk)
            groups = -(-rows_per_chunk // 8)
            first = GROUP_AT[name, 0]
            for group in range(groups):
                for block in range(4 // ys):
                    source = left_in[name][:, block * lanes : (block + 1) * lanes]
                    for mine in (False, True):
                        rows = back_dot(picked(rows_per_chunk, group, mine), source)
                        rows = rows.astype(BF16).reshape(ys, 128, WORDS)
                        span = pl.ds(block * ys, ys)
                        if mine:
                            left[first + group, span, :, 0:WORDS] = rows
                        else:
                            left_out[first + group, span] = rows
            span = pl.ds(first, groups)
            left_sent[name] = remote(
                left_out.at[span],
                left.at[span, :, :, pl.ds(WORDS, WORDS)],
                pair_left_sems,
                NAMES.index(name),
                partner,
            )
            left_sent[name].start()

    def multiply(stream):
        for name in STREAMS[stream][0]:
            loads[name].wait()
            right_sent[name].wait_recv()
            left_sent[name].wait_recv()
        for at, (of, place, _) in enumerate(PARTS):
            if of != stream:
                continue
            tiles, order = part_refs[at][0], ORDERS[place]
            offset = 0
            for piece in STREAMS[stream][1][place]:
                for name, upper, upper_at, lower, lower_at, cols, start in narrow(piece, 512):
                    base, first = RIGHT_AT[name], GROUP_AT[name, 0]
                    lanes = pl.ds(offset + start, cols)

                    @pl.loop(0, 4)
                    def _(row):
                        halves = []
                        for group, column in ((upper, upper_at), (lower, lower_at)):
                            factor = right[:, base + column : base + column + cols]
                            block = dot(left[first + group, row], factor)
                            halves.append(block.reshape(16, 1, 8, cols))
                        both = jnp.concatenate(halves, axis=1).reshape(4, 4, 16, cols)
                        both = both.astype(BF16)
                        for at_z in range(4):
                            for at_x in range(4):
                                spot = tuple((row, at_z, at_x)[axis] for axis in order)
                                tiles[spot + (slice(None), lanes)] = both[at_z, at_x]

                offset += piece[5]
        ring(stream, lambda part: part.ring_start(0))

    def ring(stream, action):
        for at, (of, _, _) in enumerate(PARTS):
            if of == stream:
                action(parts[at])

    def finish(stream):
        for at, (of, place, _) in enumerate(PARTS):
            if of != stream:
                continue
            total = parts[at].direct_end()
            if stream == len(STREAMS):
                out_conv[...] = total
                continue
            offset = 0
            for name, upper, upper_at, lower, lower_at, cols in STREAMS[stream][1][place]:
                block = total[:, offset : offset + cols]
                for group, column, top in ((upper, upper_at, 0), (lower, lower_at, 8)):
                    rows = min(8, CHUNK_ROWS[name] - 8 * group)
                    outs[name][8 * group : 8 * group + rows, column : column + cols] = block[
                        top : top + rows
                    ]
                offset += cols

    lane = lax.broadcasted_iota(jnp.int32, (WORDS, 128), 1)

    def conv_start():
        unfolded_grad[0 : TAPS - 1] = jnp.zeros((TAPS - 1, WORDS, 128), F32)
        conv_grad[...] = jnp.zeros_like(conv_grad)
        table_grad[...] = jnp.zeros_like(table_grad)

    def conv_pair(pair):
        two = unfolded[pl.ds(2 * pair, 2)].reshape(2 * WORDS, 128)
        unit = jnp.where(
            lax.broadcasted_iota(jnp.int32, (128, 128), 0)
            == lax.broadcasted_iota(jnp.int32, (128, 128), 1),
            1.0,
            0.0,
        ).astype(BF16)
        turned = back_dot(unit, two).astype(BF16)
        back = jnp.zeros((2 * WORDS, 128), F32)
        for block in range(4):
            cols = slice(block * 512, (block + 1) * 512)
            conv = dot(two, conv_w[:, cols]).reshape(2, WORDS, 512)
            shares = jnp.exp(conv - pooled[:, cols][None]) * grad_pooled[:, cols][None]
            shares = shares.astype(BF16).reshape(2 * WORDS, 512)
            conv_grad[:, cols] += dot(turned, shares)
            back = back + dot(shares, conv_back[cols, :])
        unfolded_grad[pl.ds(2 * pair + TAPS - 1, 2)] = back.reshape(2, WORDS, 128)
        high_low, onehots = [], []
        for side in (0, 1):
            place = 2 * pair + side
            taps = unfolded_grad[place + TAPS - 1]
            for tap in range(1, TAPS):
                taps = jnp.where(
                    lane // CHAR_DIM == tap, unfolded_grad[place + TAPS - 1 - tap], taps
                )
            taps = jnp.where(lane < BIAS_ROW, taps, 0.0)
            high = taps.astype(BF16)
            low = (taps - high.astype(F32)).astype(BF16)
            high_low.append(jnp.concatenate([high, low], axis=1))
            code = lax.broadcasted_iota(jnp.int32, (CHAR_ROWS, WORDS), 0)
            onehots.append(jnp.where(chars[place] == code, 1.0, 0.0).astype(BF16))
        table_grad[0:CHAR_ROWS, :] += dot(
            jnp.concatenate(onehots, axis=1), jnp.concatenate(high_low, axis=0)
        )

    conv_pairs = []

    def conv_end():
        for block in range(16):
            turned = conv_grad[:, block * 128 : (block + 1) * 128].T
            conv_rows[block] = turned.reshape(2, 64, 128)
        copy = remote(conv_rows.at[:, 1 - core], conv_other, conv_sems, 0, partner)
        copy.start()
        conv_pairs.append(copy)
        table = table_grad[:, 0:128] + table_grad[:, 128:256]
        turned = jnp.concatenate(
            [table[128 * block : 128 * (block + 1)].T for block in range(3)], axis=1
        )
        folded = turned[0:CHAR_DIM]
        for tap in range(1, TAPS):
            folded = folded + turned[tap * CHAR_DIM : (tap + 1) * CHAR_DIM]
        shared[1].start(0, folded)
        shared[2].start(0, conv_grad[BIAS_ROW : BIAS_ROW + 8, :])

    def conv_ring():
        conv_pairs[0].wait_recv()
        tiles = part_refs[-1][0]

        @pl.loop(0, 4)
        def _(at):
            for inner in range(4):
                row = at * 4 + inner
                total = conv_rows[row, core] + conv_other[row]
                tiles[at, inner] = total.astype(BF16).reshape(4, 16, 128)

        ring(len(STREAMS), lambda part: part.ring_start(0))

    def shared_step(which, level):
        if level < 3:
            shared[which].start(level + 1, shared[which].end(level))
        else:
            (out_small, out_table, out_bias)[which][...] = shared[which].end(level)

    actions = {
        "prepare": prepare,
        "multiply": multiply,
        "relay1": lambda s: ring(s, lambda part: part.ring_relay(0)),
        "end1": lambda s: ring(s, lambda part: (part.ring_end(0), part.ring_start(1))),
        "relay2": lambda s: ring(s, lambda part: part.ring_relay(1)),
        "end2": lambda s: ring(s, lambda part: (part.ring_end(1), part.direct_start())),
        "finish": finish,
        "conv_start": conv_start,
        "conv": lambda first, last: lax.fori_loop(
            first, last, lambda pair, nothing: (conv_pair(pair), nothing)[1], 0
        ),
        "conv_end": conv_end,
        "conv_ring": conv_ring,
        "small": lambda: shared[0].start(0, small_in[...]),
        "shared": shared_step,
    }
    for name, *given in schedule:
        actions[name](*given)

    for part in parts:
        part.sent()
    for one in shared:
        one.sent()
    for name in NAMES:
        right_sent[name].wait_send()
        left_sent[name].wait_send()
    conv_pairs[0].wait_send()


SCHEDULE = (
    ("prepare", 0),
    ("prepare", 1),
    ("multiply", 0),
    ("prepare", 2),
    ("small",),
    ("multiply", 1),
    ("relay1", 0),
    ("shared", 0, 0),
    ("multiply", 2),
    ("relay1", 1),
    ("multiply", 3),
    ("conv_start",),
    ("conv", 0, 3),
    ("end1", 0),
    ("shared", 0, 1),
    ("conv", 3, 6),
    ("relay1", 2),
    ("relay1", 3),
    ("end1", 1),
    ("relay2", 0),
    ("shared", 0, 2),
    ("conv", 6, 11),
    ("end2", 0),
    ("relay2", 1),
    ("shared", 0, 3),
    ("conv", 11, 16),
    ("end1", 2),
    ("finish", 0),
    ("end2", 1),
    ("conv", 16, 20),
    ("end1", 3),
    ("relay2", 2),
    ("finish", 1),
    ("conv", 20, 25),
    ("conv_end",),
    ("relay2", 3),
    ("end2", 2),
    ("conv_ring",),
    ("shared", 1, 0),
    ("shared", 2, 0),
    ("end2", 3),
    ("relay1", 4),
    ("finish", 2),
    ("shared", 1, 1),
    ("shared", 2, 1),
    ("end1", 4),
    ("finish", 3),
    ("relay2", 4),
    ("shared", 1, 2),
    ("shared", 2, 2),
    ("end2", 4),
    ("shared", 1, 3),
    ("shared", 2, 3),
    ("finish", 4),
)


def sum_gradients(left, right, chars, unfolded, conv_w, conv_back, pooled, grad_pooled, small):
    part_scratch = []
    for _, _, width in PARTS:
        part_scratch += [
            pltpu.VMEM((4, 4, 4, 16, width), BF16),
            pltpu.VMEM((2, 2, 4, 16, width), BF16),
            pltpu.VMEM((2, 4, 4, 16, width), BF16),
            pltpu.VMEM((2, 2, 16, width), BF16),
            pltpu.VMEM((2, 4, 16, width), BF16),
            pltpu.VMEM((3, 16, width), BF16),
        ]
    part_scratch += [pltpu.SemaphoreType.DMA((len(PARTS), 15))] * 2
    for shape in SHARED:
        part_scratch += [pltpu.VMEM((2,) + shape, F32), pltpu.VMEM((3, 4) + shape, F32)]
    part_scratch += [pltpu.SemaphoreType.DMA((len(SHARED), 10))] * 2
    scratch = (
        [
            pltpu.VMEM((len(GROUPS), 4, 128, 2 * WORDS), BF16),
            pltpu.VMEM((len(GROUPS), 4, 128, WORDS), BF16),
            pltpu.VMEM((2 * WORDS, RIGHT_ALL), BF16),
        ]
        + part_scratch
        + [
            pltpu.SemaphoreType.DMA((2, 6)),
            pltpu.SemaphoreType.DMA((2, 6)),
            pltpu.SemaphoreType.DMA((6,)),
            pltpu.VMEM((128, FILTERS), F32),
            pltpu.VMEM((16, 2, 64, 128), F32),
            pltpu.VMEM((16, 64, 128), F32),
            pltpu.SemaphoreType.DMA((2, 1)),
            pltpu.VMEM((WORD_CHARS + TAPS - 1, WORDS, 128), F32),
            pltpu.VMEM((384, 256), F32),
        ]
    )
    whole = pl.BlockSpec(memory_space=pltpu.VMEM)
    shapes = [(CHUNK_ROWS[name], RIGHT_COLS[name]) for name in NAMES]
    shapes += [(16, 128)] + list(SHARED)
    results = pl.pallas_call(
        functools.partial(sums_kernel, SCHEDULE),
        out_shape=tuple(jax.ShapeDtypeStruct(shape, F32) for shape in shapes),
        in_specs=[whole] * 6 + [pl.BlockSpec(memory_space=pl.ANY)] * 6 + [whole] * 7,
        out_specs=tuple(whole for _ in shapes),
        scratch_shapes=scratch,
        compiler_params=pltpu.CompilerParams(
            collective_id=1, has_side_effects=True, vmem_limit_bytes=64 << 20
        ),
    )(
        *[left[name] for name in NAMES],
        *[right[name] for name in NAMES],
        chars,
        unfolded,
        conv_w,
        conv_back,
        pooled,
        grad_pooled,
        small,
    )
    return dict(zip(NAMES, results)), results[6:]


def body(
    char_ids,
    word_lengths,
    word_home,
    seq_lengths,
    char_table,
    conv_weight,
    conv_bias,
    highway_weight,
    highway_bias,
    proj_weight,
    norm_gain,
    norm_shift,
    qkv_weight,
    out_weight,
    up_weight,
    down_weight,
    cotangent,
):
    group_len = cotangent.shape[1]
    ctx_size = lax.axis_size("ctx")
    full_len = group_len * ctx_size
    head_scale = HEAD_DIM ** (-0.5)
    conv_masked = jnp.where(tap_mask(), conv_weight, jnp.zeros_like(conv_weight))
    high_shift = highway_bias.astype(F32)
    gain_rows = norm_gain.astype(F32)
    shift_rows = norm_shift.astype(F32)

    present = jnp.arange(WORD_CHARS)[None, :] < word_lengths[:, None]
    ids = jnp.where(present, char_ids, -1)
    ids_wide = jnp.pad(ids, ((0, 0), (0, 128 - WORD_CHARS)), constant_values=-1)
    chars = ids.T.reshape(WORD_CHARS, 1, WORDS)
    table_wide = jnp.pad(
        jnp.tile(char_table, (1, TAPS)), ((0, 384 - CHARS), (0, 128 - TAPS * CHAR_DIM))
    )
    conv_w = jnp.concatenate(
        [
            conv_masked,
            conv_bias[None, :],
            jnp.full((1, FILTERS), NEG_LARGE, BF16),
            jnp.zeros((128 - ABSENT_ROW - 1, FILTERS), BF16),
        ],
        axis=0,
    )
    conv_back = jnp.pad(conv_masked, ((0, 128 - TAPS * CHAR_DIM), (0, 0))).T

    act, pooled, unfolded = pool_words(ids_wide, table_wide, conv_w)
    mixed_rows = dot(act, highway_weight[0]) + high_shift[0]
    final_rows = gate_mix(act.astype(F32), mixed_rows).astype(BF16)
    embedded = dot(final_rows, proj_weight).astype(BF16)

    seq_index = word_home // SEQ_LEN
    pos_index = word_home % SEQ_LEN
    target = seq_index * ctx_size + pos_index // group_len
    slot = pos_index % group_len
    numbers = jnp.arange(WORDS)
    send_pick = (target[None, :] == numbers[:, None]).astype(BF16)
    carried = jnp.concatenate(
        [embedded, jnp.broadcast_to(slot[:, None], (WORDS, 128)).astype(BF16)], axis=1
    )
    to_send = dot(send_pick, carried).astype(BF16)
    arrived = lax.all_to_all(to_send, ("dp", "ctx"), split_axis=0, concat_axis=0, tiled=True)
    arrived_slot = arrived[:, D].astype(jnp.int32)
    place_pick = (arrived_slot[None, :] == numbers[:, None]).astype(BF16)
    word_rows = dot(place_pick, arrived[:, :D])

    first_f, first_normal, first_inv = norm_parts(word_rows, gain_rows[0], shift_rows[0])
    first_norm = first_f.astype(BF16)
    joint_proj = dot(first_norm, qkv_weight).astype(BF16)
    queries = joint_proj[:, :D].reshape(group_len, HEADS, HEAD_DIM)
    both_all = lax.all_gather(joint_proj[:, D:], "ctx", axis=0, tiled=True)
    key_heads = both_all[:, :D].reshape(full_len, HEADS, HEAD_DIM)
    value_heads = both_all[:, D:].reshape(full_len, HEADS, HEAD_DIM)
    key_valid = jnp.arange(full_len) < seq_lengths[0]
    valid_wide = key_valid[None, None, :]
    scores = (
        jnp.einsum("qhd,khd->hqk", queries, key_heads, preferred_element_type=F32) * head_scale
    )
    masked = jnp.where(valid_wide, scores, NEG_LARGE)
    top_val = jnp.max(masked, -1, keepdims=True)
    expo_val = jnp.where(valid_wide, jnp.exp(masked - top_val), 0.0)
    totals = jnp.sum(expo_val, -1, keepdims=True)
    probs = expo_val / totals
    probs_low = probs.astype(BF16)
    context = (
        jnp.einsum("hqk,khd->qhd", probs_low, value_heads, preferred_element_type=F32)
        .reshape(WORDS, D)
        .astype(BF16)
    )
    attn_out = dot(context, out_weight)
    mid_f, mid_normal, mid_inv = norm_parts(
        first_norm.astype(F32) + attn_out, gain_rows[1], shift_rows[1]
    )
    middle = mid_f.astype(BF16)
    up_proj = dot(middle, up_weight)
    hidden_act = jax.nn.gelu(up_proj).astype(BF16)
    down_proj = dot(hidden_act, down_weight)
    out_f, out_normal, out_inv = norm_parts(
        middle.astype(F32) + down_proj, gain_rows[2], shift_rows[2]
    )
    out_hidden = out_f.astype(BF16).reshape(1, group_len, D)

    grad_rows = cotangent.reshape(WORDS, D).astype(F32)
    grad_pre2, gain_two, shift_two = norm_back(grad_rows, out_normal, out_inv, gain_rows[2])
    grad_down = grad_pre2.astype(BF16)
    _, gelu_pull = jax.vjp(jax.nn.gelu, up_proj)
    grad_up = gelu_pull(back_dot(grad_down, down_weight))[0].astype(BF16)
    grad_mid = grad_pre2 + back_dot(grad_up, up_weight)
    grad_pre1, gain_one, shift_one = norm_back(grad_mid, mid_normal, mid_inv, gain_rows[1])
    grad_attn = grad_pre1.astype(BF16)
    grad_context = (
        back_dot(grad_attn, out_weight).astype(BF16).reshape(group_len, HEADS, HEAD_DIM)
    )
    grad_probs = jnp.einsum("qhd,khd->hqk", grad_context, value_heads, preferred_element_type=F32)
    delta_rows = jnp.sum(probs * grad_probs, -1, keepdims=True)
    grad_scores = (probs * (grad_probs - delta_rows)).astype(BF16)
    grad_query = (
        jnp.einsum("hqk,khd->qhd", grad_scores, key_heads, preferred_element_type=F32) * head_scale
    )
    grad_keys = (
        jnp.einsum("hqk,qhd->khd", grad_scores, queries, preferred_element_type=F32) * head_scale
    )
    grad_values = jnp.einsum("hqk,qhd->khd", probs_low, grad_context, preferred_element_type=F32)
    grad_both = jnp.concatenate(
        [grad_keys.reshape(full_len, D), grad_values.reshape(full_len, D)], axis=1
    ).astype(BF16)
    both_sum = lax.psum_scatter(grad_both, "ctx", scatter_dimension=0, tiled=True)
    grad_joint = jnp.concatenate([grad_query.reshape(WORDS, D).astype(BF16), both_sum], axis=-1)
    grad_first = back_dot(grad_joint, qkv_weight) + grad_pre1
    grad_words, gain_zero, shift_zero = norm_back(grad_first, first_normal, first_inv, gain_rows[0])

    send_back = first_dot(place_pick, grad_words.astype(BF16)).astype(BF16)
    returned = lax.all_to_all(send_back, ("dp", "ctx"), split_axis=0, concat_axis=0, tiled=True)
    grad_embedded = first_dot(send_pick, returned).astype(BF16)
    grad_act = back_dot(grad_embedded, proj_weight)
    _, mix_pull = jax.vjp(gate_mix, act.astype(F32), mixed_rows)
    grad_direct, grad_mixed = mix_pull(grad_act)
    grad_mixed = grad_mixed.astype(BF16)
    high_bias = jnp.sum(grad_mixed.astype(F32), 0)
    grad_act = grad_direct + back_dot(grad_mixed, highway_weight[0])
    _, pool_pull = jax.vjp(jax.nn.gelu, pooled)
    grad_pooled = pool_pull(grad_act)[0]

    small = jnp.concatenate(
        [high_bias, gain_zero, gain_one, gain_two, shift_zero, shift_one, shift_two]
    ).reshape(-1, 128)
    small = jnp.pad(small, ((0, SMALL_ROWS - small.shape[0]), (0, 0)))
    sums, (conv_sum, small_sum, table_sum, bias_sum) = sum_gradients(
        {
            "high": act,
            "proj": final_rows,
            "qkv": first_norm,
            "out": context,
            "up": middle,
            "down": hidden_act,
        },
        {
            "high": grad_mixed,
            "proj": grad_embedded,
            "qkv": grad_joint,
            "out": grad_attn,
            "up": grad_up,
            "down": grad_down,
        },
        chars,
        unfolded,
        conv_w,
        conv_back,
        pooled,
        grad_pooled,
        small,
    )
    small_sum = small_sum.reshape(-1)
    norm_sum = small_sum[2 * FILTERS : 2 * FILTERS + 6 * D].reshape(2, 3, D)
    conv_shard = conv_sum[:, : TAPS * CHAR_DIM].T
    me = lax.axis_index("dp") * ctx_size + lax.axis_index("ctx")
    filters = me * conv_shard.shape[1] + jnp.arange(conv_shard.shape[1])
    taps = jnp.arange(TAPS * CHAR_DIM) // CHAR_DIM
    conv_shard = jnp.where(taps[:, None] < jnp.take(filter_widths(), filters)[None, :], conv_shard, 0.0)
    return (
        out_hidden,
        table_sum[:, :CHARS].T,
        conv_shard,
        bias_sum[0],
        sums["high"][None],
        small_sum[None, : 2 * FILTERS],
        sums["proj"],
        norm_sum[0],
        norm_sum[1],
        sums["qkv"],
        sums["out"],
        sums["up"],
        sums["down"],
    )


def solution(mesh):
    placed = (
        P(("dp", "ctx"), None),
        P(("dp", "ctx")),
        P(("dp", "ctx")),
        P("dp"),
        P(),
        P(),
        P(),
        P(),
        P(),
        P(),
        P(),
        P(),
        P(),
        P(),
        P(),
        P(),
        P("dp", "ctx", None),
    )
    return jax.shard_map(
        body,
        mesh=mesh,
        in_specs=placed,
        out_specs=(
            P("dp", "ctx", None),
            P(),
            P(None, ("dp", "ctx")),
            P(),
            P(None, ("dp", "ctx"), None),
            P(),
            P(("dp", "ctx"), None),
            P(),
            P(),
            P(("dp", "ctx"), None),
            P(("dp", "ctx"), None),
            P(("dp", "ctx"), None),
            P(("dp", "ctx"), None),
        ),
        check_vma=False,
    )
```

time: 2360 us -> 409 us (0.17)
  waiting for transfers between devices: 933 us -> 45.9 us
  blocking collectives: 484 us -> 0 us
  local copies, waits for them, and re-layouts: 335 us -> 42.2 us
  starting transfers between devices: 282 us -> 30.1 us
  Pallas kernels: 0 us -> 189 us
  matrix products: 181 us -> 60 us
  other arithmetic: 107 us -> 18.3 us
    reduce_scatter x4 -> x1, waiting for transfers between devices: 902 us -> 14.6 us  [body(): lax.psum_scatter(grad_both, 'ctx', scatter_dimension=0, tiled=True)]
    unnamed x1 -> x0, blocking collectives: 384 us -> none
    unnamed x98 -> x0, starting transfers between devices: 252 us -> none
    pallas_call x0 -> x2, Pallas kernels: none -> 189 us  [the longest x1 130 us: sum_gradients(): pl.pallas_call(functools.partial(sums_kernel, SCHEDULE), out_shape=tuple(...]
    unnamed x331 -> x115, local copies, waits for them, and re-layouts: 168 us -> 16.2 us
    scatter-add x28 -> x0, local copies, waits for them, and re-layouts: 116 us -> none  [back_block(): grad_padded.at[:, tap_index:tap_index + WORD_CHARS, :]]
    dot_general x42 -> x15, matrix products: 117 us -> 29.9 us  [the longest x8 18.5 us: dot(): return jnp.dot(left, right, preferred_element_type=F32)]
    psum x1 -> x0, blocking collectives: 69.5 us -> none  [body(): lax.psum((grad_char_table, grad_conv_bias, grad_highway_bias, grad_gain_r...]
  transfers between devices with their start and end apart: 105 -> 4, of which waited for: 8 -> 4; matrix products, arithmetic and copies ran while one was open for 29% -> 3% of each run, Pallas kernels for 0% -> 0%
where the time goes in v1:
time: 409 us; the launch traced here: 401 us
  Pallas kernels  189 us (46%)
  matrix products  60 us (15%)
  waiting for transfers between devices  45.9 us (11%)
  local copies, waits for them, and re-layouts  42.2 us (10%)
  starting transfers between devices  30.1 us (7%)
  other arithmetic  18.3 us (4%)
  between operations  15.8 us (4%)
    pallas_call x1, Pallas kernels, sum_gradients(): pl.pallas_call(functools.partial(sums_kernel, SCHEDULE), out_shape=tuple(...  130 us
    pallas_call x1, Pallas kernels, pool_words(): pl.pallas_call(pool_kernel, grid=(FILTERS // POOL_COLS,), out_shape=(jax....  59.5 us
    dot_general x6, matrix products, back_dot(): lax.dot_general(rows_in, weight_rows, (((1,), (1,)), ((), ())), preferred...  27.1 us
    dot_general x8, matrix products, dot(): return jnp.dot(left, right, preferred_element_type=F32)  18.5 us
    unnamed x115, local copies, waits for them, and re-layouts  16.2 us
    reduce_scatter x1, waiting for transfers between devices, body(): lax.psum_scatter(grad_both, 'ctx', scatter_dimension=0, tiled=True)  14.6 us
    all_gather x1, waiting for transfers between devices, body(): both_all = lax.all_gather(joint_proj[:, D:], 'ctx', axis=0, tiled=True)  11.9 us
    all_to_all x1, starting transfers between devices, body(): lax.all_to_all(to_send, ('dp', 'ctx'), split_axis=0, concat_axis=0, tiled...  11.1 us
  transfers between devices with their start and end apart: 4, of which 4 were waited for; matrix products, arithmetic and copies ran while one was open for 3% of the time, Pallas kernels for 0%

profile of v1, /device:TPU:0, one launch (start us, length us, event | category | flops | bytes accessed | tf_op | source)
XLA Modules:
  0.0 401.4 jit_solution(14112706606565314781)
XLA Ops:
  11.9 59.5 %shard_map.264 = (bf16[128,2048]{1,0:T(8,128)(2,1)S(1)}, f32[128,2048]{1,0:T(8,128)S(1)}, bf16[50,128,128]{2,1,0:T(8,128)(2,1)S(1)}) custom-call(s32[128,128]{1,0:T(8,128)S(1)} %pad.22.clone.ids_ref, bf16[384,128]{1,0:T(8,128)(2,1)S(1)} %pad.23.table_ref, bf16[128,2048]{1,0:T(8,128)(2,1)S(1)} %copy.81.weight_ref.refs_14_), custom_call_target="tpu_custom_call" | custom-call | flops 3355443200 | bytes 8388608 | tf_op jit(solution)/shard_map/pallas_call | solution.py:134
  71.5 9.3 %fusion.5 = f32[128,4096]{1,0:T(8,128)S(1)} fusion(bf16[128,2048]{1,0:T(8,128)(2,1)S(1)} %get-tuple-element.26.refs_0_, bf16[1,2048,4096]{2,1,0:T(8,128)(2,1)} %param.24, f32[4096]{0:T(1024)S(1)} %bitcast.137), kind=kOutput, calls=%fused_computation.6 | convolution fusion | flops 2148007936 | bytes 19415040 | tf_op jit(solution)/shard_map/dot_general | solution.py:70
  86.8 11.1 %all-to-all-start = ((bf16[128,2,448]{2,1,0:T(2,128)(2,1)}), bf16[128,2,448]{2,1,0:T(2,128)(2,1)S(1)}, u32[]{:S(2)}, u32[]{:S(2)}) async-start(bf16[128,2,448]{2,1,0:T(2,128)(2,1)} %reshape.256), calls=%async_computation | async-start | bytes 524288 | tf_op jit(solution)/shard_map/all_to_all | solution.py:871
  98.1 10.4 %all-to-all-done = bf16[128,2,448]{2,1,0:T(2,128)(2,1)S(1)} async-done(((bf16[128,2,448]{2,1,0:T(2,128)(2,1)}), bf16[128,2,448]{2,1,0:T(2,128)(2,1)S(1)}, u32[]{:S(2)}, u32[]{:S(2)}) %all-to-all-start) | async-done | bytes 229408 | tf_op jit(solution)/shard_map/all_to_all | solution.py:871
  110.0 2.7 convolution_convert_fusion
  113.5 10.0 %reduce-scatter.2.cloned.1.call-start = ((), (), s32[]{:S(2)}) async-start(), calls=%async_computation.4 | async-start | bytes 1966080 | tf_op jit(solution)/shard_map/reduce_scatter | solution.py:936
  124.4 11.9 %all-gather.2.cloned.1.call-done = bf16[512,1536]{1,0:T(8,128)(2,1)} async-done(((bf16[128,1536]{1,0:T(8,128)(2,1)}), bf16[512,1536]{1,0:T(8,128)(2,1)}) %all-gather.2.cloned.1.call-update) | async-done | bytes 1572880 | tf_op jit(solution)/shard_map/all_gather | solution.py:880
  136.3 2.7 fusion.84
  140.3 2.6 copy.83
  142.9 2.9 fusion.87
  145.9 3.0 convolution_convert_fusion.6
  149.7 4.1 %multiply_convert_fusion.2 = (bf16[128,3072]{1,0:T(8,128)(2,1)S(1)}, f32[128,3072]{1,0:T(8,128)S(1)}) fusion(bf16[128,768]{1,0:T(8,128)(2,1)S(1)} %add_convert_fusion.2.refs_4_, bf16[768,3072]{1,0:T(8,128)(2,1)} %param.31), kind=kOutput, calls=%fused_computation.27 | convolution fusion | flops 607518720 | bytes 7274496 | tf_op jit(solution)/shard_map/dot_general | solution.py:70
  158.1 2.4 multiply_reduce_fusion.1
  162.8 2.8 multiply_reduce_fusion
  172.0 2.3 copy.88
  174.3 2.6 pad_maximum_fusion
  184.7 2.5 fusion.22
  188.2 14.6 %reduce-scatter.2.cloned.1.call-done = bf16[128,1536]{1,0:T(8,128)(2,1)} async-done(((bf16[512,1536]{1,0:T(8,128)(2,1)}), bf16[128,1536]{1,0:T(8,128)(2,1)}) %reduce-scatter.2.cloned.1.call-update) | async-done | bytes 393232 | tf_op jit(solution)/shard_map/reduce_scatter | solution.py:936
  202.8 3.6 multiply_reduce_fusion.2
  208.3 8.9 %all-to-all-start.1 = ((bf16[128,2,384]{2,1,0:T(2,128)(2,1)}), bf16[128,2,384]{2,1,0:T(2,128)(2,1)S(1)}, u32[]{:S(2)}, u32[]{:S(2)}) async-start(bf16[128,2,384]{2,1,0:T(2,128)(2,1)} %reshape.258), calls=%async_computation.2 | async-start | bytes 393216 | tf_op jit(solution)/shard_map/all_to_all | solution.py:942
  218.1 9.0 %all-to-all-done.1 = bf16[128,2,384]{2,1,0:T(2,128)(2,1)S(1)} async-done(((bf16[128,2,384]{2,1,0:T(2,128)(2,1)}), bf16[128,2,384]{2,1,0:T(2,128)(2,1)S(1)}, u32[]{:S(2)}, u32[]{:S(2)}) %all-to-all-start.1) | async-done | bytes 196640 | tf_op jit(solution)/shard_map/all_to_all | solution.py:942
  227.5 5.3 %fusion.34 = (f32[128,2048]{1,0:T(8,128)S(1)}, f32[128,2048]{1,0:T(8,128)S(1)}, f32[128,2048]{1,0:T(8,128)}) fusion(f32[128,4096]{1,0:T(8,128)} %copy-done.4, bf16[128,2048]{1,0:T(8,128)(2,1)S(1)} %get-tuple-element.26.refs_0_, bf16[128,768]{1,0:T(8,128)(2,1)S(1)} %convolution_convert_fusion.3.refs_7_, bf16[2048,768]{1,0:T(8,128)(2,1)} %param.26), kind=kOutput, calls=%fused_computation.65 | convolution fusion | flops 411041792 | bytes 9109504 | tf_op jit(solution)/shard_map/dot_general | solution.py:74
  234.8 13.5 %fusion.40.refs_17_ = f32[128,2048]{1,0:T(8,128)} fusion(f32[128,2048]{1,0:T(8,128)S(1)} %get-tuple-element.28.refs_16_, bf16[128,4096]{1,0:T(8,128)(2,1)} %get-tuple-element.57.refs_6_, bf16[1,2048,4096]{2,1,0:T(8,128)(2,1)} %param.24, f32[128,2048]{1,0:T(8,128)} %get-tuple-element.86, f32[128,4096]{1,0:T(8,128)S(1)} %copy-done.5), kind=kOutput, calls=%fused_computation.71 | convolution fusion | flops 2153775104 | bytes 22020096 | tf_op jit(solution)/shard_map/dot_general | solution.py:74
  248.3 129.5 %shard_map.265 = (f32[16,4096]{1,0:T(8,128)}, f32[16,768]{1,0:T(8,128)}, f32[6,2304]{1,0:T(8,128)}, f32[6,768]{1,0:T(8,128)}, f32[6,3072]{1,0:T(8,128)}, /*index...) custom-call(bf16[128,2048]{1,0:T(8,128)(2,1)} %copy-done, ...), custom_call_target="tpu_custom_call" | custom-call | tf_op jit(solution)/shard_map/pallas_call | solution.py:787
  (205 shorter events, 58.5 us)
Async XLA Ops:
  7.2 4.1 %copy-start.40 = (s32[112]{0:T(128)}, s32[112]{0:T(128)S(1)}, u32[]{:S(2)}) copy-start(s32[112]{0:T(128)S(1)} %and_select_fusion.2) | copy-start | bytes 1348
  11.6 59.9 %copy-start.1 = (bf16[128,2048]{1,0:T(8,128)(2,1)}, bf16[128,2048]{1,0:T(8,128)(2,1)S(1)}, u32[]{:S(2)}) copy-start(bf16[128,2048]{1,0:T(8,128)(2,1)S(1)} %copy.81.weight_ref.refs_14_) | copy-start | bytes 1572868
  71.5 9.3 %copy-start.2 = (bf16[50,128,128]{2,1,0:T(8,128)(2,1)}, bf16[50,128,128]{2,1,0:T(8,128)(2,1)S(1)}, u32[]{:S(2)}) copy-start(bf16[50,128,128]{2,1,0:T(8,128)(2,1)S(1)} %get-tuple-element.27.refs_13_) | copy-start | bytes 4915204
  71.5 156.0 %copy-start = (bf16[128,2048]{1,0:T(8,128)(2,1)}, bf16[128,2048]{1,0:T(8,128)(2,1)S(1)}, u32[]{:S(2)}) copy-start(bf16[128,2048]{1,0:T(8,128)(2,1)S(1)} %get-tuple-element.26.refs_0_) | copy-start | bytes 1572868
  71.5 163.2 %copy-start.3 = (f32[128,2048]{1,0:T(8,128)}, f32[128,2048]{1,0:T(8,128)S(1)}, u32[]{:S(2)}) copy-start(f32[128,2048]{1,0:T(8,128)S(1)} %get-tuple-element.28.refs_16_) | copy-start | bytes 3145732
  71.5 10.0 %copy-start.43 = (s32[128]{0:T(128)S(1)}, s32[128]{0:T(128)}, u32[]{:S(2)}) copy-start(s32[128]{0:T(128)} %param.19) | copy-start | bytes 1540
  83.6 14.3 %copy-start.33 = (bf16[3,768]{1,0:T(4,128)(2,1)S(1)}, bf16[3,768]{1,0:T(4,128)(2,1)}, u32[]{:S(2)}) copy-start(bf16[3,768]{1,0:T(4,128)(2,1)} %param.27) | copy-start | bytes 13828
  83.6 14.4 %copy-start.34 = (bf16[3,768]{1,0:T(4,128)(2,1)S(1)}, bf16[3,768]{1,0:T(4,128)(2,1)}, u32[]{:S(2)}) copy-start(bf16[3,768]{1,0:T(4,128)(2,1)} %param.28) | copy-start | bytes 13828
  86.8 21.7 %all-to-all-start = ((bf16[128,2,448]{2,1,0:T(2,128)(2,1)}), bf16[128,2,448]{2,1,0:T(2,128)(2,1)S(1)}, u32[]{:S(2)}, u32[]{:S(2)}) async-start(bf16[128,2,448]{2,1,0:T(2,128)(2,1)} %reshape.256), calls=%async_computation | async-start | bytes 524288 | tf_op jit(solution)/shard_map/all_to_all | solution.py:871
  97.9 38.3 %all-gather.2.cloned.1.call-start = ((), (), s32[]{:S(2)}) async-start(), calls=%async_computation.3 | async-start | bytes 1966080 | tf_op jit(solution)/shard_map/all_gather | solution.py:880
  110.0 38.9 %copy-start.11 = (bf16[128,768]{1,0:T(8,128)(2,1)}, bf16[128,768]{1,0:T(8,128)(2,1)S(1)}, u32[]{:S(2)}) copy-start(bf16[128,768]{1,0:T(8,128)(2,1)S(1)} %add_convert_fusion.3.refs_2_) | copy-start | bytes 589828
  113.5 89.3 %reduce-scatter.2.cloned.1.call-start = ((), (), s32[]{:S(2)}) async-start(), calls=%async_computation.4 | async-start | bytes 1966080 | tf_op jit(solution)/shard_map/reduce_scatter | solution.py:936
  124.4 18.6 %copy-start.19 = (bf16[128,768]{0,1:T(8,128)(2,1)}, bf16[128,768]{0,1:T(8,128)(2,1)S(1)}, u32[]{:S(2)}) copy-start(bf16[128,768]{0,1:T(8,128)(2,1)S(1)} %copy.84) | copy-start | bytes 589828
  140.3 5.5 %copy-start.12 = (bf16[512,768]{0,1:T(8,128)(2,1)}, bf16[512,768]{0,1:T(8,128)(2,1)S(1)}, u32[]{:S(2)}) copy-start(bf16[512,768]{0,1:T(8,128)(2,1)S(1)} %copy.85) | copy-start | bytes 2359300
  145.9 19.8 %copy-start.32 = (f32[12,128]{1,0:T(8,128)}, f32[12,128]{1,0:T(8,128)S(1)}, u32[]{:S(2)}) copy-start(f32[12,128]{1,0:T(8,128)S(1)} %get-tuple-element.74) | copy-start | bytes 18436
  148.9 5.0 %slice-start = ((s8[4718592]{0:T(1024)(128)(4,1)}), s8[4194304]{0:T(1024)(128)(4,1)S(1)}, s32[]{:S(2)}) async-start(s8[4718592]{0:T(1024)(128)(4,1)} %bitcast.115), calls=%async_computation.5 | async-start | bytes 8388608
  149.7 4.1 %copy-start.15 = (bf16[128,768]{1,0:T(8,128)(2,1)}, bf16[128,768]{1,0:T(8,128)(2,1)S(1)}, u32[]{:S(2)}) copy-start(bf16[128,768]{1,0:T(8,128)(2,1)S(1)} %add_convert_fusion.2.refs_4_) | copy-start | bytes 589828
  149.7 4.1 %slice-start.1 = ((s8[4718592]{0:T(1024)(128)(4,1)}), s8[524288]{0:T(1024)(128)(4,1)S(1)}, s32[]{:S(2)}) async-start(s8[4718592]{0:T(1024)(128)(4,1)} %bitcast.115), calls=%async_computation.6 | async-start | bytes 1048576
  180.2 22.6 %copy-start.31 = (f32[128]{0:T(128)S(1)}, f32[128]{0:T(128)}, u32[]{:S(2)}) copy-start(f32[128]{0:T(128)} %copy-done.30) | copy-start | bytes 1540
  202.8 3.7 copy-start.38
  206.4 10.8 %copy-start.17 = (bf16[128,1536]{1,0:T(8,128)(2,1)S(1)}, bf16[128,1536]{1,0:T(8,128)(2,1)}, u32[]{:S(2)}) copy-start(bf16[128,1536]{1,0:T(8,128)(2,1)} %reduce-scatter.2.cloned.1.call-done) | copy-start | bytes 1179652
  206.5 20.8 %copy-start.42 = (s32[128]{0:T(128)S(1)}, s32[128]{0:T(128)}, u32[]{:S(2)}) copy-start(s32[128]{0:T(128)} %copy-done.41) | copy-start | bytes 1540
  208.3 18.8 %all-to-all-start.1 = ((bf16[128,2,384]{2,1,0:T(2,128)(2,1)}), bf16[128,2,384]{2,1,0:T(2,128)(2,1)S(1)}, u32[]{:S(2)}, u32[]{:S(2)}) async-start(bf16[128,2,384]{2,1,0:T(2,128)(2,1)} %reshape.258), calls=%async_computation.2 | async-start | bytes 393216 | tf_op jit(solution)/shard_map/all_to_all | solution.py:942
  227.5 5.3 %copy-start.22 = (bf16[128,768]{1,0:T(8,128)(2,1)}, bf16[128,768]{1,0:T(8,128)(2,1)S(1)}, u32[]{:S(2)}) copy-start(bf16[128,768]{1,0:T(8,128)(2,1)S(1)} %convolution_convert_fusion.3.refs_7_) | copy-start | bytes 589828
  (28 other events, 58.0 us)
Sparse Core Ops, SparseCore 0:
  113.6 22.5 all-gather.1
  177.0 25.7 reduce-scatter.1

commit v2 on v1

--- a/solution.py
+++ b/solution.py
@@ -80,10 +80,11 @@
     return lax.dot_general(left, right, (((0,), (0,)), ((), ())), preferred_element_type=F32)
 
 
-POOL_COLS = 256
-
-
-def pool_kernel(ids_ref, table_ref, weight_ref, act_ref, pooled_ref, unfolded_ref, values, rows):
+POOL_COLS = 512
+POOL_STEP = 10
+
+
+def pool_kernel(ids_ref, table_ref, weight_ref, act_ref, pooled_ref, unfolded_ref, values):
     @pl.when(pl.program_id(0) == 0)
     def _():
         lane = lax.broadcasted_iota(jnp.int32, (WORDS, 128), 1)
@@ -99,7 +100,7 @@
             values[place] = jnp.where(lane == ABSENT_ROW, absent, found)
             return pltpu.roll(ids, 127, 1)
 
-        lax.fori_loop(0, WORD_CHARS, look_up, ids_ref[...])
+        lax.fori_loop(0, WORD_CHARS, look_up, ids_ref[...], unroll=5)
 
         @pl.loop(0, WORD_CHARS)
         def _(place):
@@ -110,21 +111,20 @@
 
     weight = weight_ref[...]
 
-    def convolve(pair, top):
-        left = unfolded_ref[pl.ds(2 * pair, 2)].reshape(2 * WORDS, 128)
-        block = dot(left, weight).reshape(2, WORDS, POOL_COLS)
-        rows[pl.ds(2 * pair, 2)] = block
-        return jnp.maximum(top, jnp.maximum(block[0], block[1]))
-
-    top = lax.fori_loop(
-        0, WORD_CHARS // 2, convolve, jnp.full((WORDS, POOL_COLS), -3e38, F32)
-    )
-
-    def gather(pair, total):
-        block = rows[pl.ds(2 * pair, 2)]
-        return total + (jnp.exp(block[0] - top) + jnp.exp(block[1] - top))
-
-    total = lax.fori_loop(0, WORD_CHARS // 2, gather, jnp.zeros((WORDS, POOL_COLS), F32))
+    def convolve(step, state):
+        top, total = state
+        left = unfolded_ref[pl.ds(POOL_STEP * step, POOL_STEP)].reshape(POOL_STEP * WORDS, 128)
+        block = dot(left, weight).reshape(POOL_STEP, WORDS, POOL_COLS)
+        higher = jnp.maximum(top, jnp.max(block, axis=0))
+        total = total * jnp.exp(top - higher) + jnp.sum(jnp.exp(block - higher[None]), axis=0)
+        return higher, total
+
+    top, total = lax.fori_loop(
+        0,
+        WORD_CHARS // POOL_STEP,
+        convolve,
+        (jnp.full((WORDS, POOL_COLS), -3e38, F32), jnp.zeros((WORDS, POOL_COLS), F32)),
+    )
     pooled = top + jnp.log(total)
     pooled_ref[...] = pooled
     act_ref[...] = jax.nn.gelu(pooled).astype(BF16)
@@ -151,7 +151,6 @@
         ),
         scratch_shapes=[
             pltpu.VMEM((WORD_CHARS + TAPS - 1, WORDS, 128), F32),
-            pltpu.VMEM((WORD_CHARS, WORDS, POOL_COLS), F32),
         ],
         compiler_params=pltpu.CompilerParams(
             dimension_semantics=("arbitrary",), vmem_limit_bytes=40 << 20
@@ -405,6 +404,10 @@
 PICK_LANES = {16: 512, 6: 384, 24: 768}
 
 
+CONV_STEP = 10
+CONV_COLS = 512
+
+
 def sums_kernel(schedule, *refs):
     rest = list(refs)
 
@@ -428,7 +431,7 @@
     pair_left_sems, pair_right_sems, conv_sems = (
         (sems.at[0], sems.at[1]) for sems in (pair_left_sems, pair_right_sems, conv_sems)
     )
-    unfolded_grad, table_grad = take(2)
+    last_grad, table_grad = take(2)
 
     where = place_of()
     y, z, core, x = where
@@ -538,7 +541,7 @@
                     base, first = RIGHT_AT[name], GROUP_AT[name, 0]
                     lanes = pl.ds(offset + start, cols)
 
-                    @pl.loop(0, 4)
+                    @pl.loop(0, 4, unroll=4)
                     def _(row):
                         halves = []
                         for group, column in ((upper, upper_at), (lower, lower_at)):
@@ -581,36 +584,38 @@
     lane = lax.broadcasted_iota(jnp.int32, (WORDS, 128), 1)
 
     def conv_start():
-        unfolded_grad[0 : TAPS - 1] = jnp.zeros((TAPS - 1, WORDS, 128), F32)
+        last_grad[...] = jnp.zeros_like(last_grad)
         conv_grad[...] = jnp.zeros_like(conv_grad)
         table_grad[...] = jnp.zeros_like(table_grad)
 
-    def conv_pair(pair):
-        two = unfolded[pl.ds(2 * pair, 2)].reshape(2 * WORDS, 128)
+    def conv_block(step):
+        first = CONV_STEP * step
+        some = unfolded[pl.ds(first, CONV_STEP)].reshape(CONV_STEP * WORDS, 128)
         unit = jnp.where(
             lax.broadcasted_iota(jnp.int32, (128, 128), 0)
             == lax.broadcasted_iota(jnp.int32, (128, 128), 1),
             1.0,
             0.0,
         ).astype(BF16)
-        turned = back_dot(unit, two).astype(BF16)
-        back = jnp.zeros((2 * WORDS, 128), F32)
-        for block in range(4):
-            cols = slice(block * 512, (block + 1) * 512)
-            conv = dot(two, conv_w[:, cols]).reshape(2, WORDS, 512)
+        turned = back_dot(unit, some).astype(BF16)
+        back = jnp.zeros((CONV_STEP * WORDS, 128), F32)
+        for block in range(FILTERS // CONV_COLS):
+            cols = slice(block * CONV_COLS, (block + 1) * CONV_COLS)
+            conv = dot(some, conv_w[:, cols]).reshape(CONV_STEP, WORDS, CONV_COLS)
             shares = jnp.exp(conv - pooled[:, cols][None]) * grad_pooled[:, cols][None]
-            shares = shares.astype(BF16).reshape(2 * WORDS, 512)
+            shares = shares.astype(BF16).reshape(CONV_STEP * WORDS, CONV_COLS)
             conv_grad[:, cols] += dot(turned, shares)
             back = back + dot(shares, conv_back[cols, :])
-        unfolded_grad[pl.ds(2 * pair + TAPS - 1, 2)] = back.reshape(2, WORDS, 128)
+        back = back.reshape(CONV_STEP, WORDS, 128)
+        before = last_grad[...]
+        last_grad[...] = back[CONV_STEP - TAPS + 1 :]
         high_low, onehots = [], []
-        for side in (0, 1):
-            place = 2 * pair + side
-            taps = unfolded_grad[place + TAPS - 1]
+        for side in range(CONV_STEP):
+            place = first + side
+            taps = back[side]
             for tap in range(1, TAPS):
-                taps = jnp.where(
-                    lane // CHAR_DIM == tap, unfolded_grad[place + TAPS - 1 - tap], taps
-                )
+                from_tap = back[side - tap] if side >= tap else before[TAPS - 1 + side - tap]
+                taps = jnp.where(lane // CHAR_DIM == tap, from_tap, taps)
             taps = jnp.where(lane < BIAS_ROW, taps, 0.0)
             high = taps.astype(BF16)
             low = (taps - high.astype(F32)).astype(BF16)
@@ -669,7 +674,7 @@
         "finish": finish,
         "conv_start": conv_start,
         "conv": lambda first, last: lax.fori_loop(
-            first, last, lambda pair, nothing: (conv_pair(pair), nothing)[1], 0
+            first, last, lambda step, nothing: (conv_block(step), nothing)[1], 0
         ),
         "conv_end": conv_end,
         "conv_ring": conv_ring,
@@ -691,59 +696,54 @@
 
 SCHEDULE = (
     ("prepare", 0),
+    ("multiply", 0),
     ("prepare", 1),
-    ("multiply", 0),
+    ("multiply", 1),
     ("prepare", 2),
+    ("multiply", 2),
+    ("multiply", 3),
     ("small",),
-    ("multiply", 1),
+    ("conv_start",),
+    ("conv", 0, 5),
+    ("conv_end",),
+    ("shared", 0, 0),
     ("relay1", 0),
-    ("shared", 0, 0),
-    ("multiply", 2),
+    ("conv_ring",),
     ("relay1", 1),
-    ("multiply", 3),
-    ("conv_start",),
-    ("conv", 0, 3),
-    ("end1", 0),
     ("shared", 0, 1),
-    ("conv", 3, 6),
-    ("relay1", 2),
-    ("relay1", 3),
-    ("end1", 1),
-    ("relay2", 0),
-    ("shared", 0, 2),
-    ("conv", 6, 11),
-    ("end2", 0),
-    ("relay2", 1),
-    ("shared", 0, 3),
-    ("conv", 11, 16),
-    ("end1", 2),
-    ("finish", 0),
-    ("end2", 1),
-    ("conv", 16, 20),
-    ("end1", 3),
-    ("relay2", 2),
-    ("finish", 1),
-    ("conv", 20, 25),
-    ("conv_end",),
-    ("relay2", 3),
-    ("end2", 2),
-    ("conv_ring",),
     ("shared", 1, 0),
     ("shared", 2, 0),
-    ("end2", 3),
+    ("relay1", 2),
     ("relay1", 4),
-    ("finish", 2),
+    ("relay1", 3),
+    ("end1", 0),
+    ("shared", 0, 2),
     ("shared", 1, 1),
     ("shared", 2, 1),
     ("end1", 4),
-    ("finish", 3),
-    ("relay2", 4),
+    ("end1", 1),
+    ("relay2", 0),
+    ("end1", 2),
+    ("shared", 0, 3),
     ("shared", 1, 2),
     ("shared", 2, 2),
-    ("end2", 4),
+    ("relay2", 4),
+    ("relay2", 1),
+    ("end2", 0),
+    ("end1", 3),
+    ("relay2", 2),
     ("shared", 1, 3),
     ("shared", 2, 3),
+    ("end2", 4),
+    ("end2", 1),
+    ("finish", 0),
+    ("relay2", 3),
+    ("end2", 2),
+    ("finish", 1),
     ("finish", 4),
+    ("end2", 3),
+    ("finish", 2),
+    ("finish", 3),
 )
 
 
@@ -777,7 +777,7 @@
             pltpu.VMEM((16, 2, 64, 128), F32),
             pltpu.VMEM((16, 64, 128), F32),
             pltpu.SemaphoreType.DMA((2, 1)),
-            pltpu.VMEM((WORD_CHARS + TAPS - 1, WORDS, 128), F32),
+            pltpu.VMEM((TAPS - 1, WORDS, 128), F32),
             pltpu.VMEM((384, 256), F32),
         ]
     )
@@ -807,6 +807,311 @@
     return dict(zip(NAMES, results)), results[6:]
 
 
+PAIRS = HEADS // 2
+SENT = 1024
+GELU_SCALE = 0.7978845608028654
+GELU_CUBE = 0.044715
+FF_COLS = 512
+
+
+def gelu_both(value):
+    square = value * value
+    bend = jnp.tanh(GELU_SCALE * value * (1.0 + GELU_CUBE * square))
+    half = 0.5 * (1.0 + bend)
+    slope = half + 0.5 * GELU_SCALE * value * (1.0 - bend * bend) * (
+        1.0 + 3.0 * GELU_CUBE * square
+    )
+    return value * half, slope
+
+
+def encoder_kernel(*refs):
+    rest = list(refs)
+
+    def take(count):
+        taken = rest[:count]
+        del rest[:count]
+        return taken
+
+    rows_in, slot_in, order_in, valid_in, gains, shifts, cotangent = take(7)
+    weights_in = take(4)
+    out_hidden, out_first, out_context, out_middle, out_hidden_act = take(5)
+    out_joint, out_attn, out_up, out_down, out_rows, out_norms = take(6)
+    weights = take(4)
+    load_sems, go_sems, back_sems, keys_sems, sums_sems = take(5)
+    go_near, near, go_far, far = take(4)
+    back_far, home_far, back_near, home_near = take(4)
+    joint, both, probs, probs_low, slopes = take(5)
+    grads, relay, last = take(3)
+    go_near_sems, go_far_sems = (go_sems.at[0], go_sems.at[1]), (go_sems.at[2], go_sems.at[3])
+    back_near_sems, back_far_sems = (
+        (back_sems.at[0], back_sems.at[1]),
+        (back_sems.at[2], back_sems.at[3]),
+    )
+    keys_sems = (keys_sems.at[0], keys_sems.at[1])
+    sums_sems = (sums_sems.at[0], sums_sems.at[1])
+
+    y, z, core, x = place_of()
+    loads = []
+    for at in range(4):
+        loads.append(pltpu.make_async_copy(weights_in[at], weights[at], load_sems.at[at]))
+        loads[at].start()
+    qkv_w, out_w, up_w, down_w = weights
+
+    near_peers, far_peers = [], []
+    for number in range(1, 8):
+        their_core, their_x = lax.rem(core + number // 4, 2), around(x, number % 4)
+        near_peers.append((number, their_core * 4 + their_x, device_of(y, z, their_core, their_x)))
+    for number in range(1, 16):
+        their_y, their_z = around(y, number // 4), around(z, number % 4)
+        far_peers.append((number, their_y * 4 + their_z, device_of(their_y, their_z, core, x)))
+    near_me, far_me = core * 4 + x, y * 4 + z
+    right = device_of(y, z, core, around(x, 1))
+    left = device_of(y, z, core, around(x, 3))
+
+    barrier = pltpu.get_barrier_semaphore()
+    for _, _, device in near_peers + far_peers:
+        pl.semaphore_signal(barrier, inc=1, device_id=device, device_id_type=MESH)
+
+    lane = lax.broadcasted_iota(jnp.int32, (WORDS, WORDS), 1)
+    row = lax.broadcasted_iota(jnp.int32, (WORDS, WORDS), 0)
+    one_hot = lambda hit: jnp.where(hit, 1.0, 0.0).astype(BF16)
+    send_pick = one_hot(order_in[...] == row)
+    turn_pick = one_hot(lane == lax.rem(row, 8) * 16 + row // 8)
+
+    def exchange(peers, mine, sems, source, target):
+        copies = []
+        for number, index, device in peers:
+            copy = remote(source.at[index], target.at[mine], sems, number, device)
+            copy.start()
+            copies.append(copy)
+        target[mine] = source[mine]
+        for copy in copies:
+            copy.wait_recv()
+        return copies
+
+    carried = dot(send_pick, rows_in[...]).astype(BF16)
+    slots = dot(send_pick, slot_in[...]).astype(BF16)
+    go_near[:, :, 0:D] = carried.reshape(8, 16, D)
+    go_near[:, :, D : D + 128] = slots.reshape(8, 16, 128)
+    go_near[:, :, D + 128 :] = jnp.zeros((8, 16, SENT - D - 128), BF16)
+    pl.semaphore_wait(barrier, len(near_peers) + len(far_peers))
+    sent = exchange(near_peers, near_me, go_near_sems, go_near, near)
+    turned = dot(turn_pick, near[...].reshape(WORDS, SENT)).reshape(16, 8, SENT)
+    halves = [turned[:, :, : SENT // 2], turned[:, :, SENT // 2 :]]
+    go_far[...] = jnp.concatenate(halves, axis=1).astype(BF16)
+    sent += exchange(far_peers, far_me, go_far_sems, go_far, far)
+    arrived = far[...].astype(F32)
+    arrived = jnp.concatenate([arrived[:, :8], arrived[:, 8:]], axis=2).reshape(WORDS, SENT)
+    place_pick = one_hot(arrived[:, D : D + 128] == lane.astype(F32))
+    word_rows = first_dot(place_pick, arrived[:, :D].astype(BF16))
+
+    gain = [gains[at : at + 1, :] for at in range(3)]
+    shift = [shifts[at : at + 1, :] for at in range(3)]
+    first_f, first_normal, first_inv = norm_parts(word_rows, gain[0], shift[0])
+    first_norm = first_f.astype(BF16)
+    out_first[...] = first_norm
+    loads[0].wait()
+    for start in (D, 2 * D, 0):
+        cols = slice(start, start + D)
+        joint[:, cols] = dot(first_norm, qkv_w[:, cols]).astype(BF16)
+        if start:
+            half = pl.ds(start - D, D)
+            both[x, :, start - D : start] = joint[:, cols]
+            for side, device in ((0, right), (1, left)):
+                copy = remote(
+                    both.at[x, :, half], both.at[x, :, half], keys_sems, start // D * 2 + side, device
+                )
+                copy.start()
+                sent.append(copy)
+    key_right, key_left, value_right, value_left = sent[-4:]
+    key_right.wait_recv()
+    behind, ahead = around(x, 3), around(x, 1)
+    pass_key = remote(
+        both.at[behind, :, pl.ds(0, D)], both.at[behind, :, pl.ds(0, D)], keys_sems, 0, right
+    )
+    pass_key.start()
+    value_left.wait_recv()
+    pass_value = remote(
+        both.at[ahead, :, pl.ds(D, D)], both.at[ahead, :, pl.ds(D, D)], keys_sems, 1, left
+    )
+    pass_value.start()
+    sent += [pass_key, pass_value]
+    for copy in (key_left, value_right, pass_key, pass_value):
+        copy.wait_recv()
+
+    scale = HEAD_DIM ** (-0.5)
+    low_lanes = one_hot(lane < HEAD_DIM)
+    high_lanes = one_hot(lane >= HEAD_DIM)
+    valid = valid_in[...] > 0
+
+    def stacked(rows):
+        return jnp.concatenate([rows * low_lanes, rows * high_lanes], axis=0)
+
+    def unstacked(rows):
+        return jnp.where(lane < HEAD_DIM, rows[:WORDS], rows[WORDS:])
+
+    for pair in range(PAIRS):
+        cols = slice(pair * 128, pair * 128 + 128)
+        keys = both[:, :, cols].reshape(SEQ_LEN, 128)
+        values = both[:, :, D + pair * 128 : D + pair * 128 + 128].reshape(SEQ_LEN, 128)
+        scores = back_dot(stacked(joint[:, cols]), keys) * scale
+        masked = jnp.where(valid, scores, NEG_LARGE)
+        top = jnp.max(masked, -1, keepdims=True)
+        expo = jnp.where(valid, jnp.exp(masked - top), 0.0)
+        share = expo / jnp.sum(expo, -1, keepdims=True)
+        probs[pair] = share
+        share = share.astype(BF16)
+        probs_low[pair] = share
+        out_context[:, cols] = unstacked(dot(share, values)).astype(BF16)
+    loads[1].wait()
+    attn_out = dot(out_context[...], out_w[...])
+    mid_f, mid_normal, mid_inv = norm_parts(first_norm.astype(F32) + attn_out, gain[1], shift[1])
+    middle = mid_f.astype(BF16)
+    out_middle[...] = middle
+    loads[2].wait()
+    loads[3].wait()
+
+    down_proj = jnp.zeros((WORDS, D), F32)
+    for block in range(FF // FF_COLS):
+        cols = slice(block * FF_COLS, (block + 1) * FF_COLS)
+        act, slope = gelu_both(dot(middle, up_w[:, cols]))
+        act = act.astype(BF16)
+        slopes[:, cols] = slope
+        out_hidden_act[:, cols] = act
+        down_proj = down_proj + dot(act, down_w[cols, :])
+    out_f, out_normal, out_inv = norm_parts(middle.astype(F32) + down_proj, gain[2], shift[2])
+    out_hidden[...] = out_f.astype(BF16)
+
+    def note(which, gain_row, shift_row):
+        out_norms[which : which + 1, :] = gain_row[None]
+        out_norms[3 + which : 4 + which, :] = shift_row[None]
+
+    grad_pre2, gain_row, shift_row = norm_back(
+        cotangent[...].astype(F32), out_normal, out_inv, gain[2]
+    )
+    note(2, gain_row, shift_row)
+    grad_down = grad_pre2.astype(BF16)
+    out_down[...] = grad_down
+    grad_mid = grad_pre2
+    for block in range(FF // FF_COLS):
+        cols = slice(block * FF_COLS, (block + 1) * FF_COLS)
+        grad_up = (slopes[:, cols] * back_dot(grad_down, down_w[cols, :])).astype(BF16)
+        out_up[:, cols] = grad_up
+        grad_mid = grad_mid + back_dot(grad_up, up_w[:, cols])
+    grad_pre1, gain_row, shift_row = norm_back(grad_mid, mid_normal, mid_inv, gain[1])
+    note(1, gain_row, shift_row)
+    grad_attn = grad_pre1.astype(BF16)
+    out_attn[...] = grad_attn
+    grad_context = back_dot(grad_attn, out_w[...]).astype(BF16)
+
+    for pair in range(PAIRS):
+        cols = slice(pair * 128, pair * 128 + 128)
+        value_cols = slice(D + pair * 128, D + pair * 128 + 128)
+        keys = both[:, :, cols].reshape(SEQ_LEN, 128)
+        values = both[:, :, value_cols].reshape(SEQ_LEN, 128)
+        grad_rows = stacked(grad_context[:, cols])
+        share = probs[pair]
+        grad_probs = back_dot(grad_rows, values)
+        delta = jnp.sum(share * grad_probs, -1, keepdims=True)
+        grad_scores = (share * (grad_probs - delta)).astype(BF16)
+        grad_query = unstacked(dot(grad_scores, keys)) * scale
+        out_joint[:, cols] = grad_query.astype(BF16)
+        grad_keys = first_dot(grad_scores, stacked(joint[:, cols])) * scale
+        grads[:, :, cols] = grad_keys.astype(BF16).reshape(4, WORDS, 128)
+        grad_values = first_dot(probs_low[pair], grad_rows)
+        grads[:, :, value_cols] = grad_values.astype(BF16).reshape(4, WORDS, 128)
+
+    key_half, value_half = pl.ds(0, D), pl.ds(D, D)
+    opposite = around(x, 2)
+    steps = [
+        remote(grads.at[opposite, :, key_half], relay.at[0], sums_sems, 0, right),
+        remote(grads.at[opposite, :, value_half], relay.at[1], sums_sems, 1, left),
+        remote(grads.at[ahead, :, value_half], last.at[0, :, value_half], sums_sems, 2, right),
+        remote(grads.at[behind, :, key_half], last.at[1, :, key_half], sums_sems, 3, left),
+    ]
+    for copy in steps:
+        copy.start()
+    steps[0].wait_recv()
+    grads[ahead, :, 0:D] = (grads[ahead, :, 0:D].astype(F32) + relay[0].astype(F32)).astype(BF16)
+    steps.append(
+        remote(grads.at[ahead, :, key_half], last.at[0, :, key_half], sums_sems, 4, right)
+    )
+    steps[4].start()
+    steps[1].wait_recv()
+    grads[behind, :, D:] = (grads[behind, :, D:].astype(F32) + relay[1].astype(F32)).astype(BF16)
+    steps.append(
+        remote(grads.at[behind, :, value_half], last.at[1, :, value_half], sums_sems, 5, left)
+    )
+    steps[5].start()
+    sent += steps
+    for copy in steps[2:]:
+        copy.wait_recv()
+    total = grads[x].astype(F32) + last[0].astype(F32) + last[1].astype(F32)
+    out_joint[:, D:] = total.astype(BF16)
+
+    grad_first = grad_pre1
+    for start in range(0, 3 * D, D):
+        cols = slice(start, start + D)
+        grad_first = grad_first + back_dot(out_joint[:, cols], qkv_w[:, cols])
+    grad_words, gain_row, shift_row = norm_back(grad_first, first_normal, first_inv, gain[0])
+    note(0, gain_row, shift_row)
+
+    turned = dot(place_pick, grad_words.astype(BF16)).reshape(16, 8, D)
+    halves = [turned[:, :, : D // 2], turned[:, :, D // 2 :]]
+    back_far[...] = jnp.concatenate(halves, axis=1).astype(BF16)
+    sent += exchange(far_peers, far_me, back_far_sems, back_far, home_far)
+    arrived = home_far[...].astype(F32)
+    arrived = jnp.concatenate([arrived[:, :8], arrived[:, 8:]], axis=2).reshape(WORDS, D)
+    arrived = first_dot(turn_pick, arrived.astype(BF16)).astype(BF16)
+    back_near[...] = arrived.reshape(8, 16, D)
+    sent += exchange(near_peers, near_me, back_near_sems, back_near, home_near)
+    out_rows[...] = first_dot(send_pick, home_near[...].reshape(WORDS, D)).astype(BF16)
+    for copy in sent:
+        copy.wait_send()
+
+
+def encode(rows, slots, order, valid, gains, shifts, cotangent, weights):
+    whole = pl.BlockSpec(memory_space=pltpu.VMEM)
+    shapes = [(WORDS, D)] * 4 + [(WORDS, FF), (WORDS, 3 * D), (WORDS, D), (WORDS, FF)]
+    shapes += [(WORDS, D)] * 2
+    out_shapes = [jax.ShapeDtypeStruct(shape, BF16) for shape in shapes]
+    out_shapes.append(jax.ShapeDtypeStruct((6, D), F32))
+    dma = pltpu.SemaphoreType.DMA
+    return pl.pallas_call(
+        encoder_kernel,
+        out_shape=tuple(out_shapes),
+        in_specs=[whole] * 7 + [pl.BlockSpec(memory_space=pl.ANY)] * 4,
+        out_specs=tuple(whole for _ in out_shapes),
+        scratch_shapes=[
+            *(pltpu.VMEM(weight.shape, BF16) for weight in weights),
+            dma((4,)),
+            dma((4, 16)),
+            dma((4, 16)),
+            dma((2, 6)),
+            dma((2, 6)),
+            pltpu.VMEM((8, 16, SENT), BF16),
+            pltpu.VMEM((8, 16, SENT), BF16),
+            pltpu.VMEM((16, 16, SENT // 2), BF16),
+            pltpu.VMEM((16, 16, SENT // 2), BF16),
+            pltpu.VMEM((16, 16, D // 2), BF16),
+            pltpu.VMEM((16, 16, D // 2), BF16),
+            pltpu.VMEM((8, 16, D), BF16),
+            pltpu.VMEM((8, 16, D), BF16),
+            pltpu.VMEM((WORDS, 3 * D), BF16),
+            pltpu.VMEM((4, WORDS, 2 * D), BF16),
+            pltpu.VMEM((PAIRS, 2 * WORDS, SEQ_LEN), F32),
+            pltpu.VMEM((PAIRS, 2 * WORDS, SEQ_LEN), BF16),
+            pltpu.VMEM((WORDS, FF), F32),
+            pltpu.VMEM((4, WORDS, 2 * D), BF16),
+            pltpu.VMEM((2, WORDS, D), BF16),
+            pltpu.VMEM((2, WORDS, 2 * D), BF16),
+        ],
+        compiler_params=pltpu.CompilerParams(
+            collective_id=2, has_side_effects=True, vmem_limit_bytes=60 << 20
+        ),
+    )(rows, slots, order, valid, gains, shifts, cotangent, *weights)
+
+
 def body(
     char_ids,
     word_lengths,
@@ -829,7 +1134,6 @@
     group_len = cotangent.shape[1]
     ctx_size = lax.axis_size("ctx")
     full_len = group_len * ctx_size
-    head_scale = HEAD_DIM ** (-0.5)
     conv_masked = jnp.where(tap_mask(), conv_weight, jnp.zeros_like(conv_weight))
     high_shift = highway_bias.astype(F32)
     gain_rows = norm_gain.astype(F32)
@@ -860,87 +1164,34 @@
 
     seq_index = word_home // SEQ_LEN
     pos_index = word_home % SEQ_LEN
-    target = seq_index * ctx_size + pos_index // group_len
     slot = pos_index % group_len
-    numbers = jnp.arange(WORDS)
-    send_pick = (target[None, :] == numbers[:, None]).astype(BF16)
-    carried = jnp.concatenate(
-        [embedded, jnp.broadcast_to(slot[:, None], (WORDS, 128)).astype(BF16)], axis=1
-    )
-    to_send = dot(send_pick, carried).astype(BF16)
-    arrived = lax.all_to_all(to_send, ("dp", "ctx"), split_axis=0, concat_axis=0, tiled=True)
-    arrived_slot = arrived[:, D].astype(jnp.int32)
-    place_pick = (arrived_slot[None, :] == numbers[:, None]).astype(BF16)
-    word_rows = dot(place_pick, arrived[:, :D])
-
-    first_f, first_normal, first_inv = norm_parts(word_rows, gain_rows[0], shift_rows[0])
-    first_norm = first_f.astype(BF16)
-    joint_proj = dot(first_norm, qkv_weight).astype(BF16)
-    queries = joint_proj[:, :D].reshape(group_len, HEADS, HEAD_DIM)
-    both_all = lax.all_gather(joint_proj[:, D:], "ctx", axis=0, tiled=True)
-    key_heads = both_all[:, :D].reshape(full_len, HEADS, HEAD_DIM)
-    value_heads = both_all[:, D:].reshape(full_len, HEADS, HEAD_DIM)
-    key_valid = jnp.arange(full_len) < seq_lengths[0]
-    valid_wide = key_valid[None, None, :]
-    scores = (
-        jnp.einsum("qhd,khd->hqk", queries, key_heads, preferred_element_type=F32) * head_scale
-    )
-    masked = jnp.where(valid_wide, scores, NEG_LARGE)
-    top_val = jnp.max(masked, -1, keepdims=True)
-    expo_val = jnp.where(valid_wide, jnp.exp(masked - top_val), 0.0)
-    totals = jnp.sum(expo_val, -1, keepdims=True)
-    probs = expo_val / totals
-    probs_low = probs.astype(BF16)
-    context = (
-        jnp.einsum("hqk,khd->qhd", probs_low, value_heads, preferred_element_type=F32)
-        .reshape(WORDS, D)
-        .astype(BF16)
-    )
-    attn_out = dot(context, out_weight)
-    mid_f, mid_normal, mid_inv = norm_parts(
-        first_norm.astype(F32) + attn_out, gain_rows[1], shift_rows[1]
-    )
-    middle = mid_f.astype(BF16)
-    up_proj = dot(middle, up_weight)
-    hidden_act = jax.nn.gelu(up_proj).astype(BF16)
-    down_proj = dot(hidden_act, down_weight)
-    out_f, out_normal, out_inv = norm_parts(
-        middle.astype(F32) + down_proj, gain_rows[2], shift_rows[2]
-    )
-    out_hidden = out_f.astype(BF16).reshape(1, group_len, D)
-
-    grad_rows = cotangent.reshape(WORDS, D).astype(F32)
-    grad_pre2, gain_two, shift_two = norm_back(grad_rows, out_normal, out_inv, gain_rows[2])
-    grad_down = grad_pre2.astype(BF16)
-    _, gelu_pull = jax.vjp(jax.nn.gelu, up_proj)
-    grad_up = gelu_pull(back_dot(grad_down, down_weight))[0].astype(BF16)
-    grad_mid = grad_pre2 + back_dot(grad_up, up_weight)
-    grad_pre1, gain_one, shift_one = norm_back(grad_mid, mid_normal, mid_inv, gain_rows[1])
-    grad_attn = grad_pre1.astype(BF16)
-    grad_context = (
-        back_dot(grad_attn, out_weight).astype(BF16).reshape(group_len, HEADS, HEAD_DIM)
-    )
-    grad_probs = jnp.einsum("qhd,khd->hqk", grad_context, value_heads, preferred_element_type=F32)
-    delta_rows = jnp.sum(probs * grad_probs, -1, keepdims=True)
-    grad_scores = (probs * (grad_probs - delta_rows)).astype(BF16)
-    grad_query = (
-        jnp.einsum("hqk,khd->qhd", grad_scores, key_heads, preferred_element_type=F32) * head_scale
-    )
-    grad_keys = (
-        jnp.einsum("hqk,qhd->khd", grad_scores, queries, preferred_element_type=F32) * head_scale
-    )
-    grad_values = jnp.einsum("hqk,qhd->khd", probs_low, grad_context, preferred_element_type=F32)
-    grad_both = jnp.concatenate(
-        [grad_keys.reshape(full_len, D), grad_values.reshape(full_len, D)], axis=1
-    ).astype(BF16)
-    both_sum = lax.psum_scatter(grad_both, "ctx", scatter_dimension=0, tiled=True)
-    grad_joint = jnp.concatenate([grad_query.reshape(WORDS, D).astype(BF16), both_sum], axis=-1)
-    grad_first = back_dot(grad_joint, qkv_weight) + grad_pre1
-    grad_words, gain_zero, shift_zero = norm_back(grad_first, first_normal, first_inv, gain_rows[0])
-
-    send_back = first_dot(place_pick, grad_words.astype(BF16)).astype(BF16)
-    returned = lax.all_to_all(send_back, ("dp", "ctx"), split_axis=0, concat_axis=0, tiled=True)
-    grad_embedded = first_dot(send_pick, returned).astype(BF16)
+    near = seq_index % 2 * ctx_size + pos_index // group_len
+    order = near * 16 + seq_index // 2
+    slots = jnp.broadcast_to(slot[:, None], (WORDS, 128)).astype(BF16)
+    valid = (jnp.arange(full_len) < seq_lengths[0]).astype(jnp.int32)
+    (
+        out_hidden,
+        first_norm,
+        context,
+        middle,
+        hidden_act,
+        grad_joint,
+        grad_attn,
+        grad_up,
+        grad_down,
+        grad_embedded,
+        norm_grads,
+    ) = encode(
+        embedded,
+        slots,
+        order[None, :],
+        valid[None, :],
+        gain_rows,
+        shift_rows,
+        cotangent.reshape(WORDS, D),
+        (qkv_weight, out_weight, up_weight, down_weight),
+    )
+    out_hidden = out_hidden.reshape(1, group_len, D)
     grad_act = back_dot(grad_embedded, proj_weight)
     _, mix_pull = jax.vjp(gate_mix, act.astype(F32), mixed_rows)
     grad_direct, grad_mixed = mix_pull(grad_act)
@@ -950,9 +1201,7 @@
     _, pool_pull = jax.vjp(jax.nn.gelu, pooled)
     grad_pooled = pool_pull(grad_act)[0]
 
-    small = jnp.concatenate(
-        [high_bias, gain_zero, gain_one, gain_two, shift_zero, shift_one, shift_two]
-    ).reshape(-1, 128)
+    small = jnp.concatenate([high_bias, norm_grads.reshape(-1)]).reshape(-1, 128)
     small = jnp.pad(small, ((0, SMALL_ROWS - small.shape[0]), (0, 0)))
     sums, (conv_sum, small_sum, table_sum, bias_sum) = sum_gradients(
         {

time: 409 us -> 271 us (0.66)
  waiting for transfers between devices: 45.9 us -> 0 us
  matrix products: 60 us -> 28.6 us
  starting transfers between devices: 30.1 us -> 0 us
  local copies, waits for them, and re-layouts: 42.2 us -> 24.5 us
  Pallas kernels: 189 us -> 205 us
  between operations: 15.8 us -> 1.82 us
  other arithmetic: 18.3 us -> 7.2 us
    pallas_call x0 -> x1, Pallas kernels: none -> 78.4 us  [encode(): pl.pallas_call(encoder_kernel, out_shape=tuple(out_shapes), in_specs=[who...]
    pallas_call x1, Pallas kernels: 59.5 us -> 26.5 us  [pool_words(): pl.pallas_call(pool_kernel, grid=(FILTERS // POOL_COLS,), out_shape=(jax....]
    pallas_call x1, Pallas kernels: 130 us -> 99.9 us  [sum_gradients(): pl.pallas_call(functools.partial(sums_kernel, SCHEDULE), out_shape=tuple(...]
    all_to_all x2 -> x0, starting transfers between devices: 20 us -> none  [the longest x1 11.1 us: body(): lax.all_to_all(to_send, ('dp', 'ctx'), split_axis=0, concat_axis=0, tiled...]
    all_to_all x2 -> x0, waiting for transfers between devices: 19.4 us -> none  [the longest x1 10.4 us: body(): lax.all_to_all(to_send, ('dp', 'ctx'), split_axis=0, concat_axis=0, tiled...]
    reduce_scatter x1 -> x0, waiting for transfers between devices: 14.6 us -> none  [body(): lax.psum_scatter(grad_both, 'ctx', scatter_dimension=0, tiled=True)]
    all_gather x1 -> x0, waiting for transfers between devices: 11.9 us -> none  [body(): both_all = lax.all_gather(joint_proj[:, D:], 'ctx', axis=0, tiled=True)]
    dot_general x7 -> x0, matrix products: 11.5 us -> none  [the longest x1 2.96 us: body(): jnp.einsum('hqk,khd->qhd', probs_low, value_heads, preferred_element_type...]
  transfers between devices with their start and end apart: 4 -> 0, of which waited for: 4 -> 0; matrix products, arithmetic and copies ran while one was open for 3% -> 0% of each run, Pallas kernels for 0% -> 0%
where the time goes in v2:
time: 271 us; the launch traced here: 267 us
  Pallas kernels  205 us (76%)
  matrix products  28.6 us (11%)
  local copies, waits for them, and re-layouts  24.5 us (9%)
  other arithmetic  7.2 us (3%)
    pallas_call x1, Pallas kernels, sum_gradients(): pl.pallas_call(functools.partial(sums_kernel, SCHEDULE), out_shape=tuple(...  99.9 us
    pallas_call x1, Pallas kernels, encode(): pl.pallas_call(encoder_kernel, out_shape=tuple(out_shapes), in_specs=[who...  78.4 us
    pallas_call x1, Pallas kernels, pool_words(): pl.pallas_call(pool_kernel, grid=(FILTERS // POOL_COLS,), out_shape=(jax....  26.5 us
    dot_general x2, matrix products, back_dot(): lax.dot_general(rows_in, weight_rows, (((1,), (1,)), ((), ())), preferred...  18.1 us
    unnamed x41, local copies, waits for them, and re-layouts  13.5 us
    dot_general x2, matrix products, dot(): return jnp.dot(left, right, preferred_element_type=F32)  10.5 us

profile of v2, /device:TPU:0, one launch (start us, length us, event | category | flops | bytes accessed | tf_op | source)
XLA Modules:
  0.0 266.9 jit_solution(16220118672697814221)
XLA Ops:
  0.7 1.3 copy.36
  2.4 1.0 broadcast_in_dim.54
  3.6 1.3 pad_bitcast_fusion
  5.5 26.5 %shard_map.264 = (bf16[128,2048]{1,0:T(8,128)(2,1)S(1)}, f32[128,2048]{1,0:T(8,128)S(1)}, bf16[50,128,128]{2,1,0:T(8,128)(2,1)S(1)}) custom-call(s32[128,128]{1,0:T(8,128)S(1)} %pad.22.clone.ids_ref, bf16[384,128]{1,0:T(8,128)(2,1)S(1)} %pad.23.table_ref, bf16[128,2048]{1,0:T(8,128)(2,1)S(1)} %copy.39.weight_ref.refs_14_), custom_call_target="tpu_custom_call" | custom-call | flops 3355443200 | bytes 8388608 | tf_op jit(solution)/shard_map/pallas_call | solution.py:134
  32.1 9.2 %fusion.4 = f32[128,4096]{1,0:T(8,128)S(1)} fusion(bf16[128,2048]{1,0:T(8,128)(2,1)S(1)} %get-tuple-element.37.refs_0_, bf16[1,2048,4096]{2,1,0:T(8,128)(2,1)} %param.24, f32[4096]{0:T(1024)S(1)} %bitcast.45), kind=kOutput, calls=%fused_computation.5 | convolution fusion | flops 2148007936 | bytes 19415040 | tf_op jit(solution)/shard_map/dot_general | solution.py:70
  43.4 1.3 convolution_convert_fusion.refs_0_
  48.4 78.4 %shard_map.265 = (bf16[128,768]{1,0:T(8,128)(2,1)}, bf16[128,768]{1,0:T(8,128)(2,1)}, bf16[128,768]{1,0:T(8,128)(2,1)}, bf16[128,768]{1,0:T(8,128)(2,1)}, bf16[1...) custom-call(bf16[128,768]{1,0:T(8,128)(2,1)} %convolution_convert_fu, ...), custom_call_target="tpu_custom_call" | custom-call | tf_op jit(solution)/shard_map/pallas_call | solution.py:1080
  126.7 4.7 %fusion.19 = (f32[128,2048]{1,0:T(8,128)S(1)}, f32[128,2048]{1,0:T(8,128)S(1)}, f32[128,2048]{1,0:T(8,128)}) fusion(f32[128,4096]{1,0:T(8,128)S(1)} %fusion.4, bf16[128,2048]{1,0:T(8,128)(2,1)S(1)} %get-tuple-element.37.refs_0_, bf16[128,768]{1,0:T(8,128)(2,1)} %get-tuple-element.43.refs_7_, bf16[2048,768]{1,0:T(8,128)(2,1)} %param.26), kind=kOutput, calls=%fused_computation.28 | convolution fusion | flops 411041792 | bytes 9109504 | tf_op jit(solution)/shard_map/dot_general | solution.py:74
  131.4 1.1 convert_reduce_fusion
  133.2 13.4 %fusion.25.refs_17_ = f32[128,2048]{1,0:T(8,128)} fusion(f32[128,2048]{1,0:T(8,128)S(1)} %get-tuple-element.49.refs_16_, bf16[128,4096]{1,0:T(8,128)(2,1)} %get-tuple-element.62.refs_6_, bf16[1,2048,4096]{2,1,0:T(8,128)(2,1)} %param.24, f32[128,2048]{1,0:T(8,128)} %get-tuple-element.71, f32[128,4096]{1,0:T(8,128)S(1)} %fusion.4), kind=kOutput, calls=%fused_computation.34 | convolution fusion | flops 2153775104 | bytes 22020096 | tf_op jit(solution)/shard_map/dot_general | solution.py:74
  147.3 99.9 %shard_map.266 = (f32[16,4096]{1,0:T(8,128)}, f32[16,768]{1,0:T(8,128)}, f32[6,2304]{1,0:T(8,128)}, f32[6,768]{1,0:T(8,128)}, f32[6,3072]{1,0:T(8,128)}, /*index...) custom-call(bf16[128,2048]{1,0:T(8,128)(2,1)} %copy-done, ...), custom_call_target="tpu_custom_call" | custom-call | tf_op jit(solution)/shard_map/pallas_call | solution.py:787
  247.2 0.8 fusion.36
  249.2 1.4 gather_fusion
  250.6 1.4 bitcast_select_fusion
  251.9 1.3 slice_bitcast_fusion
  253.3 1.3 slice.38
  254.6 1.4 slice.37
  256.0 1.6 copy.50
  257.7 1.7 copy.51
  259.3 1.4 copy.52
  260.8 1.5 copy.53
  262.3 1.3 copy.54
  263.6 1.5 copy.55
  265.2 1.5 copy.56
  (63 shorter events, 8.7 us)
Async XLA Ops:
  0.6 4.5 %copy-start.10 = (bf16[262,16]{0,1:T(8,128)(2,1)S(1)}, bf16[262,16]{0,1:T(8,128)(2,1)}, u32[]{:S(2)}) copy-start(bf16[262,16]{0,1:T(8,128)(2,1)} %param.21) | copy-start | bytes 25156
  0.7 4.6 %copy-start.7 = (s32[128,50]{0,1:T(8,128)S(1)}, s32[128,50]{0,1:T(8,128)}, u32[]{:S(2)}) copy-start(s32[128,50]{0,1:T(8,128)} %param.17) | copy-start | bytes 76804
  0.7 4.6 %copy-start.13 = (s32[128]{0:T(128)S(1)}, s32[128]{0:T(128)}, u32[]{:S(2)}) copy-start(s32[128]{0:T(128)} %param.18) | copy-start | bytes 1540
  0.7 4.8 %copy-start.4 = (s32[2048]{0:T(1024)}, s32[2048]{0:T(1024)S(1)}, u32[]{:S(2)}) copy-start(s32[2048]{0:T(1024)S(1)} %convert_add_fusion) | copy-start | bytes 24580
  0.7 4.7 %copy-start.14 = (s32[112]{0:T(128)}, s32[112]{0:T(128)S(1)}, u32[]{:S(2)}) copy-start(s32[112]{0:T(128)S(1)} %and_select_fusion.7) | copy-start | bytes 1348
  5.1 26.9 %copy-start.1 = (bf16[128,2048]{1,0:T(8,128)(2,1)}, bf16[128,2048]{1,0:T(8,128)(2,1)S(1)}, u32[]{:S(2)}) copy-start(bf16[128,2048]{1,0:T(8,128)(2,1)S(1)} %copy.39.weight_ref.refs_14_) | copy-start | bytes 1572868
  5.5 26.6 %copy-start.9 = (bf16[1,4096]{1,0:T(2,128)(2,1)S(1)}, bf16[1,4096]{1,0:T(2,128)(2,1)}, u32[]{:S(2)}) copy-start(bf16[1,4096]{1,0:T(2,128)(2,1)} %param.25) | copy-start | bytes 24580
  32.0 9.3 %copy-start.2 = (bf16[50,128,128]{2,1,0:T(8,128)(2,1)}, bf16[50,128,128]{2,1,0:T(8,128)(2,1)S(1)}, u32[]{:S(2)}) copy-start(bf16[50,128,128]{2,1,0:T(8,128)(2,1)S(1)} %get-tuple-element.48.refs_13_) | copy-start | bytes 4915204
  32.0 94.7 %copy-start = (bf16[128,2048]{1,0:T(8,128)(2,1)}, bf16[128,2048]{1,0:T(8,128)(2,1)S(1)}, u32[]{:S(2)}) copy-start(bf16[128,2048]{1,0:T(8,128)(2,1)S(1)} %get-tuple-element.37.refs_0_) | copy-start | bytes 1572868
  32.0 101.2 %copy-start.3 = (f32[128,2048]{1,0:T(8,128)}, f32[128,2048]{1,0:T(8,128)S(1)}, u32[]{:S(2)}) copy-start(f32[128,2048]{1,0:T(8,128)S(1)} %get-tuple-element.49.refs_16_) | copy-start | bytes 3145732
  41.3 2.1 copy-start.6
  41.3 3.3 %copy-start.15 = (s32[128]{0:T(128)S(1)}, s32[128]{0:T(128)}, u32[]{:S(2)}) copy-start(s32[128]{0:T(128)} %param.19) | copy-start | bytes 1540
  41.3 4.6 %copy-start.11 = (bf16[3,768]{1,0:T(4,128)(2,1)S(1)}, bf16[3,768]{1,0:T(4,128)(2,1)}, u32[]{:S(2)}) copy-start(bf16[3,768]{1,0:T(4,128)(2,1)} %param.27) | copy-start | bytes 13828
  41.3 5.2 %copy-start.12 = (bf16[3,768]{1,0:T(4,128)(2,1)S(1)}, bf16[3,768]{1,0:T(4,128)(2,1)}, u32[]{:S(2)}) copy-start(bf16[3,768]{1,0:T(4,128)(2,1)} %param.28) | copy-start | bytes 13828
  42.0 0.8 copy-start.5
  131.4 1.1 copy-start.8

commit v3 on v2

v3 whole, which is shorter than its diff:
```python
import functools
import jax
import jax.numpy as jnp
from jax import lax
from jax.experimental import pallas as pl
from jax.experimental.pallas import tpu as pltpu
from jax.sharding import PartitionSpec as P

D = 768
FF = 3072
HEADS = 12
HEAD_DIM = 64
FILTERS = 2048
CHAR_DIM = 16
CHARS = 262
WORD_CHARS = 50
TAPS = 7
SEQ_LEN = 512
WORDS = 128

EPSILON = 1e-05
NEG_LARGE = -1e30
MESH = pl.DeviceIdType.MESH
BF16 = jnp.bfloat16
F32 = jnp.float32

BIAS_ROW = TAPS * CHAR_DIM
ABSENT_ROW = BIAS_ROW + 1
CHAR_ROWS = 272


def norm_parts(values_in, gain_row, shift_row):
    mean_val = jnp.mean(values_in, -1, keepdims=True)
    centred = values_in - mean_val
    inverse = lax.rsqrt(jnp.mean(centred * centred, -1, keepdims=True) + EPSILON)
    normal = centred * inverse
    return (normal * gain_row + shift_row, normal, inverse)


def norm_back(grad_out, normal, inverse, gain_row):
    scaled = grad_out * gain_row
    grad_in = inverse * (
        scaled
        - jnp.mean(scaled, -1, keepdims=True)
        - normal * jnp.mean(scaled * normal, -1, keepdims=True)
    )
    return (grad_in, jnp.sum(grad_out * normal, 0), jnp.sum(grad_out, 0))


def dot(left, right):
    return jnp.dot(left, right, preferred_element_type=F32)


def back_dot(rows_in, weight_rows):
    return lax.dot_general(
        rows_in, weight_rows, (((1,), (1,)), ((), ())), preferred_element_type=F32
    )


def first_dot(left, right):
    return lax.dot_general(left, right, (((0,), (0,)), ((), ())), preferred_element_type=F32)


def place_of():
    index = lax.axis_index("dp")
    return index // 8, lax.rem(index // 2, 4), lax.rem(index, 2), lax.axis_index("ctx")


def device_of(y, z, core, x):
    return ((y * 4 + z) * 2 + core, x)


def around(value, step):
    return lax.rem(value + step, 4)


def remote(source, target, sems, index, device):
    return pltpu.make_async_remote_copy(
        src_ref=source,
        dst_ref=target,
        send_sem=sems[0].at[index],
        recv_sem=sems[1].at[index],
        device_id=device,
        device_id_type=MESH,
    )


def near_peers_of(where):
    y, z, core, x = where
    peers = []
    for number in range(1, 8):
        their_core, their_x = lax.rem(core + number // 4, 2), around(x, number % 4)
        peers.append((number, their_core * 4 + their_x, device_of(y, z, their_core, their_x)))
    return peers


def far_peers_of(where):
    y, z, core, x = where
    peers = []
    for number in range(1, 16):
        their_y, their_z = around(y, number // 4), around(z, number % 4)
        peers.append((number, their_y * 4 + their_z, device_of(their_y, their_z, core, x)))
    return peers


def exchange(peers, mine, sems, source, target):
    copies = []
    for number, index, device in peers:
        copy = remote(source.at[index], target.at[mine], sems, number, device)
        copy.start()
        copies.append(copy)
    target[mine] = source[mine]
    for copy in copies:
        copy.wait_recv()
    return copies


def exact_dot(left, right):
    return jnp.dot(left, right, preferred_element_type=F32, precision=lax.Precision.HIGHEST)


POOL_COLS = 512
POOL_STEP = 10
HIGH_PARTS = 4


def embed_kernel(
    ids_ref,
    lengths_ref,
    home_ref,
    table_ref,
    conv_ref,
    conv_bias_ref,
    high_in,
    high_bias_ref,
    proj_in,
    act_ref,
    pooled_ref,
    unfolded_ref,
    weight_ref,
    chars_ref,
    mixed_ref,
    final_ref,
    embedded_ref,
    values,
    ids_turned,
    ids_wide,
    table_wide,
    high,
    proj,
    sems,
    near_sems,
    far_sems,
    go_near,
    near,
    go_far,
    far,
):
    where = place_of()
    y, z, core, x = where
    rows_each = FILTERS // HIGH_PARTS
    loads = []
    for part in range(HIGH_PARTS):
        rows = pl.ds(part * rows_each, rows_each)
        loads.append(pltpu.make_async_copy(high_in.at[0, rows], high.at[rows], sems.at[part]))
    loads.append(pltpu.make_async_copy(proj_in, proj, sems.at[HIGH_PARTS]))
    for load in loads:
        load.start()

    near_peers, far_peers = near_peers_of(where), far_peers_of(where)
    barrier = pltpu.get_barrier_semaphore()
    for _, _, device in near_peers + far_peers:
        pl.semaphore_signal(barrier, inc=1, device_id=device, device_id_type=MESH)

    lane = lax.broadcasted_iota(jnp.int32, (WORDS, 128), 1)
    row = lax.broadcasted_iota(jnp.int32, (WORDS, 128), 0)
    home = home_ref[...]
    seat, spot = home // SEQ_LEN, lax.rem(home, SEQ_LEN)
    order = (lax.rem(seat, 2) * 4 + spot // WORDS) * 16 + seat // 2
    ids_turned[...] = jnp.full((128, WORDS), -1.0, F32)
    place = lax.broadcasted_iota(jnp.int32, (WORD_CHARS, WORDS), 0)
    ids_turned[0:WORD_CHARS, :] = jnp.where(place < lengths_ref[...], ids_ref[...], -1).astype(F32)
    carried = jnp.where(row == 127, lax.rem(spot, WORDS).astype(F32), ids_turned[...]).T
    carried = exact_dot(jnp.where(order == row, 1.0, 0.0), carried)
    go_near[...] = carried.reshape(8, 16, 128)
    pl.semaphore_wait(barrier, len(near_peers) + len(far_peers))
    sent = exchange(near_peers, core * 4 + x, (near_sems.at[0], near_sems.at[1]), go_near, near)
    turn = jnp.where(lane == lax.rem(row, 8) * 16 + row // 8, 1.0, 0.0)
    go_far[...] = exact_dot(turn, near[...].reshape(WORDS, 128)).reshape(16, 8, 128)
    sent += exchange(far_peers, y * 4 + z, (far_sems.at[0], far_sems.at[1]), go_far, far)
    arrived = far[...].reshape(WORDS, 128)
    slots = jnp.sum(jnp.where(lane == 127, arrived, 0.0), -1, keepdims=True)
    placed = jnp.where(slots == lane.astype(F32), 1.0, 0.0).T
    placed = jnp.where(lane < WORD_CHARS, exact_dot(placed, arrived), -1.0)
    ids_wide[...] = placed.astype(jnp.int32)
    chars_ref[...] = placed.T.astype(jnp.int32)

    code = lax.broadcasted_iota(jnp.int32, (WORDS, 384), 1)
    spread_lane = lax.broadcasted_iota(jnp.int32, (CHAR_DIM, 128), 1)
    spread_row = lax.broadcasted_iota(jnp.int32, (CHAR_DIM, 128), 0)
    spread = jnp.logical_and(lax.rem(spread_lane, CHAR_DIM) == spread_row, spread_lane < BIAS_ROW)
    spread = jnp.where(spread, 1.0, 0.0).astype(BF16)
    table_wide[...] = jnp.zeros((384, 128), BF16)
    table_wide[0:CHARS, :] = first_dot(table_ref[...], spread).astype(BF16)
    values[WORD_CHARS:, :, :] = jnp.zeros((TAPS - 1, WORDS, 128), F32)

    def look_up(place, ids):
        column = ids[:, :1]
        onehot = (column == code).astype(F32).astype(BF16)
        found = dot(onehot, table_wide[...])
        found = jnp.where(lane == BIAS_ROW, 1.0, found)
        absent = jnp.where(column < 0, 1.0, 0.0)
        values[place] = jnp.where(lane == ABSENT_ROW, absent, found)
        return pltpu.roll(ids, 127, 1)

    lax.fori_loop(0, WORD_CHARS, look_up, ids_wide[...], unroll=5)

    @pl.loop(0, WORD_CHARS)
    def _(place):
        taps = values[place]
        for tap in range(1, TAPS):
            taps = jnp.where(lane // CHAR_DIM == tap, values[place + tap], taps)
        unfolded_ref[place] = taps.astype(BF16)

    @pl.loop(0, FILTERS // POOL_COLS)
    def _(block):
        cols = pl.ds(pl.multiple_of(block * POOL_COLS, POOL_COLS), POOL_COLS)
        filters = lax.broadcasted_iota(jnp.int32, (BIAS_ROW, POOL_COLS), 1) + block * POOL_COLS
        tap_rows = lax.broadcasted_iota(jnp.int32, (BIAS_ROW, POOL_COLS), 0) // CHAR_DIM
        widths = jnp.ones((BIAS_ROW, POOL_COLS), jnp.int32)
        for bound in (1, 2, 4, 8, 16, 32):
            widths = widths + (filters >= FILTERS // 64 * bound).astype(jnp.int32)
        masked = jnp.where(tap_rows < widths, conv_ref[:, cols].astype(F32), 0.0)
        rest_row = lax.broadcasted_iota(jnp.int32, (128 - BIAS_ROW, POOL_COLS), 0)
        rest = jnp.where(rest_row == 0, conv_bias_ref[:, cols].astype(F32), 0.0)
        rest = jnp.where(rest_row == ABSENT_ROW - BIAS_ROW, NEG_LARGE, rest)
        weight = jnp.concatenate([masked, rest], axis=0).astype(BF16)
        weight_ref[:, cols] = weight

        def convolve(step, state):
            top, total = state
            left = unfolded_ref[pl.ds(POOL_STEP * step, POOL_STEP)]
            rows = dot(left.reshape(POOL_STEP * WORDS, 128), weight)
            rows = rows.reshape(POOL_STEP, WORDS, POOL_COLS)
            higher = jnp.maximum(top, jnp.max(rows, axis=0))
            more = jnp.sum(jnp.exp(rows - higher[None]), axis=0)
            return higher, total * jnp.exp(top - higher) + more

        top, total = lax.fori_loop(
            0,
            WORD_CHARS // POOL_STEP,
            convolve,
            (jnp.full((WORDS, POOL_COLS), -3e38, F32), jnp.zeros((WORDS, POOL_COLS), F32)),
        )
        pooled = top + jnp.log(total)
        pooled_ref[:, cols] = pooled
        act_ref[:, cols] = jax.nn.gelu(pooled).astype(BF16)

    for load in loads:
        load.wait()
    act = act_ref[...]
    for start in range(0, FILTERS, 512):
        near_cols, far_cols = slice(start, start + 512), slice(FILTERS + start, FILTERS + start + 512)
        mixed = dot(act, high[:, near_cols]) + high_bias_ref[:, near_cols].astype(F32)
        gates = dot(act, high[:, far_cols]) + high_bias_ref[:, far_cols].astype(F32)
        mixed_ref[:, near_cols] = mixed
        mixed_ref[:, far_cols] = gates
        carry = jax.nn.sigmoid(gates)
        final = carry * act[:, near_cols].astype(F32) + (1.0 - carry) * jax.nn.gelu(mixed)
        final_ref[:, near_cols] = final.astype(BF16)
    embedded_ref[...] = dot(final_ref[...], proj[...]).astype(BF16)
    for copy in sent:
        copy.wait_send()


def embed_words(ids, lengths, home, table, conv, conv_bias, high, high_bias, proj):
    whole = pl.BlockSpec(memory_space=pltpu.VMEM)
    outside = pl.BlockSpec(memory_space=pl.ANY)
    shapes = [
        ((WORDS, FILTERS), BF16),
        ((WORDS, FILTERS), F32),
        ((WORD_CHARS, WORDS, 128), BF16),
        ((128, FILTERS), BF16),
        ((128, WORDS), jnp.int32),
        ((WORDS, 2 * FILTERS), F32),
        ((WORDS, FILTERS), BF16),
        ((WORDS, D), BF16),
    ]
    dma = pltpu.SemaphoreType.DMA
    return pl.pallas_call(
        embed_kernel,
        out_shape=tuple(jax.ShapeDtypeStruct(*shape) for shape in shapes),
        in_specs=[whole] * 6 + [outside, whole, outside],
        out_specs=tuple(whole for _ in shapes),
        scratch_shapes=[
            pltpu.VMEM((WORD_CHARS + TAPS - 1, WORDS, 128), F32),
            pltpu.VMEM((128, WORDS), F32),
            pltpu.VMEM((WORDS, 128), jnp.int32),
            pltpu.VMEM((384, 128), BF16),
            pltpu.VMEM((FILTERS, 2 * FILTERS), BF16),
            pltpu.VMEM((FILTERS, D), BF16),
            dma((HIGH_PARTS + 1,)),
            dma((2, 8)),
            dma((2, 16)),
            pltpu.VMEM((8, 16, 128), F32),
            pltpu.VMEM((8, 16, 128), F32),
            pltpu.VMEM((16, 8, 128), F32),
            pltpu.VMEM((16, 8, 128), F32),
        ],
        compiler_params=pltpu.CompilerParams(
            collective_id=3, has_side_effects=True, vmem_limit_bytes=60 << 20
        ),
    )(ids, lengths, home, table, conv, conv_bias, high, high_bias, proj)


Y, Z, X = 0, 1, 2
LEFT_COLS = {"high": 2048, "proj": 2048, "qkv": 768, "out": 768, "up": 768, "down": 3072}
RIGHT_COLS = {"high": 4096, "proj": 768, "qkv": 2304, "out": 768, "up": 3072, "down": 768}
CHUNK_ROWS = {"high": 16, "proj": 16, "qkv": 6, "out": 6, "up": 6, "down": 24}

PIECES = {
    "high": (("high", 0, 0, 1, 0, 2048), ("high", 0, 2048, 1, 2048, 2048)),
    "proj": (("proj", 0, 0, 1, 0, 768),),
    "qkv": (("qkv", 0, 0, 0, 1152, 1152),),
    "out": (("out", 0, 0, 0, 384, 384),),
    "up": (("up", 0, 0, 0, 1536, 1536),),
    "down": (("down", 0, 0, 1, 0, 768), ("down", 2, 0, 2, 384, 384)),
}


def cut(pieces, widths):
    parts, rest = [], list(pieces)
    for width in widths:
        part, room = [], width
        while room:
            name, upper, upper_at, lower, lower_at, cols = rest.pop(0)
            used = min(cols, room)
            part.append((name, upper, upper_at, lower, lower_at, used))
            room -= used
            if used < cols:
                rest.insert(
                    0, (name, upper, upper_at + used, lower, lower_at + used, cols - used)
                )
        parts.append(tuple(part))
    assert not rest
    return tuple(parts)


def narrow(piece, most):
    name, upper, upper_at, lower, lower_at, cols = piece
    start = 0
    while start < cols:
        used = min(most, cols - start)
        yield (name, upper, upper_at + start, lower, lower_at + start, used, start)
        start += used


class Plan:
    def __init__(self, names, streams, plain=()):
        self.names = names
        self.stream_names, self.parts = [], []
        self.groups, self.group_at, self.right_at = 0, {}, {}
        self.right_cols = 0
        for name in names:
            self.group_at[name] = self.groups
            self.groups += -(-CHUNK_ROWS[name] // 8)
            self.right_at[name] = self.right_cols
            self.right_cols += RIGHT_COLS[name]
        for stream, (of, pieces, orders, widths) in enumerate(streams):
            self.stream_names.append(of)
            for order, part, width in zip(orders, cut(pieces, widths), widths, strict=True):
                self.parts.append((stream, order, part, width))
        for stream, order, width in plain:
            self.parts.append((stream, order, (), width))

    def scratch(self):
        dma = pltpu.SemaphoreType.DMA
        shapes = [
            pltpu.VMEM((self.groups, 4, 128, 2 * WORDS), BF16),
            pltpu.VMEM((self.groups, 4, 128, WORDS), BF16),
            pltpu.VMEM((2 * WORDS, self.right_cols), BF16),
            dma((2, len(self.names))),
            dma((2, len(self.names))),
            dma((2, len(self.parts), 15)),
        ]
        for _, _, _, width in self.parts:
            shapes += [
                pltpu.VMEM((4, 4, 4, 16, width), BF16),
                pltpu.VMEM((2, 2, 4, 16, width), BF16),
                pltpu.VMEM((2, 4, 4, 16, width), BF16),
                pltpu.VMEM((2, 2, 16, width), BF16),
                pltpu.VMEM((2, 4, 16, width), BF16),
                pltpu.VMEM((3, 16, width), BF16),
            ]
        return shapes


ORDERS = ((Y, Z, X), (Z, X, Y), (X, Y, Z))
DOWN_PLAN = Plan(("down",), ((("down",), PIECES["down"], ((Y, Z, X), (Z, Y, X)), (640, 512)),))
LATE_PLAN = Plan(
    ("proj", "qkv", "out", "up"),
    (
        (("up",), PIECES["up"], ORDERS, (512, 512, 512)),
        (
            ("proj", "qkv", "out"),
            PIECES["qkv"] + PIECES["out"] + PIECES["proj"],
            ORDERS,
            (768, 768, 768),
        ),
    ),
    plain=(
        (2, (Y, Z, X), 128),
        (3, (Z, X, Y), 384),
        (3, (X, Z, Y), 128),
        (4, (Y, X, Z), 384),
        (4, (X, Y, Z), 128),
    ),
)
CONV, DEALT = 2, {Y: 3, Z: 4}
RING_WORDS = 8 * WORDS
DEAL_COLS = 512
SHARED = ((16, D), (16, 384), (8, FILTERS))


class Part:
    def __init__(self, order, refs, sems, where):
        self.tiles, self.relay1, self.last1, self.relay2, self.last2, self.last3 = refs
        self.order, self.sems, self.where = order, sems, where
        self.width = self.tiles.shape[-1]
        y, z, core, x = where
        self.here = [(y, z, x)[axis] for axis in order]
        self.copies = {}

    def peer(self, level, step):
        y, z, core, x = self.where
        spot = [y, z, x]
        spot[self.order[level]] = around(self.here[level], step)
        return device_of(spot[0], spot[1], core, spot[2])

    def start(self, index, source, target, level, step):
        copy = remote(source, target, self.sems, index, self.peer(level, step))
        copy.start()
        self.copies[index] = copy

    def slices(self, level):
        prefix = tuple(self.here[:level])
        return lambda at, half=None: self.tiles.at[
            prefix + (at,) + (() if half is None else (pl.ds(2 * half, 2),))
        ]

    def buffers(self, level):
        return (self.relay1, self.last1) if level == 0 else (self.relay2, self.last2)

    def ring_start(self, level):
        me, base, tiles = self.here[level], 6 * level, self.slices(level)
        relay, last = self.buffers(level)
        far, right, left = around(me, 2), around(me, 1), around(me, 3)
        self.start(base, tiles(far, 0), relay.at[0], level, 1)
        self.start(base + 1, tiles(far, 1), relay.at[1], level, 3)
        self.start(base + 2, tiles(right, 1), last.at[0, pl.ds(2, 2)], level, 1)
        self.start(base + 3, tiles(left, 0), last.at[1, pl.ds(0, 2)], level, 3)

    def ring_relay(self, level):
        me, base, tiles = self.here[level], 6 * level, self.slices(level)
        relay, last = self.buffers(level)
        for side in (0, 1):
            target = tiles(around(me, (1, 3)[side]), side)
            self.copies[base + side].wait_recv()
            self.add(target, (relay.at[side],), 3 - level)
            self.start(
                base + 4 + side, target, last.at[side, pl.ds(2 * side, 2)], level, (1, 3)[side]
            )

    def ring_end(self, level):
        me, base, tiles = self.here[level], 6 * level, self.slices(level)
        _, last = self.buffers(level)
        for index in range(2, 6):
            self.copies[base + index].wait_recv()
        self.add(tiles(me), (last.at[0], last.at[1]), 3 - level)

    def add(self, target, terms, dims):
        lead = target.shape[:-2]
        count = 1
        for size in lead:
            count *= size

        @pl.loop(0, count)
        def _(flat):
            at, rest = [], flat
            for size in reversed(lead):
                at.insert(0, lax.rem(rest, size))
                rest = rest // size
            at = tuple(at)
            total = target[at].astype(F32)
            for term in terms:
                total = total + term[at].astype(F32)
            target[at] = total.astype(BF16)

    def direct_start(self):
        for step in (1, 2, 3):
            source = self.tiles.at[self.here[0], self.here[1], around(self.here[2], step)]
            self.start(11 + step, source, self.last3.at[step - 1], 2, step)

    def dealt_end(self, out, start):
        for step in (0, 1, 2, 3):
            if step:
                self.copies[11 + step].wait_recv()
                block = self.last3[step - 1]
            else:
                block = self.tiles[tuple(self.here)]
            column = around(self.here[2], 4 - step) * DEAL_COLS + start
            out[:, pl.ds(pl.multiple_of(column, 128), self.width)] = block.astype(F32)

    def direct_end(self):
        total = self.tiles[tuple(self.here)].astype(F32)
        for step in (1, 2, 3):
            self.copies[11 + step].wait_recv()
            total = total + self.last3[step - 1].astype(F32)
        return total

    def sent(self):
        for copy in self.copies.values():
            copy.wait_send()


class Shared:
    def __init__(self, pair, rings, sems, where):
        self.pair, self.rings, self.sems, self.where = pair, rings, sems, where
        self.copies = []

    def start(self, level, value):
        y, z, core, x = self.where
        if level == 0:
            self.pair[core] = value
            mine = self.pair.at[core]
            peers = [device_of(y, z, 1 - core, x)]
            targets = mine
        else:
            axis = level - 1
            here = (y, z, x)[axis]
            self.rings[axis, here] = value
            mine = self.rings.at[axis, here]
            peers = []
            for step in (1, 2, 3):
                spot = [y, z, x]
                spot[axis] = around(here, step)
                peers.append(device_of(spot[0], spot[1], core, spot[2]))
            targets = mine
        base = 0 if level == 0 else 3 * level - 2
        self.now = []
        for number, peer in enumerate(peers):
            copy = remote(mine, targets, self.sems, base + number, peer)
            copy.start()
            self.now.append(copy)
        self.copies += self.now

    def end(self, level):
        for copy in self.now:
            copy.wait_recv()
        if level == 0:
            return self.pair[0] + self.pair[1]
        ring = self.rings.at[level - 1]
        return (ring[0] + ring[1]) + (ring[2] + ring[3])

    def sent(self):
        for copy in self.copies:
            copy.wait_send()


def pick(rows_per_chunk, group, core, blocks, lanes):
    rows = blocks * 32
    row = lax.broadcasted_iota(jnp.int32, (rows, lanes), 0)
    lane = lax.broadcasted_iota(jnp.int32, (rows, lanes), 1)
    inner = lax.rem(row, 8) + 8 * group
    wanted = ((row // 32 * 2 + core) * 4 + lax.rem(row // 8, 4)) * rows_per_chunk + inner
    hit = jnp.logical_and(wanted == lane, inner < rows_per_chunk)
    return jnp.where(hit, 1.0, 0.0).astype(BF16)


PICK_LANES = {16: 512, 6: 384, 24: 768}


class Sums:
    def __init__(self, plan, refs, where):
        self.plan, self.where = plan, where
        y, z, core, x = where
        self.partner = device_of(y, z, 1 - core, x)
        self.left, self.left_out, self.right, left_sems, right_sems, part_sems = refs[:6]
        self.left_sems = (left_sems.at[0], left_sems.at[1])
        self.right_sems = (right_sems.at[0], right_sems.at[1])
        self.parts = []
        for at, (_, order, _, _) in enumerate(plan.parts):
            sems = (part_sems.at[0, at], part_sems.at[1, at])
            self.parts.append(Part(order, refs[6 + 6 * at : 12 + 6 * at], sems, where))
        self.picks, self.copies = {}, {}

    def right_part(self, name, mine):
        cols = pl.ds(self.plan.right_at[name], RIGHT_COLS[name])
        return self.right.at[pl.ds(0 if mine else WORDS, WORDS), cols]

    def send_right(self, name, source):
        copy = remote(
            source,
            self.right_part(name, False),
            self.right_sems,
            self.plan.names.index(name),
            self.partner,
        )
        copy.start()
        self.copies["right", name] = copy

    def picked(self, rows_per_chunk, group, mine):
        key = (rows_per_chunk, group, mine)
        if key not in self.picks:
            lanes = PICK_LANES[rows_per_chunk]
            core = self.where[2] if mine else 1 - self.where[2]
            self.picks[key] = pick(
                rows_per_chunk, group, core, lanes // (8 * rows_per_chunk), lanes
            )
        return self.picks[key]

    def send_left(self, name, source):
        rows_per_chunk = CHUNK_ROWS[name]
        lanes = PICK_LANES[rows_per_chunk]
        ys = lanes // (32 * rows_per_chunk)
        groups = -(-rows_per_chunk // 8)
        first = self.plan.group_at[name]
        for mine in (False, True):
            for group in range(groups):
                for block in range(4 // ys):
                    columns = source[:, block * lanes : (block + 1) * lanes]
                    rows = back_dot(self.picked(rows_per_chunk, group, mine), columns)
                    rows = rows.astype(BF16).reshape(ys, 128, WORDS)
                    span = pl.ds(block * ys, ys)
                    if mine:
                        self.left[first + group, span, :, 0:WORDS] = rows
                    else:
                        self.left_out[first + group, span] = rows
            if not mine:
                span = pl.ds(first, groups)
                copy = remote(
                    self.left_out.at[span],
                    self.left.at[span, :, :, pl.ds(WORDS, WORDS)],
                    self.left_sems,
                    self.plan.names.index(name),
                    self.partner,
                )
                copy.start()
                self.copies["left", name] = copy

    def multiply(self, stream):
        for name in self.plan.stream_names[stream]:
            self.copies["right", name].wait_recv()
            self.copies["left", name].wait_recv()
        for at, (of, order, pieces, _) in enumerate(self.plan.parts):
            if of != stream:
                continue
            tiles = self.parts[at].tiles
            offset = 0
            for piece in pieces:
                for name, upper, upper_at, lower, lower_at, cols, start in narrow(piece, 512):
                    base, first = self.plan.right_at[name], self.plan.group_at[name]
                    lanes = pl.ds(offset + start, cols)

                    @pl.loop(0, 4, unroll=4)
                    def _(row):
                        halves = []
                        for group, column in ((upper, upper_at), (lower, lower_at)):
                            factor = self.right[:, base + column : base + column + cols]
                            block = dot(self.left[first + group, row], factor)
                            halves.append(block.reshape(16, 1, 8, cols))
                        both = jnp.concatenate(halves, axis=1).reshape(4, 4, 16, cols)
                        both = both.astype(BF16)
                        for at_z in range(4):
                            for at_x in range(4):
                                spot = tuple((row, at_z, at_x)[axis] for axis in order)
                                tiles[spot + (slice(None), lanes)] = both[at_z, at_x]

                offset += piece[5]
        self.each(stream, lambda part: part.ring_start(0))

    def each(self, stream, action):
        for at, (of, _, _, _) in enumerate(self.plan.parts):
            if of == stream:
                action(self.parts[at])

    def relay1(self, stream):
        self.each(stream, lambda part: part.ring_relay(0))

    def end1(self, stream):
        self.each(stream, lambda part: (part.ring_end(0), part.ring_start(1)))

    def relay2(self, stream):
        self.each(stream, lambda part: part.ring_relay(1))

    def end2(self, stream):
        self.each(stream, lambda part: (part.ring_end(1), part.direct_start()))

    def finish(self, stream, outs):
        for at, (of, _, pieces, _) in enumerate(self.plan.parts):
            if of != stream:
                continue
            total = self.parts[at].direct_end()
            if not pieces:
                outs[...] = total
            offset = 0
            for name, upper, upper_at, lower, lower_at, cols in pieces:
                block = total[:, offset : offset + cols]
                for group, column, top in ((upper, upper_at, 0), (lower, lower_at, 8)):
                    rows = min(8, CHUNK_ROWS[name] - 8 * group)
                    outs[name][8 * group : 8 * group + rows, column : column + cols] = block[
                        top : top + rows
                    ]
                offset += cols

    def sent(self):
        for part in self.parts:
            part.sent()
        for copy in self.copies.values():
            copy.wait_send()


def sums_peers(where):
    y, z, core, x = where
    peers = [device_of(y, z, 1 - core, x)]
    for step in (1, 2, 3):
        peers.append(device_of(around(y, step), z, core, x))
        peers.append(device_of(y, around(z, step), core, x))
        peers.append(device_of(y, z, core, around(x, step)))
    return peers


PAIRS = HEADS // 2
GELU_SCALE = 0.7978845608028654
GELU_CUBE = 0.044715
FF_COLS = 512


def gelu_both(value):
    square = value * value
    bend = jnp.tanh(GELU_SCALE * value * (1.0 + GELU_CUBE * square))
    half = 0.5 * (1.0 + bend)
    slope = half + 0.5 * GELU_SCALE * value * (1.0 - bend * bend) * (
        1.0 + 3.0 * GELU_CUBE * square
    )
    return value * half, slope


def encoder_kernel(*refs):
    rest = list(refs)

    def take(count):
        taken = rest[:count]
        del rest[:count]
        return taken

    rows_in, act, length_in, gains, shifts, cotangent = take(6)
    weights_in = take(4)
    out_hidden, out_first, out_context, out_joint, out_attn, out_rows = take(6)
    out_middle, out_up, out_norms, out_down = take(4)
    out_rings = dict(zip((Y, Z), take(2)))
    sums_refs = take(6 + 6 * len(DOWN_PLAN.parts))
    weights = take(4)
    (hidden_rows,) = take(1)
    high_out, high_sems, ring_sems, store_sems = take(4)
    rings = dict(zip((Y, Z), take(2)))
    load_sems, keys_sems, sums_sems = take(3)
    joint, both, probs, probs_low, slopes = take(5)
    grads, relay, last = take(3)
    keys_sems = (keys_sems.at[0], keys_sems.at[1])
    sums_sems = (sums_sems.at[0], sums_sems.at[1])

    where = place_of()
    y, z, core, x = where
    sums = Sums(DOWN_PLAN, sums_refs, where)
    loads = []
    for at in range(4):
        loads.append(pltpu.make_async_copy(weights_in[at], weights[at], load_sems.at[at]))
        loads[at].start()
    qkv_w, out_w, up_w, down_w = weights

    right = device_of(y, z, core, around(x, 1))
    left = device_of(y, z, core, around(x, 3))

    barrier = pltpu.get_barrier_semaphore()
    greeted = sums_peers(where)
    for device in greeted:
        pl.semaphore_signal(barrier, inc=1, device_id=device, device_id_type=MESH)

    lane = lax.broadcasted_iota(jnp.int32, (WORDS, WORDS), 1)
    one_hot = lambda hit: jnp.where(hit, 1.0, 0.0).astype(BF16)
    sent = []
    word_rows = rows_in[...].astype(F32)
    gain = [gains[at : at + 1, :].astype(F32) for at in range(3)]
    shift = [shifts[at : at + 1, :].astype(F32) for at in range(3)]
    first_f, first_normal, first_inv = norm_parts(word_rows, gain[0], shift[0])
    first_norm = first_f.astype(BF16)
    out_first[...] = first_norm
    loads[0].wait()
    pl.semaphore_wait(barrier, len(greeted))
    for start in (D, 2 * D, 0):
        cols = slice(start, start + D)
        joint[:, cols] = dot(first_norm, qkv_w[:, cols]).astype(BF16)
        if start:
            half = pl.ds(start - D, D)
            both[x, :, start - D : start] = joint[:, cols]
            for side, device in ((0, right), (1, left)):
                copy = remote(
                    both.at[x, :, half], both.at[x, :, half], keys_sems, start // D * 2 + side, device
                )
                copy.start()
                sent.append(copy)
    key_right, key_left, value_right, value_left = sent[-4:]

    span = lambda at: pl.ds(pl.multiple_of(at * 2 * WORDS, 128), 2 * WORDS)
    mine = lambda at: pl.ds(pl.multiple_of(at * 2 * WORDS, 128), WORDS)
    theirs = lambda at: pl.ds(pl.multiple_of(at * 2 * WORDS + WORDS, 128), WORDS)
    spots = {Y: y, Z: z}
    partner = device_of(y, z, 1 - core, x)
    for keep in (False, True):
        for group in range(2):
            chosen = sums.picked(16, group, keep)
            for block in range(4):
                rows = back_dot(chosen, act[:, block * 512 : (block + 1) * 512]).astype(BF16)
                if not keep:
                    high_out[group, block] = rows
                    continue
                for axis, spot in spots.items():
                    rings[axis][group, block, :, mine(spot)] = rows
        if not keep:
            for axis, spot in spots.items():
                copy = remote(
                    high_out,
                    rings[axis].at[:, :, :, theirs(spot)],
                    (high_sems.at[0], high_sems.at[1]),
                    axis,
                    partner,
                )
                copy.start()
                sent.append(copy)
    for copy in sent[-2:]:
        copy.wait_recv()
    gathers = {}

    def gather(axis, index, source, group, step):
        place = [y, z, x]
        place[axis] = around(spots[axis], step)
        view = rings[axis].at[:, :, :, span(source)]
        if group is not None:
            view = rings[axis].at[group, :, :, span(source)]
        copy = remote(
            view,
            view,
            (ring_sems.at[0, axis], ring_sems.at[1, axis]),
            index,
            device_of(place[0], place[1], core, place[2]),
        )
        copy.start()
        sent.append(copy)
        gathers[axis, index] = copy

    for axis, spot in spots.items():
        gather(axis, 0, spot, None, 1)
        gather(axis, 1, spot, None, 3)
    key_right.wait_recv()
    behind, ahead = around(x, 3), around(x, 1)
    pass_key = remote(
        both.at[behind, :, pl.ds(0, D)], both.at[behind, :, pl.ds(0, D)], keys_sems, 0, right
    )
    pass_key.start()
    value_left.wait_recv()
    pass_value = remote(
        both.at[ahead, :, pl.ds(D, D)], both.at[ahead, :, pl.ds(D, D)], keys_sems, 1, left
    )
    pass_value.start()
    sent += [pass_key, pass_value]
    for copy in (key_left, value_right, pass_key, pass_value):
        copy.wait_recv()

    scale = HEAD_DIM ** (-0.5)
    low_lanes = one_hot(lane < HEAD_DIM)
    high_lanes = one_hot(lane >= HEAD_DIM)
    valid = lax.broadcasted_iota(jnp.int32, (1, SEQ_LEN), 1) < length_in[...]

    def stacked(rows):
        return jnp.concatenate([rows * low_lanes, rows * high_lanes], axis=0)

    def unstacked(rows):
        return jnp.where(lane < HEAD_DIM, rows[:WORDS], rows[WORDS:])

    for pair in range(PAIRS):
        cols = slice(pair * 128, pair * 128 + 128)
        keys = both[:, :, cols].reshape(SEQ_LEN, 128)
        values = both[:, :, D + pair * 128 : D + pair * 128 + 128].reshape(SEQ_LEN, 128)
        scores = back_dot(stacked(joint[:, cols]), keys) * scale
        masked = jnp.where(valid, scores, NEG_LARGE)
        top = jnp.max(masked, -1, keepdims=True)
        expo = jnp.where(valid, jnp.exp(masked - top), 0.0)
        share = expo / jnp.sum(expo, -1, keepdims=True)
        probs[pair] = share
        share = share.astype(BF16)
        probs_low[pair] = share
        out_context[:, cols] = unstacked(dot(share, values)).astype(BF16)
    for axis, spot in spots.items():
        for index, step in ((0, 1), (1, 3)):
            gathers[axis, index].wait_recv()
            gather(axis, 2 + index, around(spot, 4 - step), index, step)
    loads[1].wait()
    attn_out = dot(out_context[...], out_w[...])
    mid_f, mid_normal, mid_inv = norm_parts(first_norm.astype(F32) + attn_out, gain[1], shift[1])
    middle = mid_f.astype(BF16)
    out_middle[...] = middle
    loads[2].wait()
    loads[3].wait()

    down_proj = jnp.zeros((WORDS, D), F32)
    for block in range(FF // FF_COLS):
        cols = slice(block * FF_COLS, (block + 1) * FF_COLS)
        act, slope = gelu_both(dot(middle, up_w[:, cols]))
        act = act.astype(BF16)
        slopes[:, cols] = slope
        hidden_rows[:, cols] = act
        down_proj = down_proj + dot(act, down_w[cols, :])
    out_f, out_normal, out_inv = norm_parts(middle.astype(F32) + down_proj, gain[2], shift[2])
    out_hidden[...] = out_f.astype(BF16)

    def note(which, gain_row, shift_row):
        out_norms[which : which + 1, :] = gain_row[None]
        out_norms[3 + which : 4 + which, :] = shift_row[None]

    grad_pre2, gain_row, shift_row = norm_back(
        cotangent[...].astype(F32), out_normal, out_inv, gain[2]
    )
    note(2, gain_row, shift_row)
    grad_down = grad_pre2.astype(BF16)
    sums.right_part("down", True)[...] = grad_down
    sums.send_right("down", sums.right_part("down", True))
    sums.send_left("down", hidden_rows)
    grad_mid = grad_pre2
    for block in range(FF // FF_COLS):
        cols = slice(block * FF_COLS, (block + 1) * FF_COLS)
        grad_up = (slopes[:, cols] * back_dot(grad_down, down_w[cols, :])).astype(BF16)
        out_up[:, cols] = grad_up
        grad_mid = grad_mid + back_dot(grad_up, up_w[:, cols])
    grad_pre1, gain_row, shift_row = norm_back(grad_mid, mid_normal, mid_inv, gain[1])
    note(1, gain_row, shift_row)
    grad_attn = grad_pre1.astype(BF16)
    out_attn[...] = grad_attn
    grad_context = back_dot(grad_attn, out_w[...]).astype(BF16)
    stores = []
    for axis in spots:
        for index in (2, 3):
            gathers[axis, index].wait_recv()
        stores.append(pltpu.make_async_copy(rings[axis], out_rings[axis], store_sems.at[axis]))
        stores[-1].start()
    sums.multiply(0)

    for pair in range(PAIRS):
        cols = slice(pair * 128, pair * 128 + 128)
        value_cols = slice(D + pair * 128, D + pair * 128 + 128)
        keys = both[:, :, cols].reshape(SEQ_LEN, 128)
        values = both[:, :, value_cols].reshape(SEQ_LEN, 128)
        grad_rows = stacked(grad_context[:, cols])
        share = probs[pair]
        grad_probs = back_dot(grad_rows, values)
        delta = jnp.sum(share * grad_probs, -1, keepdims=True)
        grad_scores = (share * (grad_probs - delta)).astype(BF16)
        grad_query = unstacked(dot(grad_scores, keys)) * scale
        out_joint[:, cols] = grad_query.astype(BF16)
        grad_keys = first_dot(grad_scores, stacked(joint[:, cols])) * scale
        grads[:, :, cols] = grad_keys.astype(BF16).reshape(4, WORDS, 128)
        grad_values = first_dot(probs_low[pair], grad_rows)
        grads[:, :, value_cols] = grad_values.astype(BF16).reshape(4, WORDS, 128)

    key_half, value_half = pl.ds(0, D), pl.ds(D, D)
    opposite = around(x, 2)
    steps = [
        remote(grads.at[opposite, :, key_half], relay.at[0], sums_sems, 0, right),
        remote(grads.at[opposite, :, value_half], relay.at[1], sums_sems, 1, left),
        remote(grads.at[ahead, :, value_half], last.at[0, :, value_half], sums_sems, 2, right),
        remote(grads.at[behind, :, key_half], last.at[1, :, key_half], sums_sems, 3, left),
    ]
    for copy in steps:
        copy.start()
    sums.relay1(0)
    steps[0].wait_recv()
    grads[ahead, :, 0:D] = (grads[ahead, :, 0:D].astype(F32) + relay[0].astype(F32)).astype(BF16)
    steps.append(
        remote(grads.at[ahead, :, key_half], last.at[0, :, key_half], sums_sems, 4, right)
    )
    steps[4].start()
    steps[1].wait_recv()
    grads[behind, :, D:] = (grads[behind, :, D:].astype(F32) + relay[1].astype(F32)).astype(BF16)
    steps.append(
        remote(grads.at[behind, :, value_half], last.at[1, :, value_half], sums_sems, 5, left)
    )
    steps[5].start()
    sent += steps
    sums.end1(0)
    for copy in steps[2:]:
        copy.wait_recv()
    total = grads[x].astype(F32) + last[0].astype(F32) + last[1].astype(F32)
    out_joint[:, D:] = total.astype(BF16)

    grad_first = grad_pre1
    for start in range(0, 3 * D, D):
        cols = slice(start, start + D)
        grad_first = grad_first + back_dot(out_joint[:, cols], qkv_w[:, cols])
    grad_words, gain_row, shift_row = norm_back(grad_first, first_normal, first_inv, gain[0])
    note(0, gain_row, shift_row)

    out_rows[...] = grad_words.astype(BF16)
    sums.relay2(0)
    sums.end2(0)
    sums.finish(0, {"down": out_down})
    for copy in sent:
        copy.wait_send()
    for store in stores:
        store.wait()
    sums.sent()


def encode(rows, act, length, gains, shifts, cotangent, weights):
    whole = pl.BlockSpec(memory_space=pltpu.VMEM)
    shapes = [(WORDS, D)] * 3 + [(WORDS, 3 * D)] + [(WORDS, D)] * 3 + [(WORDS, FF)]
    out_shapes = [jax.ShapeDtypeStruct(shape, BF16) for shape in shapes]
    for shape in ((6, D), (CHUNK_ROWS["down"], D)):
        out_shapes.append(jax.ShapeDtypeStruct(shape, F32))
    ring_shape = (2, 4, 128, RING_WORDS)
    out_shapes += [jax.ShapeDtypeStruct(ring_shape, BF16)] * 2
    dma = pltpu.SemaphoreType.DMA
    return pl.pallas_call(
        encoder_kernel,
        out_shape=tuple(out_shapes),
        in_specs=[whole] * 6 + [pl.BlockSpec(memory_space=pl.ANY)] * 4,
        out_specs=(whole,) * (len(out_shapes) - 2) + (pl.BlockSpec(memory_space=pl.ANY),) * 2,
        scratch_shapes=[
            *DOWN_PLAN.scratch(),
            *(pltpu.VMEM(weight.shape, BF16) for weight in weights),
            pltpu.VMEM((WORDS, FF), BF16),
            pltpu.VMEM((2, 4, 128, WORDS), BF16),
            dma((2, 2)),
            dma((2, 2, 4)),
            dma((2,)),
            pltpu.VMEM(ring_shape, BF16),
            pltpu.VMEM(ring_shape, BF16),
            dma((4,)),
            dma((2, 6)),
            dma((2, 6)),
            pltpu.VMEM((WORDS, 3 * D), BF16),
            pltpu.VMEM((4, WORDS, 2 * D), BF16),
            pltpu.VMEM((PAIRS, 2 * WORDS, SEQ_LEN), F32),
            pltpu.VMEM((PAIRS, 2 * WORDS, SEQ_LEN), BF16),
            pltpu.VMEM((WORDS, FF), F32),
            pltpu.VMEM((4, WORDS, 2 * D), BF16),
            pltpu.VMEM((2, WORDS, D), BF16),
            pltpu.VMEM((2, WORDS, 2 * D), BF16),
        ],
        compiler_params=pltpu.CompilerParams(
            collective_id=2, has_side_effects=True, vmem_limit_bytes=62 << 20
        ),
    )(rows, act, length, gains, shifts, cotangent, *weights)


CONV_STEP = 10
CONV_COLS = 512
HIGH_ROWS = 256
HIGH_SLOTS = 3


def late_kernel(schedule, *refs):
    rest = list(refs)

    def take(count):
        taken = rest[:count]
        del rest[:count]
        return taken

    act, final_rows, first_norm, context, middle = take(5)
    chars, unfolded, conv_w, pooled, mixed, norms = take(6)
    right_in = dict(zip(("proj", "qkv", "out", "up"), take(4)))
    high_in, proj_in = take(2)
    rings_in = dict(zip((Y, Z), take(2)))
    outs = dict(zip(("high", "proj", "qkv", "out", "up"), take(5)))
    (out_conv,) = take(1)
    out_shared = take(3)
    sums_refs = take(6 + 6 * len(LATE_PLAN.parts))
    shared_refs = [take(2) for _ in SHARED]
    shared_sems, load_sems, high_sems = take(3)
    conv_back, conv_grad, conv_rows, conv_other, conv_sems = take(5)
    last_grad, table_grad, high_slots, proj, grad_pooled, small = take(6)
    grad_mixed, ring_sems, deal_sems, pair_sems = take(4)
    rings = dict(zip((Y, Z), take(2)))
    dealt = dict(zip((Y, Z), take(2)))
    conv_sems = (conv_sems.at[0], conv_sems.at[1])

    where = place_of()
    y, z, core, x = where
    partner = device_of(y, z, 1 - core, x)
    sums = Sums(LATE_PLAN, sums_refs, where)
    shared = [
        Shared(pair, rings, (shared_sems.at[0, at], shared_sems.at[1, at]), where)
        for at, (pair, rings) in enumerate(shared_refs)
    ]

    loads = {"proj_w": pltpu.make_async_copy(proj_in, proj, load_sems.at[4])}
    for at, name in enumerate(right_in):
        loads[name] = pltpu.make_async_copy(
            right_in[name], sums.right_part(name, True), load_sems.at[at]
        )
    for axis in (Y, Z):
        loads[axis] = pltpu.make_async_copy(rings_in[axis], rings[axis], ring_sems.at[axis])
    for load in loads.values():
        load.start()
    high_loads = [
        pltpu.make_async_copy(
            high_in.at[0, pl.ds(at * HIGH_ROWS, HIGH_ROWS)],
            high_slots.at[at % HIGH_SLOTS],
            high_sems.at[at],
        )
        for at in range(FILTERS // HIGH_ROWS)
    ]
    for at in range(HIGH_SLOTS):
        high_loads[at].start()

    barrier = pltpu.get_barrier_semaphore()
    peers = sums_peers(where)
    for device in peers:
        pl.semaphore_signal(barrier, inc=1, device_id=device, device_id_type=MESH)
    small[...] = jnp.zeros_like(small)
    small[0:6, :] = norms[...]
    pl.semaphore_wait(barrier, len(peers))
    for name in right_in:
        sums.send_right(name, right_in[name])

    def prepare(*names):
        for name in names:
            lefts = {"proj": final_rows, "qkv": first_norm, "out": context, "up": middle}
            sums.send_left(name, lefts[name])

    def multiply(stream):
        for name in LATE_PLAN.stream_names[stream]:
            if name in loads and name != "proj":
                loads[name].wait()
        sums.multiply(stream)

    def gates():
        loads["proj_w"].wait()
        loads["proj"].wait()
        grad_rows = sums.right_part("proj", True)[...]
        for start in range(0, FILTERS, 512):
            near, far = slice(start, start + 512), slice(FILTERS + start, FILTERS + start + 512)
            grad = back_dot(grad_rows, proj[near, :])
            carry = jax.nn.sigmoid(mixed[:, far])
            value, slope = gelu_both(mixed[:, near])
            grad_near = ((1.0 - carry) * slope * grad).astype(BF16)
            grad_far = (act[:, near].astype(F32) - value) * carry * (1.0 - carry) * grad
            grad_far = grad_far.astype(BF16)
            grad_mixed[:, near] = grad_near
            grad_mixed[:, far] = grad_far
            grad_pooled[:, near] = carry * grad
            for grads, at in ((grad_near, start), (grad_far, FILTERS + start)):
                total = jnp.sum(grads.astype(F32), 0, keepdims=True)
                for block in range(0, 512, 256):
                    line, lane_at = divmod(at + block, D)
                    small[6 + line : 7 + line, lane_at : lane_at + 256] = total[
                        :, block : block + 256
                    ]
        for axis, here in spots.items():
            share = lambda at: pl.ds(pl.multiple_of(axis * FILTERS + at * DEAL_COLS, 128), DEAL_COLS)
            rows = pl.ds(pl.multiple_of(here * 2 * WORDS, 128), WORDS)
            for step in (1, 2, 3):
                place = [y, z, x]
                place[axis] = around(here, step)
                copy = remote(
                    grad_mixed.at[:, share(place[axis])],
                    dealt[axis].at[rows, :],
                    (deal_sems.at[0, axis], deal_sems.at[1, axis]),
                    step,
                    device_of(place[0], place[1], core, place[2]),
                )
                copy.start()
                deals[axis, step] = copy
            dealt[axis][rows, :] = grad_mixed[:, share(here)]
            pass_on(axis, 0)

    spots = {Y: y, Z: z}
    deals, passes = {}, {}

    def pass_on(axis, step):
        source = around(spots[axis], 4 - step) * 2 * WORDS
        copy = remote(
            dealt[axis].at[pl.ds(pl.multiple_of(source, 128), WORDS), :],
            dealt[axis].at[pl.ds(pl.multiple_of(source + WORDS, 128), WORDS), :],
            (pair_sems.at[0, axis], pair_sems.at[1, axis]),
            step,
            partner,
        )
        copy.start()
        passes[axis, step] = copy

    def pass_all():
        for step in (1, 3, 2):
            for axis in spots:
                deals[axis, step].wait_recv()
                pass_on(axis, step)

    def multiply_high(axis):
        loads[axis].wait()
        for step in (0, 1, 2, 3):
            passes[axis, step].wait_recv()
        stream = DEALT[axis]
        chosen = [at for at, part in enumerate(LATE_PLAN.parts) if part[0] == stream]

        @pl.loop(0, 4, unroll=4)
        def _(row):
            halves = []
            for group in range(2):
                block = dot(rings[axis][group, row], dealt[axis][...])
                halves.append(block.reshape(16, 1, 8, DEAL_COLS))
            both = jnp.concatenate(halves, axis=1).reshape(4, 4, 16, DEAL_COLS).astype(BF16)
            start = 0
            for at in chosen:
                _, order, _, width = LATE_PLAN.parts[at]
                for at_z in range(4):
                    for at_x in range(4):
                        spot = tuple((row, at_z, at_x)[one] for one in order)
                        sums.parts[at].tiles[spot] = both[at_z, at_x][:, start : start + width]
                start += width

        sums.each(stream, lambda part: part.ring_start(0))

    def finish(stream):
        if stream == CONV:
            sums.finish(stream, out_conv)
        elif stream in (DEALT[Y], DEALT[Z]):
            axis = Y if stream == DEALT[Y] else Z
            start = [axis * FILTERS]

            def end(part):
                part.dealt_end(outs["high"], start[0])
                start[0] += part.width

            sums.each(stream, end)
        else:
            sums.finish(stream, outs)

    def highway(first, last):
        for at in range(first, last):
            cols = slice(at * HIGH_ROWS, (at + 1) * HIGH_ROWS)
            high_loads[at].wait()
            weight = high_slots.at[at % HIGH_SLOTS]
            grad = grad_pooled[:, cols]
            grad = grad + back_dot(grad_mixed[:, 0:FILTERS], weight[:, 0:FILTERS])
            grad = grad + back_dot(grad_mixed[:, FILTERS:], weight[:, FILTERS:])
            _, slope = gelu_both(pooled[:, cols])
            grad_pooled[:, cols] = slope * grad
            if at + HIGH_SLOTS < len(high_loads):
                high_loads[at + HIGH_SLOTS].start()

    lane = lax.broadcasted_iota(jnp.int32, (WORDS, 128), 1)

    def conv_start():
        last_grad[...] = jnp.zeros_like(last_grad)
        conv_grad[...] = jnp.zeros_like(conv_grad)
        table_grad[...] = jnp.zeros_like(table_grad)
        tap_row = lax.broadcasted_iota(jnp.int32, (128, 128), 0)
        for block in range(FILTERS // 128):
            weight = conv_w[:, block * 128 : (block + 1) * 128].astype(F32)
            weight = jnp.where(tap_row < BIAS_ROW, weight, 0.0)
            conv_back[block * 128 : (block + 1) * 128, :] = weight.T.astype(BF16)

    def conv_block(step):
        first = CONV_STEP * step
        some = unfolded[pl.ds(first, CONV_STEP)].reshape(CONV_STEP * WORDS, 128)
        unit = jnp.where(
            lax.broadcasted_iota(jnp.int32, (128, 128), 0)
            == lax.broadcasted_iota(jnp.int32, (128, 128), 1),
            1.0,
            0.0,
        ).astype(BF16)
        turned = back_dot(unit, some).astype(BF16)
        back = jnp.zeros((CONV_STEP * WORDS, 128), F32)
        for block in range(FILTERS // CONV_COLS):
            cols = slice(block * CONV_COLS, (block + 1) * CONV_COLS)
            conv = dot(some, conv_w[:, cols]).reshape(CONV_STEP, WORDS, CONV_COLS)
            shares = jnp.exp(conv - pooled[:, cols][None]) * grad_pooled[:, cols][None]
            shares = shares.astype(BF16).reshape(CONV_STEP * WORDS, CONV_COLS)
            conv_grad[:, cols] += dot(turned, shares)
            back = back + dot(shares, conv_back[cols, :])
        back = back.reshape(CONV_STEP, WORDS, 128)
        before = last_grad[...]
        last_grad[...] = back[CONV_STEP - TAPS + 1 :]
        high_low, onehots = [], []
        for side in range(CONV_STEP):
            taps = back[side]
            for tap in range(1, TAPS):
                from_tap = back[side - tap] if side >= tap else before[TAPS - 1 + side - tap]
                taps = jnp.where(lane // CHAR_DIM == tap, from_tap, taps)
            taps = jnp.where(lane < BIAS_ROW, taps, 0.0)
            high = taps.astype(BF16)
            low = (taps - high.astype(F32)).astype(BF16)
            high_low.append(jnp.concatenate([high, low], axis=1))
            code = lax.broadcasted_iota(jnp.int32, (CHAR_ROWS, WORDS), 0)
            ids = chars[pl.ds(first + side, 1), :]
            onehots.append(jnp.where(ids == code, 1.0, 0.0).astype(BF16))
        table_grad[0:CHAR_ROWS, :] += dot(
            jnp.concatenate(onehots, axis=1), jnp.concatenate(high_low, axis=0)
        )

    conv_pairs = []

    def conv_end():
        for block in range(16):
            turned = conv_grad[:, block * 128 : (block + 1) * 128].T
            conv_rows[block] = turned.reshape(2, 64, 128)
        copy = remote(conv_rows.at[:, 1 - core], conv_other, conv_sems, 0, partner)
        copy.start()
        conv_pairs.append(copy)
        table = table_grad[:, 0:128] + table_grad[:, 128:256]
        turned = jnp.concatenate(
            [table[128 * block : 128 * (block + 1)].T for block in range(3)], axis=1
        )
        folded = turned[0:CHAR_DIM]
        for tap in range(1, TAPS):
            folded = folded + turned[tap * CHAR_DIM : (tap + 1) * CHAR_DIM]
        shared[1].start(0, folded)
        shared[2].start(0, conv_grad[BIAS_ROW : BIAS_ROW + 8, :])

    def conv_ring():
        conv_pairs[0].wait_recv()
        tiles = [
            part.tiles for part, of in zip(sums.parts, LATE_PLAN.parts) if of[0] == CONV
        ][0]

        @pl.loop(0, 4)
        def _(at):
            for inner in range(4):
                row = at * 4 + inner
                total = conv_rows[row, core] + conv_other[row]
                tiles[at, inner] = total.astype(BF16).reshape(4, 16, 128)

        sums.each(CONV, lambda part: part.ring_start(0))

    def shared_step(level, *which):
        for one in which:
            if level < 3:
                shared[one].start(level + 1, shared[one].end(level))
            else:
                out_shared[one][...] = shared[one].end(level)

    actions = {
        "prepare": prepare,
        "gates": gates,
        "highway": highway,
        "multiply": multiply,
        "relay1": sums.relay1,
        "end1": sums.end1,
        "relay2": sums.relay2,
        "end2": sums.end2,
        "finish": finish,
        "pass_all": pass_all,
        "multiply_high": multiply_high,
        "conv_start": conv_start,
        "conv": lambda first, last: lax.fori_loop(
            first, last, lambda step, nothing: (conv_block(step), nothing)[1], 0
        ),
        "conv_end": conv_end,
        "conv_ring": conv_ring,
        "small": lambda: shared[0].start(0, small[...]),
        "shared": shared_step,
    }
    for name, *given in schedule:
        actions[name](*given)

    sums.sent()
    for one in shared:
        one.sent()
    conv_pairs[0].wait_send()
    for copy in (*deals.values(), *passes.values()):
        copy.wait_send()


LATE_SCHEDULE = (
    ("prepare", "up"),
    ("multiply", 0),
    ("prepare", "proj", "qkv", "out"),
    ("gates",),
    ("multiply", 1),
    ("small",),
    ("highway", 0, 3),
    ("pass_all",),
    ("highway", 3, 5),
    ("multiply_high", 0),
    ("multiply_high", 1),
    ("relay1", 0),
    ("highway", 5, 8),
    ("conv_start",),
    ("conv", 0, 1),
    ("relay1", 1),
    ("shared", 0, 0),
    ("conv", 1, 2),
    ("relay1", 3),
    ("relay1", 4),
    ("end1", 0),
    ("conv", 2, 3),
    ("end1", 1),
    ("conv", 3, 4),
    ("end1", 3),
    ("end1", 4),
    ("relay2", 0),
    ("conv", 4, 5),
    ("conv_end",),
    ("relay2", 1),
    ("shared", 1, 0),
    ("conv_ring",),
    ("end2", 0),
    ("relay2", 3),
    ("relay2", 4),
    ("shared", 0, 1, 2),
    ("relay1", 2),
    ("end2", 1),
    ("shared", 2, 0),
    ("shared", 1, 1, 2),
    ("end1", 2),
    ("end2", 3),
    ("end2", 4),
    ("finish", 0),
    ("relay2", 2),
    ("shared", 3, 0),
    ("shared", 2, 1, 2),
    ("finish", 1),
    ("end2", 2),
    ("shared", 3, 1, 2),
    ("finish", 3),
    ("finish", 4),
    ("finish", 2),
)


def late_sums(vmem_in, right, high_weight, proj_weight, rings):
    dma = pltpu.SemaphoreType.DMA
    scratch = LATE_PLAN.scratch()
    for shape in SHARED:
        scratch += [pltpu.VMEM((2,) + shape, F32), pltpu.VMEM((3, 4) + shape, F32)]
    scratch += [
        dma((2, len(SHARED), 10)),
        dma((5,)),
        dma((FILTERS // HIGH_ROWS,)),
        pltpu.VMEM((FILTERS, 128), BF16),
        pltpu.VMEM((128, FILTERS), F32),
        pltpu.VMEM((16, 2, 64, 128), F32),
        pltpu.VMEM((16, 64, 128), F32),
        dma((2, 1)),
        pltpu.VMEM((TAPS - 1, WORDS, 128), F32),
        pltpu.VMEM((384, 256), F32),
        pltpu.VMEM((HIGH_SLOTS, HIGH_ROWS, 2 * FILTERS), BF16),
        pltpu.VMEM((FILTERS, D), BF16),
        pltpu.VMEM((WORDS, FILTERS), F32),
        pltpu.VMEM(SHARED[0], F32),
        pltpu.VMEM((WORDS, 2 * FILTERS), BF16),
        dma((2,)),
        dma((2, 2, 4)),
        dma((2, 2, 4)),
        pltpu.VMEM((2, 4, 128, RING_WORDS), BF16),
        pltpu.VMEM((2, 4, 128, RING_WORDS), BF16),
        pltpu.VMEM((RING_WORDS, DEAL_COLS), BF16),
        pltpu.VMEM((RING_WORDS, DEAL_COLS), BF16),
    ]
    whole = pl.BlockSpec(memory_space=pltpu.VMEM)
    outside = pl.BlockSpec(memory_space=pl.ANY)
    names = ("high", "proj", "qkv", "out", "up")
    shapes = [(CHUNK_ROWS[name], RIGHT_COLS[name]) for name in names]
    shapes += [(16, 128)] + list(SHARED)
    return pl.pallas_call(
        functools.partial(late_kernel, LATE_SCHEDULE),
        out_shape=tuple(jax.ShapeDtypeStruct(shape, F32) for shape in shapes),
        in_specs=[whole] * len(vmem_in) + [outside] * 8,
        out_specs=tuple(whole for _ in shapes),
        scratch_shapes=scratch,
        compiler_params=pltpu.CompilerParams(
            collective_id=1, has_side_effects=True, vmem_limit_bytes=64 << 20
        ),
    )(*vmem_in, *right, high_weight, proj_weight, *rings)


def results_kernel(*refs):
    hidden, high, proj, qkv, out, up, down, conv, small, table, bias = refs[:11]
    (
        to_hidden,
        to_table,
        to_conv,
        to_conv_bias,
        to_high,
        to_high_bias,
        to_proj,
        to_gain,
        to_shift,
        to_qkv,
        to_out,
        to_up,
        to_down,
    ) = refs[11:]
    to_hidden[0] = hidden[...]
    to_high[0] = high[...]
    for source, target in ((proj, to_proj), (qkv, to_qkv), (out, to_out), (up, to_up), (down, to_down)):
        target[...] = source[...]
    to_gain[...] = small[0:3, :]
    to_shift[...] = small[3:6, :]
    for line in range(0, 2 * FILTERS, D):
        used = min(D, 2 * FILTERS - line)
        to_high_bias[:, line : line + used] = small[6 + line // D : 7 + line // D, 0:used]
    to_conv_bias[...] = bias[0:1, :]
    to_table[...] = table[:, 0:CHARS]
    me = lax.axis_index("dp") * 4 + lax.axis_index("ctx")
    filters = me * 16 + lax.broadcasted_iota(jnp.int32, (16, BIAS_ROW), 0)
    widths = jnp.ones((16, BIAS_ROW), jnp.int32)
    for bound in (1, 2, 4, 8, 16, 32):
        widths = widths + (filters >= FILTERS // 64 * bound).astype(jnp.int32)
    taps = lax.broadcasted_iota(jnp.int32, (16, BIAS_ROW), 1) // CHAR_DIM
    to_conv[...] = jnp.where(taps < widths, conv[:, 0:BIAS_ROW], 0.0)


def results(*arrays):
    shapes = [
        ((1, WORDS, D), BF16),
        ((CHAR_DIM, CHARS), F32),
        ((16, BIAS_ROW), F32),
        ((1, FILTERS), F32),
        ((1, 16, 2 * FILTERS), F32),
        ((1, 2 * FILTERS), F32),
        ((16, D), F32),
        ((3, D), F32),
        ((3, D), F32),
        ((6, 3 * D), F32),
        ((6, D), F32),
        ((6, FF), F32),
        ((24, D), F32),
    ]
    whole = pl.BlockSpec(memory_space=pltpu.VMEM)
    return pl.pallas_call(
        results_kernel,
        out_shape=tuple(jax.ShapeDtypeStruct(*shape) for shape in shapes),
        in_specs=[whole] * len(arrays),
        out_specs=tuple(whole for _ in shapes),
    )(*arrays)


def body(
    char_ids,
    word_lengths,
    word_home,
    seq_lengths,
    char_table,
    conv_weight,
    conv_bias,
    highway_weight,
    highway_bias,
    proj_weight,
    norm_gain,
    norm_shift,
    qkv_weight,
    out_weight,
    up_weight,
    down_weight,
    cotangent,
):
    act, pooled, unfolded, conv_w, chars, mixed, final_rows, embedded = embed_words(
        char_ids.T,
        word_lengths[None, :],
        word_home[None, :],
        char_table.T,
        conv_weight,
        conv_bias[None, :],
        highway_weight,
        highway_bias,
        proj_weight,
    )
    (
        out_hidden,
        first_norm,
        context,
        grad_joint,
        grad_attn,
        grad_embedded,
        middle,
        grad_up,
        norms,
        grad_down_weight,
        *rings,
    ) = encode(
        embedded,
        act,
        seq_lengths[None, :],
        norm_gain,
        norm_shift,
        cotangent.reshape(WORDS, D),
        (qkv_weight, out_weight, up_weight, down_weight),
    )
    high, proj, qkv, out, grad_up_weight, conv, small, table, bias = late_sums(
        (
            act,
            final_rows,
            first_norm,
            context,
            middle,
            chars,
            unfolded,
            conv_w,
            pooled,
            mixed,
            norms,
        ),
        (grad_embedded, grad_joint, grad_attn, grad_up),
        highway_weight,
        proj_weight,
        rings,
    )
    outs = list(
        results(
            out_hidden,
            high,
            proj,
            qkv,
            out,
            grad_up_weight,
            grad_down_weight,
            conv,
            small,
            table,
            bias,
        )
    )
    outs[1], outs[2] = outs[1].T, outs[2].T
    outs[3] = outs[3].reshape(-1)
    return tuple(outs)


def solution(mesh):
    placed = (
        P(("dp", "ctx"), None),
        P(("dp", "ctx")),
        P(("dp", "ctx")),
        P("dp"),
        P(),
        P(),
        P(),
        P(),
        P(),
        P(),
        P(),
        P(),
        P(),
        P(),
        P(),
        P(),
        P("dp", "ctx", None),
    )
    return jax.shard_map(
        body,
        mesh=mesh,
        in_specs=placed,
        out_specs=(
            P("dp", "ctx", None),
            P(),
            P(None, ("dp", "ctx")),
            P(),
            P(None, ("dp", "ctx"), None),
            P(),
            P(("dp", "ctx"), None),
            P(),
            P(),
            P(("dp", "ctx"), None),
            P(("dp", "ctx"), None),
            P(("dp", "ctx"), None),
            P(("dp", "ctx"), None),
        ),
        check_vma=False,
    )
```

time: 271 us -> 209 us (0.77)
  matrix products: 28.6 us -> 0 us
  local copies, waits for them, and re-layouts: 24.5 us -> 1.29 us
  other arithmetic: 7.2 us -> 0 us
    dot_general x4 -> x0, matrix products: 28.6 us -> none  [the longest x2 18.1 us: back_dot(): lax.dot_general(rows_in, weight_rows, (((1,), (1,)), ((), ())), preferred...]
    pallas_call x1, Pallas kernels: 78.4 us -> 59.9 us  [encode(): pl.pallas_call(encoder_kernel, out_shape=tuple(out_shapes), in_specs=[who...]
    pallas_call x2 -> x3, Pallas kernels: 126 us -> 143 us  [the longest x1 90.7 us: late_sums(): pl.pallas_call(functools.partial(late_kernel, LATE_SCHEDULE), out_shape=t...]
    unnamed x41 -> x0, local copies, waits for them, and re-layouts: 13.5 us -> none
    slice x3 -> x0, local copies, waits for them, and re-layouts: 3.55 us -> none  [the longest x1 1.44 us: body(): bias_sum[0]]
where the time goes in v3:
time: 209 us; the launch traced here: 206 us
  Pallas kernels  203 us (97%)
    pallas_call x1, Pallas kernels, late_sums(): pl.pallas_call(functools.partial(late_kernel, LATE_SCHEDULE), out_shape=t...  90.7 us
    pallas_call x1, Pallas kernels, encode(): pl.pallas_call(encoder_kernel, out_shape=tuple(out_shapes), in_specs=[who...  59.9 us
    pallas_call x1, Pallas kernels, embed_words(): pl.pallas_call(embed_kernel, out_shape=tuple((jax.ShapeDtypeStruct(*shape...  50.5 us

profile of v3, /device:TPU:0, one launch (start us, length us, event | category | flops | bytes accessed | tf_op | source)
XLA Modules:
  0.0 206.1 jit_solution(3967822818383909509)
XLA Ops:
  1.3 1.3 broadcast_in_dim.14.conv_bias_ref
  2.6 50.5 %shard_map.264 = (bf16[128,2048]{1,0:T(8,128)(2,1)}, f32[128,2048]{1,0:T(8,128)}, bf16[50,128,128]{2,1,0:T(8,128)(2,1)}, bf16[128,2048]{1,0:T(8,128)(2,1)}, s32[...) custom-call(s32[50,128]{1,0:T(8,128)} %bitcast.11, ...), custom_call_target="tpu_custom_call" | custom-call | tf_op jit(solution)/shard_map/pallas_call | solution.py:290
  53.1 59.9 %shard_map.265 = (bf16[128,768]{1,0:T(8,128)(2,1)}, bf16[128,768]{1,0:T(8,128)(2,1)}, bf16[128,768]{1,0:T(8,128)(2,1)}, bf16[128,2304]{1,0:T(8,128)(2,1)}, bf16[...) custom-call(bf16[128,768]{1,0:T(8,128)(2,1)} %get-tuple-element.55.r, ...), custom_call_target="tpu_custom_call" | custom-call | tf_op jit(solution)/shard_map/pallas_call | solution.py:1032
  113.0 90.7 %shard_map.266 = (f32[16,4096]{1,0:T(8,128)}, f32[16,768]{1,0:T(8,128)}, f32[6,2304]{1,0:T(8,128)}, f32[6,768]{1,0:T(8,128)}, f32[6,3072]{1,0:T(8,128)}, /*index...) custom-call(bf16[128,2048]{1,0:T(8,128)(2,1)} %get-tuple-element.56.refs_1_.refs_0_, ...), custom_call_target="tpu_custom_call" | custom-call | tf_op jit(solution)/shard_map/pallas_call | solution.py:1475
  203.6 2.1 %shard_map.267 = (bf16[1,128,768]{2,1,0:T(8,128)(2,1)}, f32[16,262]{1,0:T(8,128)}, f32[16,112]{1,0:T(8,128)}, f32[1,2048]{1,0:T(1,128)}, f32[1,16,4096]{2,1,0:T(...) custom-call(bf16[128,768]{1,0:T(8,128)(2,1)} %get-tuple-element.57.r, ...), custom_call_target="tpu_custom_call" | custom-call | tf_op jit(solution)/shard_map/pallas_call | solution.py:1541
